TPU v7x, 256 devices: a whole 4x4x8 slice. The times are simulated.
256 devices in a mesh: wide: 32 (over y_hi, z, core), narrow: 8 (over y_lo, x).
Axes of the slice: x: 4, y: 4 (y_hi: 2, y_lo: 2; y = y_hi * 2 + y_lo), z: 8, core: 2. Of those that a mesh axis runs over, the one named last changes fastest.
Arguments:
- student_picture_vectors: bfloat16 [1152, 16384], P('narrow', 'wide'), may hold values from -52 to 52
- student_caption_vectors: bfloat16 [1152, 16384], P('narrow', 'wide'), may hold values from -52 to 52
- teacher_picture_vectors: bfloat16 [1152, 16384], P('narrow', 'wide'), may hold values from -52 to 52
- teacher_caption_vectors: bfloat16 [1152, 16384], P('narrow', 'wide'), may hold values from -52 to 52
- sharpness_factors: float32 [2], replicated, may hold values from 8 to 130, as said below
- offset_couple: float32 [2], replicated, may hold values from -17 to -7, as said below
Outputs:
- image_losses: float32 [2, 16384], P(None, ('wide', 'narrow'))
- text_losses: float32 [2, 16384], P(None, ('wide', 'narrow'))
Inputs may be any that keep to these rules, and one draw needn't show every extreme that they name: `sharpness_factors`: entry 0 lies in 8 to 14, entry 1 in 90 to 130. `offset_couple`: entry 0 lies in -9 to -7, entry 1 in -17 to -12.
All inputs are finite; a program needn't handle non-finite values.
Results may differ from a plain program's by a relative error of at most 0.0003.
Values may be sent and summed in bfloat16 or wider, within the bound.
No kernel may reach another device: no remote copies, remote signals or barrier semaphores. Data moves between devices by JAX's collectives and lax.ppermute only.
A program may use at most 64 MiB of HBM per device.

v0:
```python
import jax
import jax.numpy as jnp
from jax import lax
from jax.sharding import PartitionSpec as P

epsilon = 1e-06


def column_norms(cols_in):
    return lax.rsqrt(jnp.sum(jnp.square(cols_in.astype(jnp.float32)), axis=0) + epsilon)


def row_norms(rows_in):
    return lax.rsqrt(jnp.sum(jnp.square(rows_in.astype(jnp.float32)), axis=1) + epsilon)


def pair_losses(image_cols, image_scale, text_rows, temper, offset, text_index, image_index):
    text_scale = row_norms(text_rows)
    products = jnp.dot(text_rows, image_cols, preferred_element_type=jnp.float32)
    cosine = products * text_scale[:, None] * image_scale[None, :]
    logits = temper * cosine + offset
    matched = text_index[:, None] == image_index[None, :]
    losses = jax.nn.softplus(jnp.where(matched, -logits, logits))
    return (jnp.sum(losses, axis=0), jnp.sum(losses, axis=1))


def on_device(
    student_picture_vectors,
    student_caption_vectors,
    teacher_picture_vectors,
    teacher_caption_vectors,
    sharpness_factors,
    offset_couple,
):
    image_pair = (
        lax.all_gather(student_picture_vectors, "narrow", axis=0, tiled=True),
        lax.all_gather(teacher_picture_vectors, "narrow", axis=0, tiled=True),
    )
    text_cols = (
        lax.all_to_all(student_caption_vectors, "narrow", split_axis=1, concat_axis=0, tiled=True),
        lax.all_to_all(teacher_caption_vectors, "narrow", split_axis=1, concat_axis=0, tiled=True),
    )
    text_pair = (text_cols[0].T, text_cols[1].T)
    rows_block = image_pair[0].shape[1]
    share = text_pair[0].shape[0]
    wide_place = lax.axis_index("wide")
    narrow_place = lax.axis_index("narrow")
    image_index = wide_place * rows_block + jnp.arange(rows_block, dtype=jnp.int32)
    scale_learn = column_norms(image_pair[0])
    scale_refer = column_norms(image_pair[1])
    pieces = (
        lax.all_gather(text_pair[0], "wide", axis=0, tiled=True),
        lax.all_gather(text_pair[1], "wide", axis=0, tiled=True),
    )
    row_count = pieces[0].shape[0]
    local_index = jnp.arange(row_count, dtype=jnp.int32)
    text_index = local_index // share * rows_block + narrow_place * share + local_index % share
    student_picture_totals, student_caption_totals = pair_losses(
        image_pair[0],
        scale_learn,
        pieces[0],
        sharpness_factors[0],
        offset_couple[0],
        text_index,
        image_index,
    )
    teacher_picture_totals, teacher_caption_totals = pair_losses(
        image_pair[1],
        scale_refer,
        pieces[1],
        sharpness_factors[1],
        offset_couple[1],
        text_index,
        image_index,
    )
    (
        student_picture_totals,
        teacher_picture_totals,
        student_caption_totals,
        teacher_caption_totals,
    ) = (
        student_picture_totals,
        teacher_picture_totals,
        student_caption_totals,
        teacher_caption_totals,
    )
    totals = (
        student_picture_totals,
        teacher_picture_totals,
        student_caption_totals,
        teacher_caption_totals,
    )
    student_picture_totals, teacher_picture_totals = (totals[0], totals[1])
    student_caption_totals, teacher_caption_totals = (
        lax.psum_scatter(totals[2], "wide", scatter_dimension=0, tiled=True),
        lax.psum_scatter(totals[3], "wide", scatter_dimension=0, tiled=True),
    )
    student_picture_totals, teacher_picture_totals = (
        lax.psum_scatter(student_picture_totals, "narrow", scatter_dimension=0, tiled=True),
        lax.psum_scatter(teacher_picture_totals, "narrow", scatter_dimension=0, tiled=True),
    )
    return (
        jnp.stack([student_picture_totals, teacher_picture_totals]),
        jnp.stack([student_caption_totals, teacher_caption_totals]),
    )


def solution(mesh):
    return jax.shard_map(
        on_device,
        mesh=mesh,
        in_specs=(
            P("narrow", "wide"),
            P("narrow", "wide"),
            P("narrow", "wide"),
            P("narrow", "wide"),
            P(),
            P(),
        ),
        out_specs=(P(None, ("wide", "narrow")), P(None, ("wide", "narrow"))),
        check_vma=False,
    )
```

profile of v0, /device:TPU:1, one launch (start us, length us, event | category | flops | bytes accessed | tf_op | source)
XLA Modules:
  0.0 445.9 jit_solution(17694841139659089823)
XLA Ops:
  7.2 0.0 copy-start.6
  7.2 0.0 copy-start.5
  7.2 0.0 copy-start.3
  7.2 0.0 copy-start.4
  7.2 0.0 all-gather.7.cloned.1.call-start
  7.3 0.7 all-gather.7.cloned.1.call-update
  7.9 0.0 all-gather.11.cloned.1.call-start
  8.0 0.7 all-gather.11.cloned.1.call-update
  8.7 0.0 all-gather.5.cloned.1.call-start
  8.7 1.0 copy.14
  9.8 12.0 %all_to_all.38 = bf16[144,8,64]{0,2,1:T(8,128)(2,1)S(1)} all-to-all(bf16[144,8,64]{0,2,1:T(8,128)(2,1)S(1)} %bitcast.32), channel_id=1, replica_groups=mesh['wide'=32,'narrow'=8] {'narrow'}, dimensions={1} | all-to-all | bytes 294912 | tf_op jit(solution)/shard_map/all_to_all | solution.py:40
  21.7 0.1 copy.11
  21.9 0.9 all_to_all.31
  22.8 0.0 all-gather.5.cloned.1.call-update
  22.8 0.0 all-gather.9.cloned.1.call-start
  22.9 1.0 copy.15
  23.9 10.1 %all_to_all.39 = bf16[144,8,64]{0,2,1:T(8,128)(2,1)S(1)} all-to-all(bf16[144,8,64]{0,2,1:T(8,128)(2,1)S(1)} %bitcast.33), channel_id=1, replica_groups=mesh['wide'=32,'narrow'=8] {'narrow'}, dimensions={1} | all-to-all | bytes 294912 | tf_op jit(solution)/shard_map/all_to_all | solution.py:41
  34.1 0.1 copy.13
  34.2 0.9 all_to_all.35
  35.1 0.0 all-gather.9.cloned.1.call-update
  35.2 0.0 copy-done.6
  35.2 0.6 dynamic-slice.4
  35.8 0.0 copy-done.5
  35.8 0.6 dynamic-slice
  37.7 0.0 copy-done.3
  37.7 0.6 fusion.12
  38.3 0.0 copy-done.4
  38.3 0.6 fusion.13
  38.9 11.6 %all-gather.7.cloned.1.call-done = bf16[1152,512]{1,0:T(8,128)(2,1)} async-done(((bf16[144,512]{1,0:T(8,128)(2,1)}), bf16[1152,512]{1,0:T(8,128)(2,1)}) %all-gather.7.cloned.1.call-update) | async-done | bytes 1179664 | tf_op jit(solution)/shard_map/all_gather | solution.py:36
  50.4 1.6 multiply_reduce_fusion.3
  52.0 42.0 %all-gather.11.cloned.1.call-done = bf16[1152,512]{1,0:T(8,128)(2,1)} async-done(((bf16[144,512]{1,0:T(8,128)(2,1)}), bf16[1152,512]{1,0:T(8,128)(2,1)}) %all-gather.11.cloned.1.call-update) | async-done | bytes 1179664 | tf_op jit(solution)/shard_map/all_gather | solution.py:37
  94.0 1.6 multiply_reduce_fusion.2
  95.6 94.3 %all-gather.5.cloned.1.call-done = bf16[2048,1152]{1,0:T(8,128)(2,1)} async-done(((bf16[64,1152]{1,0:T(8,128)(2,1)}), bf16[2048,1152]{1,0:T(8,128)(2,1)}) %all-gather.5.cloned.1.call-update) | async-done | bytes 4718608 | tf_op jit(solution)/shard_map/all_gather | solution.py:52
  189.9 3.3 multiply_reduce_fusion.1
  193.2 84.9 %all-gather.9.cloned.1.call-done = bf16[2048,1152]{1,0:T(8,128)(2,1)} async-done(((bf16[64,1152]{1,0:T(8,128)(2,1)}), bf16[2048,1152]{1,0:T(8,128)(2,1)}) %all-gather.9.cloned.1.call-update) | async-done | bytes 4718608 | tf_op jit(solution)/shard_map/all_gather | solution.py:53
  278.1 3.5 multiply_reduce_fusion
  281.6 0.3 copy-done
  281.8 8.2 %fusion.10 = (f32[2048]{0:T(1024)S(1)}, f32[512]{0:T(512)S(1)}) fusion(f32[]{:T(128)} %bitcast.4, f32[512]{0:T(512)S(1)} %add_rsqrt_fusion.3, f32[2048]{0:T(1024)S(1)} %add_rsqrt_fusion.1, bf16[2048,1152]{1,0:T(8,128)(2,1)S(1)} %copy-done, bf16[1152,512]{1,0:T(8,128)(2,1)S(1)} %copy-done.2, f32[]{:T(128)} %bitcast, s32[512]{0:T(512)S(1)} %iota_add_fusion, ...), kind=kOutput, calls=%fused_computation.33 | convolution fusion | flops 2431645184 | bytes 5928968 | tf_op jit(solution)/shard_map/dot_general | solution.py:19
  290.1 0.0 slice-done
  290.1 0.0 slice-done.1
  290.1 0.0 copy-done.1
  290.1 7.9 %fusion.11 = (f32[2048]{0:T(1024)S(1)}, f32[512]{0:T(512)S(1)}) fusion(f32[]{:T(128)} %bitcast.10, f32[512]{0:T(512)S(1)} %add_rsqrt_fusion.2, f32[2048]{0:T(1024)S(1)} %add_rsqrt_fusion, bf16[2048,1152]{1,0:T(8,128)(2,1)S(1)} %bitcast.29, bf16[1152,512]{1,0:T(8,128)(2,1)S(1)} %copy-done.1, f32[]{:T(128)} %bitcast.6, s32[512]{0:T(512)S(1)} %iota_add_fusion, ...), kind=kOutput, calls=%fused_computation.34 | convolution fusion | flops 2431645184 | bytes 5928968 | tf_op jit(solution)/shard_map/dot_general | solution.py:19
  298.0 124.3 %all-reduce.4 = (f32[2048]{0:T(1024)S(1)}, f32[2048]{0:T(1024)S(1)}) all-reduce(f32[2048]{0:T(1024)S(1)} %get-tuple-element.4, f32[2048]{0:T(1024)S(1)} %get-tuple-element.2), channel_id=5, replica_groups=mesh['wide'=32,'narrow'=8] {'wide'}, use_global_device_ids=true, to_apply=%region_11.12.clone | all-reduce | flops 4096 | bytes 32768
  422.3 0.1 dynamic-slice_bitcast_fusion
  422.4 0.6 pad_maximum_fusion.1
  423.0 15.8 %all-reduce.5 = (f32[512]{0:T(512)S(1)}, f32[512]{0:T(512)S(1)}) all-reduce(f32[512]{0:T(512)S(1)} %get-tuple-element.5, f32[512]{0:T(512)S(1)} %get-tuple-element.3), channel_id=3, replica_groups=mesh['wide'=32,'narrow'=8] {'narrow'}, use_global_device_ids=true, to_apply=%region_7.8.clone | all-reduce | flops 1024 | bytes 8192
  438.8 0.1 dynamic-slice_bitcast_fusion.2
  438.8 0.6 pad_maximum_fusion
  (13 shorter events, 0.0 us)
Async XLA Ops:
  7.2 28.0 %copy-start.6 = (u32[256]{0:T(256)S(1)}, u32[256]{0:T(256)}, u32[]{:S(2)}) copy-start(u32[256]{0:T(256)} %constant.61) | copy-start | bytes 3076
  7.2 28.6 %copy-start.5 = (u32[256]{0:T(256)S(1)}, u32[256]{0:T(256)}, u32[]{:S(2)}) copy-start(u32[256]{0:T(256)} %constant.53) | copy-start | bytes 3076
  7.2 30.5 %copy-start.3 = (f32[2]{0:T(128)S(1)}, f32[2]{0:T(128)}, u32[]{:S(2)}) copy-start(f32[2]{0:T(128)} %param.10) | copy-start | bytes 28
  7.2 31.1 %copy-start.4 = (f32[2]{0:T(128)S(1)}, f32[2]{0:T(128)}, u32[]{:S(2)}) copy-start(f32[2]{0:T(128)} %param.11) | copy-start | bytes 28
  7.2 43.2 %all-gather.7.cloned.1.call-start = ((), (), s32[]{:S(2)}) async-start(), calls=%async_computation.3 | async-start | bytes 1327104 | tf_op jit(solution)/shard_map/all_gather | solution.py:36
  7.9 86.0 %all-gather.11.cloned.1.call-start = ((), (), s32[]{:S(2)}) async-start(), calls=%async_computation.5 | async-start | bytes 1327104 | tf_op jit(solution)/shard_map/all_gather | solution.py:37
  8.7 181.2 %all-gather.5.cloned.1.call-start = ((), (), s32[]{:S(2)}) async-start(), calls=%async_computation.2 | async-start | bytes 4866048 | tf_op jit(solution)/shard_map/all_gather | solution.py:52
  22.8 255.2 %all-gather.9.cloned.1.call-start = ((), (), s32[]{:S(2)}) async-start(), calls=%async_computation.4 | async-start | bytes 4866048 | tf_op jit(solution)/shard_map/all_gather | solution.py:53
  95.6 186.0 %copy-start.2 = (bf16[1152,512]{1,0:T(8,128)(2,1)S(1)}, bf16[1152,512]{1,0:T(8,128)(2,1)}, u32[]{:S(2)}) copy-start(bf16[1152,512]{1,0:T(8,128)(2,1)} %all-gather.7.cloned.1.call-done) | copy-start | bytes 3538948
  278.1 3.8 copy-start
  278.1 12.0 %slice-start = ((s8[4718592]{0:T(1024)(128)(4,1)}), s8[4194304]{0:T(1024)(128)(4,1)S(1)}, s32[]{:S(2)}) async-start(s8[4718592]{0:T(1024)(128)(4,1)} %bitcast.28), calls=%async_computation.6 | async-start | bytes 8388608
  281.8 8.3 %slice-start.1 = ((s8[4718592]{0:T(1024)(128)(4,1)}), s8[524288]{0:T(1024)(128)(4,1)S(1)}, s32[]{:S(2)}) async-start(s8[4718592]{0:T(1024)(128)(4,1)} %bitcast.28), calls=%async_computation.7 | async-start | bytes 1048576
  281.8 8.3 %copy-start.1 = (bf16[1152,512]{1,0:T(8,128)(2,1)S(1)}, bf16[1152,512]{1,0:T(8,128)(2,1)}, u32[]{:S(2)}) copy-start(bf16[1152,512]{1,0:T(8,128)(2,1)} %all-gather.11.cloned.1.call-done) | copy-start | bytes 3538948
Sparse Core Ops, SparseCore 0:
  9.8 40.5 all-gather.6
  52.2 41.7 all-gather.10
  96.8 93.0 all-gather.4
  192.5 85.5 all-gather.8
where the time goes:
time: 454 us; the launch traced here: 446 us
  waiting for transfers between devices  234 us (52%)
  blocking collectives  162 us (36%)
  matrix products  16.1 us (4%)
  between operations  15.2 us (3%)
  other arithmetic  11.1 us (2%)
  local copies, waits for them, and re-layouts  7 us (2%)
    unnamed x2, blocking collectives  140 us
    all_gather x1, waiting for transfers between devices, on_device(): lax.all_gather(text_pair[0], 'wide', axis=0, tiled=True)  94.3 us
    all_gather x1, waiting for transfers between devices, on_device(): lax.all_gather(text_pair[1], 'wide', axis=0, tiled=True)  84.9 us
    all_gather x1, waiting for transfers between devices, on_device(): lax.all_gather(teacher_picture_vectors, 'narrow', axis=0, tiled=True)  42 us
    dot_general x2, matrix products, pair_losses(): jnp.dot(text_rows, image_cols, preferred_element_type=jnp.float32)  16.1 us
    all_to_all x1, blocking collectives, on_device(): lax.all_to_all(student_caption_vectors, 'narrow', split_axis=1, concat_ax...  12 us
    all_gather x1, waiting for transfers between devices, on_device(): lax.all_gather(student_picture_vectors, 'narrow', axis=0, tiled=True)  11.6 us
    all_to_all x1, blocking collectives, on_device(): lax.all_to_all(teacher_caption_vectors, 'narrow', split_axis=1, concat_ax...  10.1 us
  transfers between devices with their start and end apart: 4, of which 4 were waited for; matrix products, arithmetic and copies ran while one was open for 3% of the time, Pallas kernels for 0%

commit v1 on v0

v1 whole, which is shorter than its diff:
```python
import functools

import jax
import jax.numpy as jnp
from jax import lax
from jax.experimental import pallas as pl
from jax.experimental.pallas import tpu as pltpu
from jax.sharding import PartitionSpec as P

epsilon = 1e-06
AXES = ("wide", "narrow")
X, LO, HI, Z, CORES = 4, 2, 2, 8, 2
NARROW = LO * X


def device(hi, z, core, lo, x):
    return ((hi * Z + z) * CORES + core) * NARROW + lo * X + x


def places():
    for hi in range(HI):
        for z in range(Z):
            for core in range(CORES):
                for lo in range(LO):
                    for x in range(X):
                        yield hi, z, core, lo, x


def send(value, step):
    pairs = [(place, step(*place)) for place in places()]
    pairs = [(device(*place), device(*target)) for place, target in pairs if target]
    return lax.ppermute(value, AXES, pairs)


def send_core(value):
    return send(value, lambda hi, z, core, lo, x: (hi, z, core ^ 1, lo, x))


def send_first(value, d):
    return send(
        value,
        lambda hi, z, core, lo, x: (
            (hi ^ (d >> 1), z, core, lo ^ (d & 1), x) if core else (hi, z, core, lo, x ^ d)
        ),
    )


def send_second(value, d):
    return send(
        value,
        lambda hi, z, core, lo, x: (
            (hi, z, core, lo, x ^ d) if core else (hi ^ (d >> 1), z, core, lo ^ (d & 1), x)
        ),
    )


def groups_by(key, order):
    groups = {}
    for place in places():
        groups.setdefault(key(*place), []).append(place)
    return [
        [device(*place) for place in sorted(group, key=lambda place: order(*place))]
        for group in groups.values()
    ]


def exchange(value, groups):
    return lax.all_to_all(value, AXES, 0, 0, axis_index_groups=groups, tiled=True)


def send_z(value, dz):
    return send(value, lambda hi, z, core, lo, x: (hi, (z + dz) % Z, core, lo, x))


VMEM = pl.BlockSpec(memory_space=pltpu.VMEM)
SMEM = pl.BlockSpec(memory_space=pltpu.SMEM)
LARGE = 60 * 1024 * 1024
SMALL = pltpu.CompilerParams(vmem_limit_bytes=4 * 1024 * 1024)


FOLD = 80


def start_kernel(p0, p1, c0, c1, own_ref, give_ref, out_ref):
    core = lax.axis_index("wide") % CORES
    give_ref[...] = jnp.where(core == 0, p1[...], p0[...])
    own_ref[...] = jnp.where(core == 0, p0[...], p1[...])
    features, block = c0.shape
    share = block // NARROW
    for model, ref in enumerate((c0, c1)):
        for n in range(NARROW):
            piece = ref[:, n * share : (n + 1) * share]
            rest = jnp.concatenate(
                [piece[FOLD:], jnp.zeros((2 * FOLD - features, share), piece.dtype)], axis=0
            )
            out_ref[model * NARROW + n] = jnp.concatenate([piece[:FOLD], rest], axis=1)


def start(pictures, captions):
    features, block = captions[0].shape
    dtype = captions[0].dtype
    return pl.pallas_call(
        start_kernel,
        in_specs=[VMEM] * 4,
        out_specs=[VMEM] * 3,
        out_shape=[
            jax.ShapeDtypeStruct((features, block), dtype),
            jax.ShapeDtypeStruct((features, block), dtype),
            jax.ShapeDtypeStruct((CORES * NARROW, FOLD, 2 * block // NARROW), dtype),
        ],
        compiler_params=pltpu.CompilerParams(vmem_limit_bytes=LARGE),
    )(*pictures, *captions)


def rows_kernel(place, in_ref, out_ref):
    features = out_ref.shape[1] // NARROW
    share = out_ref.shape[0] // CORES
    columns = []
    for other in range(CORES):
        parts = []
        for slot in range(NARROW):
            piece = in_ref[(place[2] ^ other) * NARROW + (place[0] ^ slot)]
            parts += [piece[:, :share], piece[: features - FOLD, share:]]
        columns.append(jnp.concatenate(parts, axis=0))
    out_ref[...] = jnp.concatenate(columns, axis=1).T


def text_rows(place, shares, features):
    return pl.pallas_call(
        rows_kernel,
        in_specs=[SMEM, VMEM],
        out_specs=VMEM,
        out_shape=jax.ShapeDtypeStruct((shares.shape[2], NARROW * features), shares.dtype),
        compiler_params=SMALL,
    )(place, shares)


def softplus(value):
    power = jnp.exp2(jnp.abs(value) * -1.4426950408889634)
    near = 1.0 + power
    return jnp.maximum(value, 0.0) + (jnp.log(near) + (power - (near - 1.0)))


def pair_kernel(sharpness, offsets, place, *refs, texts, first):
    text_refs, refs = refs[:texts], refs[texts:]
    text, even, odd, text_scale, total = refs[-5:]
    if first:
        line, one, two_low, two_high, three, image_sums, text_sums, image, image_scale = refs[:9]
    else:
        image, image_scale, before_image, before_text, keep_out, give_out = refs[:6]
        image_sums, text_sums = refs[6:8]
    narrow, hi, core = place[0], place[1], place[2]
    low = narrow // X
    temper = jnp.where(core == 0, sharpness[0], sharpness[1])
    offset = jnp.where(core == 0, offsets[0], offsets[1])
    rows, depth = text.shape
    columns = image.shape[4]

    row = 0
    for ref in text_refs:
        size = ref.shape[0]
        text[row : row + size, :] = ref[...]
        row += size

    if first:

        @pl.when(core == 0)
        def _():
            for block in range(4):
                owner = block // 2
                if block % 2 == 0:
                    image[block, 0] = line[:, owner]
                    image[block, 1] = one[:, owner]
                else:
                    image[block, 0, 0:2] = two_low[:, owner]
                    image[block, 0, 2:4] = two_high[:, owner]
                    image[block, 1] = three[:, owner]

        @pl.when(core == 1)
        def _():
            for block in range(4):
                owner, at = block // 2, slice(block % 2 * 2, block % 2 * 2 + 2)
                two = two_high if block % 2 else two_low
                image[block, :, 0] = line[at, owner]
                image[block, :, 1] = one[at, owner]
                image[block, :, 2] = two[:, owner]
                image[block, :, 3] = three[at, owner]

    total[...] = jnp.zeros_like(total)

    @pl.loop(0, rows // 128)
    def _(i):
        at = pl.ds(pl.multiple_of(i * 128, 128), 128)
        squares = jnp.square(text[at, :].astype(jnp.float32))
        norm = jnp.sum(squares, axis=1, keepdims=True) + epsilon
        text_scale[at, :] = jnp.broadcast_to(temper * lax.rsqrt(norm), (128, 128))

    def scale_block(block):
        flat = image.at[block].reshape(depth, columns)
        norm = jnp.zeros((8, columns), jnp.float32)
        for r in range(0, depth, 32):
            part = jnp.square(flat[r : r + 32, :].astype(jnp.float32))
            norm += jnp.sum(part.reshape(4, 8, columns), axis=0)
        norm = jnp.sum(norm, axis=0, keepdims=True) + epsilon
        image_scale[block] = lax.rsqrt(norm)

    def product(block, out):
        flat = image.at[block].reshape(depth, columns)
        out[...] = jnp.dot(text[...], flat[...], preferred_element_type=jnp.float32)

    def losses(block, products):
        owner, high = block // 2, block % 2
        across = image_scale[block]
        image_total = jnp.zeros((8, columns), jnp.float32)
        step = 32
        for r in range(0, rows, step):
            at = slice(r, r + step)
            down = text_scale[at, :]
            down = jnp.concatenate([down] * (columns // 128), axis=1)
            logit = products[at, :] * down * across + offset
            if first and high == 0 and r < 128:
                mine = owner == (core ^ (r // 64))
                shift = jnp.where(mine, narrow * 64 + r % 64, -columns)
                i = lax.broadcasted_iota(jnp.int32, logit.shape, 0)
                j = lax.broadcasted_iota(jnp.int32, logit.shape, 1)
                logit = jnp.where(j - i == shift, -logit, logit)
            loss = softplus(logit)
            image_total += jnp.sum(loss.reshape(step // 8, 8, columns), axis=0)
            total[at, :] += sum(loss[:, lane : lane + 128] for lane in range(0, columns, 128))
        summed = jnp.sum(image_total, axis=0, keepdims=True)
        for j in range(columns // 128):
            row = (high * 2 + ((j // 2) ^ low)) * 4 + owner * 2 + j % 2
            lanes = summed[:, j * 128 : (j + 1) * 128]
            image_sums[pl.ds(row, 1), :] = lanes

    buffers = (even, odd)
    for block in range(5):
        if block < 4:
            if first:
                scale_block(block)
            product(block, buffers[block % 2])
        if block > 0:
            losses(block - 1, buffers[(block - 1) % 2])

    text_sums[...] = jnp.zeros_like(text_sums) if first else before_text[...]
    for i, planes in enumerate((0, 1, 7, 2, 6) if first else (3, 5, 4)):
        summed = jnp.sum(total[i * 128 : (i + 1) * 128, :].T, axis=0, keepdims=True)
        summed = jnp.where(core == 0, summed, pltpu.roll(summed, 64, 1))
        row = planes // 2 * 4 + planes % 2
        text_sums[row : row + 1, :] = summed
    if not first:
        images_all = image_sums[...] + before_image[...]
        keep_out[...] = jnp.where(core == 0, images_all, text_sums[...])
        give_out[...] = jnp.where(core == 0, text_sums[...], images_all)


def pair_sums(sharpness, offsets, place, texts, operands, first):
    rows = sum(text.shape[0] for text in texts)
    depth = texts[0].shape[1]
    features, columns = operands[0].shape[-2:]
    sums = jax.ShapeDtypeStruct((16, 128), jnp.float32)
    outs = [sums, sums]
    buffers = [
        pltpu.VMEM((rows, depth), jnp.bfloat16),
        pltpu.VMEM((rows, columns), jnp.float32),
        pltpu.VMEM((rows, columns), jnp.float32),
        pltpu.VMEM((rows, 128), jnp.float32),
        pltpu.VMEM((rows, 128), jnp.float32),
    ]
    if first:
        outs += [
            jax.ShapeDtypeStruct((4, LO, X, features, columns), jnp.bfloat16),
            jax.ShapeDtypeStruct((4, 1, columns), jnp.float32),
        ]
    else:
        buffers = [pltpu.VMEM((16, 128), jnp.float32)] * 2 + buffers
    operands = (*texts, *operands)
    return pl.pallas_call(
        functools.partial(pair_kernel, texts=len(texts), first=first),
        in_specs=[SMEM] * 3 + [VMEM] * len(operands),
        out_specs=[VMEM] * len(outs),
        out_shape=outs,
        scratch_shapes=buffers,
        compiler_params=pltpu.CompilerParams(vmem_limit_bytes=24 * 1024 * 1024),
        cost_estimate=pl.CostEstimate(
            flops=8 * rows * columns * depth,
            bytes_accessed=2 * depth * (rows + 4 * columns),
            transcendentals=8 * rows * columns,
        ),
    )(sharpness, offsets, place, *operands)


def spread_kernel(place, keep_ref, got_ref, out_ref):
    narrow, hi, core, z = place[0], place[1], place[2], place[3]
    y = hi * 2 + narrow // X
    out_ref[...] = jnp.zeros_like(out_ref)

    @pl.when(core == 0)
    def _():
        for model, ref in enumerate((keep_ref, got_ref)):
            for dy in range(HI * LO):
                for x in range(X):
                    row, lanes = dy * 4 + x // 2, slice(x % 2 * 64, x % 2 * 64 + 64)
                    out_ref[(y ^ dy) * X + x, model : model + 1, :] = jnp.concatenate(
                        [ref[row : row + 1, lanes], ref[row + 2 : row + 3, lanes]], axis=1
                    )

    @pl.when(core == 1)
    def _():
        for model, ref in enumerate((keep_ref, got_ref)):
            for planes in range(Z):
                row = planes // 2 * 4 + planes % 2
                to = lax.rem(z + Z - planes, Z)
                out_ref[to * HI + hi, model : model + 1, :] = ref[row : row + 1, :]


def last_kernel(place, mine_ref, got_ref, image_ref, text_ref):
    mine, got = jnp.sum(mine_ref[...], axis=0), jnp.sum(got_ref[...], axis=0)

    @pl.when(place[2] == 0)
    def _():
        image_ref[...] = mine[:, :64]
        text_ref[0:1, :] = got[1:2, :64]
        text_ref[1:2, :] = got[0:1, :64]

    @pl.when(place[2] == 1)
    def _():
        image_ref[...] = got[:, 64:]
        text_ref[0:1, :] = mine[1:2, 64:]
        text_ref[1:2, :] = mine[0:1, 64:]


def reduce_sums(place, keep, give):
    def part(*shape):
        return jax.ShapeDtypeStruct(shape, jnp.float32)

    def call(kernel, specs, outs, *operands):
        return pl.pallas_call(
            kernel,
            in_specs=specs,
            out_specs=[VMEM] * len(outs),
            out_shape=outs,
            compiler_params=SMALL,
        )(*operands)

    groups = groups_by(
        lambda hi, z, c, lo, x: (c, lo, x) if c else (c, z, 0),
        lambda hi, z, c, lo, x: (z, hi) if c else (hi, lo, x),
    )
    chunks = HI * LO * X
    (sums,) = call(
        spread_kernel, [SMEM, VMEM, VMEM], [part(chunks, 2, 128)], place, keep, send_core(give)
    )
    mine = exchange(sums, groups)
    got = send_core(mine)
    return call(last_kernel, [SMEM, VMEM, VMEM], [part(2, 64)] * 2, place, mine, got)


def on_device(
    student_picture_vectors,
    student_caption_vectors,
    teacher_picture_vectors,
    teacher_caption_vectors,
    sharpness_factors,
    offset_couple,
):
    features = student_picture_vectors.shape[0]
    narrow = lax.axis_index("narrow")
    wide = lax.axis_index("wide")
    core = wide % CORES
    place = jnp.stack([narrow, wide // (Z * CORES), core, wide // CORES % Z]).astype(jnp.int32)
    learner = core == 0

    own_pictures, pictures, shares = start(
        (student_picture_vectors, teacher_picture_vectors),
        (student_caption_vectors, teacher_caption_vectors),
    )

    by_row = groups_by(lambda hi, z, c, lo, x: (hi, z), lambda hi, z, c, lo, x: (c, lo, x))
    text = text_rows(place, exchange(shares, by_row), features)

    other_pictures = send_core(pictures)
    both = jnp.where(
        learner,
        jnp.stack([own_pictures, other_pictures]),
        jnp.stack([other_pictures, own_pictures]),
    )
    ring = [both] + [send_first(both, d) for d in (1, 2, 3)]
    _, *ring = lax.optimization_barrier((text, *ring))
    line = jnp.stack(ring)
    one, three = send_second(line, 1), send_second(line, 3)
    two_low, two_high = send_second(three[:2], 1), send_second(one[2:], 3)

    up1, down1 = send_z(text, 1), send_z(text, -1)
    up2, down2 = send_z(up1, 1), send_z(down1, -1)
    up3, down3 = send_z(up2, 1), send_z(down2, -1)
    middle = text.shape[0] // 2
    up4, down4 = send_z(up3[:middle], 1), send_z(down3[middle:], -1)

    scalars = (sharpness_factors, offset_couple, place)
    image_sums, text_sums, image, scale = pair_sums(
        *scalars, (text, up1, down1, up2, down2), (line, one, two_low, two_high, three), True
    )
    keep, give = pair_sums(
        *scalars, (up3, down3, up4, down4), (image, scale, image_sums, text_sums), False
    )
    return tuple(reduce_sums(place, keep, give))


def solution(mesh):
    return jax.shard_map(
        on_device,
        mesh=mesh,
        in_specs=(
            P("narrow", "wide"),
            P("narrow", "wide"),
            P("narrow", "wide"),
            P("narrow", "wide"),
            P(),
            P(),
        ),
        out_specs=(P(None, ("wide", "narrow")), P(None, ("wide", "narrow"))),
        check_vma=False,
    )
```

time: 454 us -> 92.5 us (0.20); the launches traced: 446 us -> 91.4 us
  waiting for transfers between devices: 234 us -> 22.4 us
  blocking collectives: 162 us -> 15.4 us
  starting transfers between devices: 0.16 us -> 34.7 us
  Pallas kernels: 0 us -> 16.8 us
  matrix products: 16.1 us -> 0 us
  between operations: 15.2 us -> 0.74 us
  other arithmetic: 11.1 us -> 1.26 us
  local copies, waits for them, and re-layouts: 7 us -> 0.12 us
    all_gather x4 -> x0, waiting for transfers between devices: 233 us -> none  [the longest x1 94.3 us: on_device(): lax.all_gather(text_pair[0], 'wide', axis=0, tiled=True)]
    unnamed x2 -> x0, blocking collectives: 140 us -> none
    ppermute x0 -> x18, starting transfers between devices: none -> 30.9 us  [send(): return lax.ppermute(value, AXES, pairs)]
    ppermute x0 -> x18, waiting for transfers between devices: none -> 18.9 us  [send(): return lax.ppermute(value, AXES, pairs)]
    pallas_call x0 -> x6, Pallas kernels: none -> 16.8 us  [the longest x2 12.1 us: pair_sums(): pl.pallas_call(functools.partial(pair_kernel, texts=len(texts), first=fir...]
    dot_general x2 -> x0, matrix products: 16.1 us -> none  [pair_losses(): jnp.dot(text_rows, image_cols, preferred_element_type=jnp.float32)]
    reduce_sum x4 -> x0, other arithmetic: 9.95 us -> none  [the longest x2 6.8 us: row_norms(): jnp.sum(jnp.square(rows_in.astype(jnp.float32)), axis=1) + epsilon]
    all_to_all x2 -> x1, blocking collectives: 22.1 us -> 15.4 us  [exchange(): lax.all_to_all(value, AXES, 0, 0, axis_index_groups=groups, tiled=True)]
  transfers between devices with their start and end apart: 4 -> 19, of which waited for: 4 -> 10; matrix products, arithmetic and copies ran while one was open for 3% -> 1% of each run, Pallas kernels for 0% -> 9%
where the time goes in v1:
time: 92.5 us; the launch traced here: 91.4 us
  starting transfers between devices  34.7 us (38%)
  waiting for transfers between devices  22.4 us (24%)
  Pallas kernels  16.8 us (18%)
  blocking collectives  15.4 us (17%)
  other arithmetic  1.26 us (1%)
    ppermute x18, starting transfers between devices, send(): return lax.ppermute(value, AXES, pairs)  30.9 us
    ppermute x18, waiting for transfers between devices, send(): return lax.ppermute(value, AXES, pairs)  18.9 us
    all_to_all x1, blocking collectives, exchange(): lax.all_to_all(value, AXES, 0, 0, axis_index_groups=groups, tiled=True)  15.4 us
    pallas_call x2, Pallas kernels, pair_sums(): pl.pallas_call(functools.partial(pair_kernel, texts=len(texts), first=fir...  12.1 us
    all_to_all x1, starting transfers between devices, exchange(): lax.all_to_all(value, AXES, 0, 0, axis_index_groups=groups, tiled=True)  3.71 us
    all_to_all x1, waiting for transfers between devices, exchange(): lax.all_to_all(value, AXES, 0, 0, axis_index_groups=groups, tiled=True)  3.47 us
    pallas_call x1, Pallas kernels, start(): pl.pallas_call(start_kernel, in_specs=[VMEM] * 4, out_specs=[VMEM] * 3, o...  2.09 us
  transfers between devices with their start and end apart: 19, of which 10 were waited for; matrix products, arithmetic and copies ran while one was open for 1% of the time, Pallas kernels for 9%

profile of v1, /device:TPU:1, one launch (start us, length us, event | category | flops | bytes accessed | tf_op | source)
XLA Modules:
  0.0 91.4 jit_solution(17192985033564944148)
XLA Ops:
  0.6 2.1 %shard_map.77 = (bf16[144,512]{1,0:T(8,128)(2,1)}, bf16[144,512]{1,0:T(8,128)(2,1)}, bf16[16,80,128]{2,1,0:T(8,128)(2,1)}) custom-call(bf16[144,512]{1,0:T(8,128)(2,1)} %p0.1, bf16[144,512]{1,0:T(8,128)(2,1)} %p1.1, bf16[144,512]{1,0:T(8,128)(2,1)} %c0.1, bf16[144,512]{1,0:T(8,128)(2,1)} %c1.1), custom_call_target="tpu_custom_call" | custom-call | tf_op jit(solution)/shard_map/pallas_call | solution.py:102
  2.7 3.2 %collective-permute-start.8 = (bf16[144,512]{1,0:T(8,128)(2,1)}, bf16[144,512]{1,0:T(8,128)(2,1)S(1)}, u32[]{:S(2)}, u32[]{:S(2)}) collective-permute-start(bf16[144,512]{1,0:T(8,128)(2,1)} %get-tuple-element.17), channel_id=1, source_target_pairs={{0,8},{1,9},{2,10},{3,11},{4,12},{5,13},{6,14},{7,15},{8,0},{9,1},... | collective-permute-start | bytes 442376 | tf_op jit(solution)/shard_map/ppermute | solution.py:32
  6.0 3.7 %all-to-all-start = ((bf16[16,80,128]{2,1,0:T(8,128)(2,1)}), bf16[16,80,128]{2,1,0:T(8,128)(2,1)S(1)}, u32[]{:S(2)}, u32[]{:S(2)}) async-start(bf16[16,80,128]{2,1,0:T(8,128)(2,1)} %get-tuple-element.15), calls=%async_computation | async-start | bytes 655360 | tf_op jit(solution)/shard_map/all_to_all | solution.py:68
  9.7 0.0 collective-permute-done.8
  9.7 1.0 %maximum_select_fusion = bf16[2,144,512]{2,1,0:T(8,128)(2,1)S(1)} fusion(bf16[1,144,512]{2,1,0:T(8,128)(2,1)S(1)} %bitcast.15, bf16[1,144,512]{2,1,0:T(8,128)(2,1)} %bitcast.14, pred[]{:T(512)S(6)} %eq.6), kind=kLoop, calls=%fused_computation.1 | loop fusion | flops 442368 | bytes 589825 | tf_op jit(solution)/shard_map/jit(_where)/select_n | solution.py:383
  10.7 2.7 %collective-permute-start.10 = (bf16[2,144,512]{2,1,0:T(8,128)(2,1)S(1)}, bf16[2,144,512]{2,1,0:T(8,128)(2,1)S(1)}, u32[]{:S(2)}, u32[]{:S(2)}) collective-permute-start(bf16[2,144,512]{2,1,0:T(8,128)(2,1)S(1)} %maximum_select_fusion), channel_id=1, source_target_pairs={{0,2},{1,3},{2,0},{3,1},{4,6},{5,7},{6,4},{7,5},{8,136},{9,137},{1... | collective-permute-start | bytes 884744 | tf_op jit(solution)/shard_map/ppermute | solution.py:32
  13.4 1.2 %collective-permute-start.11 = (bf16[2,144,512]{2,1,0:T(8,128)(2,1)S(1)}, bf16[2,144,512]{2,1,0:T(8,128)(2,1)S(1)}, u32[]{:S(2)}, u32[]{:S(2)}) collective-permute-start(bf16[2,144,512]{2,1,0:T(8,128)(2,1)S(1)} %maximum_select_fusion), channel_id=1, source_target_pairs={{0,3},{1,2},{2,1},{3,0},{4,7},{5,6},{6,5},{7,4},{8,140},{9,141},{1... | collective-permute-start | bytes 884744 | tf_op jit(solution)/shard_map/ppermute | solution.py:32
  14.6 0.0 collective-permute-start.9
  14.6 0.1 pad_add_fusion.place
  14.7 3.5 %all-to-all-done.in_ref = bf16[16,80,128]{2,1,0:T(8,128)(2,1)S(1)} async-done(((bf16[16,80,128]{2,1,0:T(8,128)(2,1)}), bf16[16,80,128]{2,1,0:T(8,128)(2,1)S(1)}, u32[]{:S(2)}, u32[]{:S(2)}) %all-to-all-start) | async-done | bytes 327712 | tf_op jit(solution)/shard_map/all_to_all | solution.py:68
  18.1 0.8 shard_map.78.refs_0_
  19.0 1.7 %collective-permute-done.10 = bf16[2,144,512]{2,1,0:T(8,128)(2,1)S(1)} collective-permute-done((bf16[2,144,512]{2,1,0:T(8,128)(2,1)S(1)}, bf16[2,144,512]{2,1,0:T(8,128)(2,1)S(1)}, u32[]{:S(2)}, u32[]{:S(2)}) %collective-permute-start.10) | collective-permute-done | bytes 294944 | tf_op jit(solution)/shard_map/ppermute | solution.py:32
  20.7 1.8 %collective-permute-done.11 = bf16[2,144,512]{2,1,0:T(8,128)(2,1)S(1)} collective-permute-done((bf16[2,144,512]{2,1,0:T(8,128)(2,1)S(1)}, bf16[2,144,512]{2,1,0:T(8,128)(2,1)S(1)}, u32[]{:S(2)}, u32[]{:S(2)}) %collective-permute-start.11) | collective-permute-done | bytes 294944 | tf_op jit(solution)/shard_map/ppermute | solution.py:32
  22.4 1.2 %collective-permute-done.9 = bf16[2,144,512]{2,1,0:T(8,128)(2,1)S(1)} collective-permute-done((bf16[2,144,512]{2,1,0:T(8,128)(2,1)S(1)}, bf16[2,144,512]{2,1,0:T(8,128)(2,1)S(1)}, u32[]{:S(2)}, u32[]{:S(2)}) %collective-permute-start.9) | collective-permute-done | bytes 294944 | tf_op jit(solution)/shard_map/ppermute | solution.py:32
  23.7 0.1 pad_maximum_fusion.refs_5_
  23.8 0.0 copy-start
  23.8 0.0 copy-start.1
  23.8 2.2 %collective-permute-start.13 = (bf16[4,2,144,512]{3,2,1,0:T(8,128)(2,1)S(1)}, bf16[4,2,144,512]{3,2,1,0:T(8,128)(2,1)S(1)}, u32[]{:S(2)}, u32[]{:S(2)}) collective-permute-start(bf16[4,2,144,512]{3,2,1,0:T(8,128)(2,1)S(1)} %pad_maximum_fusion.refs_5_), channel_id=1, source_target_pairs={{0,132},{1,133},{2,134},{3,135},{4,128},{5,129},{6,130},{7,131},{8... | collective-permute-start | bytes 3538952 | tf_op jit(solution)/shard_map/ppermute | solution.py:32
  26.0 0.0 collective-permute-start.12
  26.0 1.6 %collective-permute-start = (bf16[128,1152]{1,0:T(8,128)(2,1)S(1)}, bf16[128,1152]{1,0:T(8,128)(2,1)S(1)}, u32[]{:S(2)}, u32[]{:S(2)}) collective-permute-start(bf16[128,1152]{1,0:T(8,128)(2,1)S(1)} %shard_map.78.refs_0_), channel_id=1, source_target_pairs={{0,16},{1,17},{2,18},{3,19},{4,20},{5,21},{6,22},{7,23},{8,24},{9,... | collective-permute-start | bytes 884744 | tf_op jit(solution)/shard_map/ppermute | solution.py:32
  27.7 3.9 %collective-permute-start.3 = (bf16[128,1152]{1,0:T(8,128)(2,1)S(1)}, bf16[128,1152]{1,0:T(8,128)(2,1)S(1)}, u32[]{:S(2)}, u32[]{:S(2)}) collective-permute-start(bf16[128,1152]{1,0:T(8,128)(2,1)S(1)} %shard_map.78.refs_0_), channel_id=1, source_target_pairs={{0,112},{1,113},{2,114},{3,115},{4,116},{5,117},{6,118},{7,119},{8... | collective-permute-start | bytes 884744 | tf_op jit(solution)/shard_map/ppermute | solution.py:32
  31.6 5.9 %collective-permute-done.refs_1_ = bf16[128,1152]{1,0:T(8,128)(2,1)S(1)} collective-permute-done((bf16[128,1152]{1,0:T(8,128)(2,1)S(1)}, bf16[128,1152]{1,0:T(8,128)(2,1)S(1)}, u32[]{:S(2)}, u32[]{:S(2)}) %collective-permute-start) | collective-permute-done | bytes 294944 | tf_op jit(solution)/shard_map/ppermute | solution.py:32
  37.5 0.0 collective-permute-start.1
  37.5 0.0 collective-permute-done.3.refs_2_
  37.5 2.7 %collective-permute-start.4 = (bf16[128,1152]{1,0:T(8,128)(2,1)S(1)}, bf16[128,1152]{1,0:T(8,128)(2,1)S(1)}, u32[]{:S(2)}, u32[]{:S(2)}) collective-permute-start(bf16[128,1152]{1,0:T(8,128)(2,1)S(1)} %collective-permute-done.3.refs_2_), channel_id=1, source_target_pairs={{0,112},{1,113},{2,114},{3,115},{4,116},{5,117},{6,118},{7,119},{8... | collective-permute-start | bytes 884744 | tf_op jit(solution)/shard_map/ppermute | solution.py:32
  40.2 0.3 collective-permute-done.13.refs_9_
  40.5 2.6 %collective-permute-start.14 = (bf16[2,2,144,512]{3,2,1,0:T(8,128)(2,1)S(1)}, bf16[2,2,144,512]{3,2,1,0:T(8,128)(2,1)S(1)}, u32[]{:S(2)}, u32[]{:S(2)}) collective-permute-start(bf16[2,2,144,512]{3,2,1,0:T(8,128)(2,1)S(1)} %slice.18), channel_id=1, source_target_pairs={{0,4},{1,5},{2,6},{3,7},{4,0},{5,1},{6,2},{7,3},{8,9},{9,8},{10,11... | collective-permute-start | bytes 1769480 | tf_op jit(solution)/shard_map/ppermute | solution.py:32
  43.2 0.0 collective-permute-done.12.refs_6_
  43.2 0.3 collective-permute-start.15
  43.5 1.8 %collective-permute-done.1.refs_3_ = bf16[128,1152]{1,0:T(8,128)(2,1)S(1)} collective-permute-done((bf16[128,1152]{1,0:T(8,128)(2,1)S(1)}, bf16[128,1152]{1,0:T(8,128)(2,1)S(1)}, u32[]{:S(2)}, u32[]{:S(2)}) %collective-permute-start.1) | collective-permute-done | bytes 294944 | tf_op jit(solution)/shard_map/ppermute | solution.py:32
  45.2 0.0 collective-permute-start.2
  45.2 0.0 collective-permute-done.4.refs_4_
  45.2 3.3 %collective-permute-start.5 = (bf16[128,1152]{1,0:T(8,128)(2,1)S(1)}, bf16[128,1152]{1,0:T(8,128)(2,1)S(1)}, u32[]{:S(2)}, u32[]{:S(2)}) collective-permute-start(bf16[128,1152]{1,0:T(8,128)(2,1)S(1)} %collective-permute-done.4.refs_4_), channel_id=1, source_target_pairs={{0,112},{1,113},{2,114},{3,115},{4,116},{5,117},{6,118},{7,119},{8... | collective-permute-start | bytes 884744 | tf_op jit(solution)/shard_map/ppermute | solution.py:32
  48.5 4.6 %collective-permute-done.2.refs_0_ = bf16[128,1152]{1,0:T(8,128)(2,1)S(1)} collective-permute-done((bf16[128,1152]{1,0:T(8,128)(2,1)S(1)}, bf16[128,1152]{1,0:T(8,128)(2,1)S(1)}, u32[]{:S(2)}, u32[]{:S(2)}) %collective-permute-start.2) | collective-permute-done | bytes 294944 | tf_op jit(solution)/shard_map/ppermute | solution.py:32
  53.1 0.1 collective-permute-start.6
  53.2 2.7 %collective-permute-start.7 = (bf16[64,1152]{1,0:T(8,128)(2,1)S(1)}, bf16[64,1152]{1,0:T(8,128)(2,1)S(1)}, u32[]{:S(2)}, u32[]{:S(2)}) collective-permute-start(bf16[64,1152]{1,0:T(8,128)(2,1)S(1)} %slice.17), channel_id=1, source_target_pairs={{0,112},{1,113},{2,114},{3,115},{4,116},{5,117},{6,118},{7,119},{8... | collective-permute-start | bytes 442376 | tf_op jit(solution)/shard_map/ppermute | solution.py:32
  56.0 0.0 collective-permute-done.15.refs_8_
  56.0 7.6 %shard_map.79 = (f32[16,128]{1,0:T(8,128)S(1)}, f32[16,128]{1,0:T(8,128)S(1)}, bf16[4,2,4,144,512]{4,3,2,1,0:T(8,128)(2,1)S(1)}, f32[4,1,512]{2,1,0:T(1,128)S(1)}) custom-call(f32[2]{0:T(128)S(1)} %copy-done, f32[2]{0:T(128)S(1)} %copy-done.1, s32[4]{0:T(128)S(1)} %pad_add_fusion.place, bf16[128,1152]{1,0:T(8,128)(2,1)S(1)} %shard_map.78.refs_0_, ...), custom_call_target="tpu_custom_call" | custom-call | flops 3019898880 | bytes 6193152 | tf_op jit(solution)/shard_map/pallas_call | solution.py:278
  63.6 0.0 collective-permute-done.6.refs_2_
  63.6 0.0 collective-permute-done.7.refs_3_
  63.6 4.5 %shard_map.80 = (f32[16,128]{1,0:T(8,128)S(1)}, f32[16,128]{1,0:T(8,128)S(1)}) custom-call(f32[2]{0:T(128)S(1)} %copy-done, f32[2]{0:T(128)S(1)} %copy-done.1, s32[4]{0:T(128)S(1)} %pad_add_fusion.place, bf16[128,1152]{1,0:T(8,128)(2,1)S(1)} %collective-permute-done.2.refs_0_, bf16[128,1152]{1,0:T(8,128)(2,1)S(1)} %collective-permute-done.5.refs_1_, ...), custom_call_target="tpu_custom_call" | custom-call | flops 1811939328 | bytes 5603328 | tf_op jit(solution)/shard_map/pallas_call | solution.py:278
  68.1 3.9 %collective-permute-start.16 = (f32[16,128]{1,0:T(8,128)S(1)}, f32[16,128]{1,0:T(8,128)S(1)}, u32[]{:S(2)}, u32[]{:S(2)}) collective-permute-start(f32[16,128]{1,0:T(8,128)S(1)} %get-tuple-element.27), channel_id=1, source_target_pairs={{0,8},{1,9},{2,10},{3,11},{4,12},{5,13},{6,14},{7,15},{8,0},{9,1},... | collective-permute-start | bytes 24584 | tf_op jit(solution)/shard_map/ppermute | solution.py:32
  72.0 0.8 collective-permute-done.16.got_ref
  72.8 0.6 shard_map.81
  73.4 15.4 %all_to_all.10.mine_ref = f32[16,2,128]{2,1,0:T(2,128)S(1)} all-to-all(f32[16,2,128]{2,1,0:T(2,128)S(1)} %shard_map.81), channel_id=1, replica_groups={{0,1,2,3,4,5,6,7,128,129,130,131,132,133,134,135},{8,136,24,152,40,168,..., dimensions={0} | all-to-all | bytes 32768 | tf_op jit(solution)/shard_map/all_to_all | solution.py:68
  88.8 0.5 collective-permute-start.17
  89.3 0.8 collective-permute-done.17.got_ref
  90.2 1.2 %shard_map.82 = (f32[2,64]{1,0:T(2,128)}, f32[2,64]{1,0:T(2,128)}) custom-call(s32[4]{0:T(128)S(1)} %pad_add_fusion.place, f32[16,2,128]{2,1,0:T(2,128)S(1)} %all_to_all.10.mine_ref, f32[16,2,128]{2,1,0:T(2,128)S(1)} %collective-permute-done.17.got_ref), custom_call_target="tpu_custom_call" | custom-call | tf_op jit(solution)/shard_map/pallas_call | solution.py:338
  (8 shorter events, 0.1 us)
Async XLA Ops:
  2.7 7.0 %collective-permute-start.8 = (bf16[144,512]{1,0:T(8,128)(2,1)}, bf16[144,512]{1,0:T(8,128)(2,1)S(1)}, u32[]{:S(2)}, u32[]{:S(2)}) collective-permute-start(bf16[144,512]{1,0:T(8,128)(2,1)} %get-tuple-element.17), channel_id=1, source_target_pairs={{0,8},{1,9},{2,10},{3,11},{4,12},{5,13},{6,14},{7,15},{8,0},{9,1},... | collective-permute-start | bytes 442376 | tf_op jit(solution)/shard_map/ppermute | solution.py:32
  6.0 12.2 %all-to-all-start = ((bf16[16,80,128]{2,1,0:T(8,128)(2,1)}), bf16[16,80,128]{2,1,0:T(8,128)(2,1)S(1)}, u32[]{:S(2)}, u32[]{:S(2)}) async-start(bf16[16,80,128]{2,1,0:T(8,128)(2,1)} %get-tuple-element.15), calls=%async_computation | async-start | bytes 655360 | tf_op jit(solution)/shard_map/all_to_all | solution.py:68
  10.7 10.0 %collective-permute-start.10 = (bf16[2,144,512]{2,1,0:T(8,128)(2,1)S(1)}, bf16[2,144,512]{2,1,0:T(8,128)(2,1)S(1)}, u32[]{:S(2)}, u32[]{:S(2)}) collective-permute-start(bf16[2,144,512]{2,1,0:T(8,128)(2,1)S(1)} %maximum_select_fusion), channel_id=1, source_target_pairs={{0,2},{1,3},{2,0},{3,1},{4,6},{5,7},{6,4},{7,5},{8,136},{9,137},{1... | collective-permute-start | bytes 884744 | tf_op jit(solution)/shard_map/ppermute | solution.py:32
  13.4 9.0 %collective-permute-start.11 = (bf16[2,144,512]{2,1,0:T(8,128)(2,1)S(1)}, bf16[2,144,512]{2,1,0:T(8,128)(2,1)S(1)}, u32[]{:S(2)}, u32[]{:S(2)}) collective-permute-start(bf16[2,144,512]{2,1,0:T(8,128)(2,1)S(1)} %maximum_select_fusion), channel_id=1, source_target_pairs={{0,3},{1,2},{2,1},{3,0},{4,7},{5,6},{6,5},{7,4},{8,140},{9,141},{1... | collective-permute-start | bytes 884744 | tf_op jit(solution)/shard_map/ppermute | solution.py:32
  14.6 9.1 %collective-permute-start.9 = (bf16[2,144,512]{2,1,0:T(8,128)(2,1)S(1)}, bf16[2,144,512]{2,1,0:T(8,128)(2,1)S(1)}, u32[]{:S(2)}, u32[]{:S(2)}) collective-permute-start(bf16[2,144,512]{2,1,0:T(8,128)(2,1)S(1)} %maximum_select_fusion), channel_id=1, source_target_pairs={{0,1},{1,0},{2,3},{3,2},{4,5},{5,4},{6,7},{7,6},{8,12},{9,13},{10,... | collective-permute-start | bytes 884744 | tf_op jit(solution)/shard_map/ppermute | solution.py:32
  23.8 32.1 %copy-start = (f32[2]{0:T(128)S(1)}, f32[2]{0:T(128)}, u32[]{:S(2)}) copy-start(f32[2]{0:T(128)} %sharpness.3) | copy-start | bytes 28
  23.8 32.1 %copy-start.1 = (f32[2]{0:T(128)S(1)}, f32[2]{0:T(128)}, u32[]{:S(2)}) copy-start(f32[2]{0:T(128)} %offsets.3) | copy-start | bytes 28
  23.8 16.6 %collective-permute-start.13 = (bf16[4,2,144,512]{3,2,1,0:T(8,128)(2,1)S(1)}, bf16[4,2,144,512]{3,2,1,0:T(8,128)(2,1)S(1)}, u32[]{:S(2)}, u32[]{:S(2)}) collective-permute-start(bf16[4,2,144,512]{3,2,1,0:T(8,128)(2,1)S(1)} %pad_maximum_fusion.refs_5_), channel_id=1, source_target_pairs={{0,132},{1,133},{2,134},{3,135},{4,128},{5,129},{6,130},{7,131},{8... | collective-permute-start | bytes 3538952 | tf_op jit(solution)/shard_map/ppermute | solution.py:32
  26.0 17.1 %collective-permute-start.12 = (bf16[4,2,144,512]{3,2,1,0:T(8,128)(2,1)S(1)}, bf16[4,2,144,512]{3,2,1,0:T(8,128)(2,1)S(1)}, u32[]{:S(2)}, u32[]{:S(2)}) collective-permute-start(bf16[4,2,144,512]{3,2,1,0:T(8,128)(2,1)S(1)} %pad_maximum_fusion.refs_5_), channel_id=1, source_target_pairs={{0,4},{1,5},{2,6},{3,7},{4,0},{5,1},{6,2},{7,3},{8,9},{9,8},{10,11... | collective-permute-start | bytes 3538952 | tf_op jit(solution)/shard_map/ppermute | solution.py:32
  26.0 11.5 %collective-permute-start = (bf16[128,1152]{1,0:T(8,128)(2,1)S(1)}, bf16[128,1152]{1,0:T(8,128)(2,1)S(1)}, u32[]{:S(2)}, u32[]{:S(2)}) collective-permute-start(bf16[128,1152]{1,0:T(8,128)(2,1)S(1)} %shard_map.78.refs_0_), channel_id=1, source_target_pairs={{0,16},{1,17},{2,18},{3,19},{4,20},{5,21},{6,22},{7,23},{8,24},{9,... | collective-permute-start | bytes 884744 | tf_op jit(solution)/shard_map/ppermute | solution.py:32
  27.7 9.9 %collective-permute-start.3 = (bf16[128,1152]{1,0:T(8,128)(2,1)S(1)}, bf16[128,1152]{1,0:T(8,128)(2,1)S(1)}, u32[]{:S(2)}, u32[]{:S(2)}) collective-permute-start(bf16[128,1152]{1,0:T(8,128)(2,1)S(1)} %shard_map.78.refs_0_), channel_id=1, source_target_pairs={{0,112},{1,113},{2,114},{3,115},{4,116},{5,117},{6,118},{7,119},{8... | collective-permute-start | bytes 884744 | tf_op jit(solution)/shard_map/ppermute | solution.py:32
  37.5 7.7 %collective-permute-start.1 = (bf16[128,1152]{1,0:T(8,128)(2,1)S(1)}, bf16[128,1152]{1,0:T(8,128)(2,1)S(1)}, u32[]{:S(2)}, u32[]{:S(2)}) collective-permute-start(bf16[128,1152]{1,0:T(8,128)(2,1)S(1)} %collective-permute-done.refs_1_), channel_id=1, source_target_pairs={{0,16},{1,17},{2,18},{3,19},{4,20},{5,21},{6,22},{7,23},{8,24},{9,... | collective-permute-start | bytes 884744 | tf_op jit(solution)/shard_map/ppermute | solution.py:32
  37.5 7.7 %collective-permute-start.4 = (bf16[128,1152]{1,0:T(8,128)(2,1)S(1)}, bf16[128,1152]{1,0:T(8,128)(2,1)S(1)}, u32[]{:S(2)}, u32[]{:S(2)}) collective-permute-start(bf16[128,1152]{1,0:T(8,128)(2,1)S(1)} %collective-permute-done.3.refs_2_), channel_id=1, source_target_pairs={{0,112},{1,113},{2,114},{3,115},{4,116},{5,117},{6,118},{7,119},{8... | collective-permute-start | bytes 884744 | tf_op jit(solution)/shard_map/ppermute | solution.py:32
  40.5 15.4 %collective-permute-start.14 = (bf16[2,2,144,512]{3,2,1,0:T(8,128)(2,1)S(1)}, bf16[2,2,144,512]{3,2,1,0:T(8,128)(2,1)S(1)}, u32[]{:S(2)}, u32[]{:S(2)}) collective-permute-start(bf16[2,2,144,512]{3,2,1,0:T(8,128)(2,1)S(1)} %slice.18), channel_id=1, source_target_pairs={{0,4},{1,5},{2,6},{3,7},{4,0},{5,1},{6,2},{7,3},{8,9},{9,8},{10,11... | collective-permute-start | bytes 1769480 | tf_op jit(solution)/shard_map/ppermute | solution.py:32
  43.2 12.8 %collective-permute-start.15 = (bf16[2,2,144,512]{3,2,1,0:T(8,128)(2,1)S(1)}, bf16[2,2,144,512]{3,2,1,0:T(8,128)(2,1)S(1)}, u32[]{:S(2)}, u32[]{:S(2)}) collective-permute-start(bf16[2,2,144,512]{3,2,1,0:T(8,128)(2,1)S(1)} %slice.19), channel_id=1, source_target_pairs={{0,132},{1,133},{2,134},{3,135},{4,128},{5,129},{6,130},{7,131},{8... | collective-permute-start | bytes 1769480 | tf_op jit(solution)/shard_map/ppermute | solution.py:32
  45.2 7.8 %collective-permute-start.2 = (bf16[128,1152]{1,0:T(8,128)(2,1)S(1)}, bf16[128,1152]{1,0:T(8,128)(2,1)S(1)}, u32[]{:S(2)}, u32[]{:S(2)}) collective-permute-start(bf16[128,1152]{1,0:T(8,128)(2,1)S(1)} %collective-permute-done.1.refs_3_), channel_id=1, source_target_pairs={{0,16},{1,17},{2,18},{3,19},{4,20},{5,21},{6,22},{7,23},{8,24},{9,... | collective-permute-start | bytes 884744 | tf_op jit(solution)/shard_map/ppermute | solution.py:32
  45.2 8.0 %collective-permute-start.5 = (bf16[128,1152]{1,0:T(8,128)(2,1)S(1)}, bf16[128,1152]{1,0:T(8,128)(2,1)S(1)}, u32[]{:S(2)}, u32[]{:S(2)}) collective-permute-start(bf16[128,1152]{1,0:T(8,128)(2,1)S(1)} %collective-permute-done.4.refs_4_), channel_id=1, source_target_pairs={{0,112},{1,113},{2,114},{3,115},{4,116},{5,117},{6,118},{7,119},{8... | collective-permute-start | bytes 884744 | tf_op jit(solution)/shard_map/ppermute | solution.py:32
  53.1 10.5 %collective-permute-start.6 = (bf16[64,1152]{1,0:T(8,128)(2,1)S(1)}, bf16[64,1152]{1,0:T(8,128)(2,1)S(1)}, u32[]{:S(2)}, u32[]{:S(2)}) collective-permute-start(bf16[64,1152]{1,0:T(8,128)(2,1)S(1)} %slice.16), channel_id=1, source_target_pairs={{0,16},{1,17},{2,18},{3,19},{4,20},{5,21},{6,22},{7,23},{8,24},{9,... | collective-permute-start | bytes 442376 | tf_op jit(solution)/shard_map/ppermute | solution.py:32
  53.2 10.3 %collective-permute-start.7 = (bf16[64,1152]{1,0:T(8,128)(2,1)S(1)}, bf16[64,1152]{1,0:T(8,128)(2,1)S(1)}, u32[]{:S(2)}, u32[]{:S(2)}) collective-permute-start(bf16[64,1152]{1,0:T(8,128)(2,1)S(1)} %slice.17), channel_id=1, source_target_pairs={{0,112},{1,113},{2,114},{3,115},{4,116},{5,117},{6,118},{7,119},{8... | collective-permute-start | bytes 442376 | tf_op jit(solution)/shard_map/ppermute | solution.py:32
  68.1 4.7 %collective-permute-start.16 = (f32[16,128]{1,0:T(8,128)S(1)}, f32[16,128]{1,0:T(8,128)S(1)}, u32[]{:S(2)}, u32[]{:S(2)}) collective-permute-start(f32[16,128]{1,0:T(8,128)S(1)} %get-tuple-element.27), channel_id=1, source_target_pairs={{0,8},{1,9},{2,10},{3,11},{4,12},{5,13},{6,14},{7,15},{8,0},{9,1},... | collective-permute-start | bytes 24584 | tf_op jit(solution)/shard_map/ppermute | solution.py:32
  88.8 1.3 %collective-permute-start.17 = (f32[16,2,128]{2,1,0:T(2,128)S(1)}, f32[16,2,128]{2,1,0:T(2,128)S(1)}, u32[]{:S(2)}, u32[]{:S(2)}) collective-permute-start(f32[16,2,128]{2,1,0:T(2,128)S(1)} %all_to_all.10.mine_ref), channel_id=1, source_target_pairs={{0,8},{1,9},{2,10},{3,11},{4,12},{5,13},{6,14},{7,15},{8,0},{9,1},... | collective-permute-start | bytes 49160 | tf_op jit(solution)/shard_map/ppermute | solution.py:32

commit v2 on v1

--- a/solution.py
+++ b/solution.py
@@ -135,10 +135,17 @@
     )(place, shares)
 
 
-def softplus(value):
-    power = jnp.exp2(jnp.abs(value) * -1.4426950408889634)
-    near = 1.0 + power
-    return jnp.maximum(value, 0.0) + (jnp.log(near) + (power - (near - 1.0)))
+def tail_power(value):
+    return jnp.exp2(jnp.abs(value) * -1.4426950408889634)
+
+
+def both_tails(a, b):
+    return (a + b) + a * b
+
+
+def log_tail(tail):
+    near = 1.0 + tail
+    return jnp.log(near) + (tail - (near - 1.0))
 
 
 def pair_kernel(sharpness, offsets, place, *refs, texts, first):
@@ -204,43 +211,64 @@
         norm = jnp.sum(norm, axis=0, keepdims=True) + epsilon
         image_scale[block] = lax.rsqrt(norm)
 
-    def product(block, out):
+    span = even.shape[0]
+    parts = rows // span
+
+    def product(block, part, out):
         flat = image.at[block].reshape(depth, columns)
-        out[...] = jnp.dot(text[...], flat[...], preferred_element_type=jnp.float32)
-
-    def losses(block, products):
+        out[...] = jnp.dot(
+            text[part * span : (part + 1) * span, :],
+            flat[...],
+            preferred_element_type=jnp.float32,
+        )
+
+    def losses(block, part, products):
         owner, high = block // 2, block % 2
         across = image_scale[block]
         image_total = jnp.zeros((8, columns), jnp.float32)
         step = 32
-        for r in range(0, rows, step):
-            at = slice(r, r + step)
+        column_tail = None
+        for r in range(0, span, step):
+            at = slice(part * span + r, part * span + r + step)
             down = text_scale[at, :]
             down = jnp.concatenate([down] * (columns // 128), axis=1)
-            logit = products[at, :] * down * across + offset
-            if first and high == 0 and r < 128:
+            logit = products[r : r + step, :] * down * across + offset
+            if first and high == 0 and part == 0 and r < 128:
                 mine = owner == (core ^ (r // 64))
                 shift = jnp.where(mine, narrow * 64 + r % 64, -columns)
                 i = lax.broadcasted_iota(jnp.int32, logit.shape, 0)
                 j = lax.broadcasted_iota(jnp.int32, logit.shape, 1)
                 logit = jnp.where(j - i == shift, -logit, logit)
-            loss = softplus(logit)
-            image_total += jnp.sum(loss.reshape(step // 8, 8, columns), axis=0)
-            total[at, :] += sum(loss[:, lane : lane + 128] for lane in range(0, columns, 128))
+            above = jnp.maximum(logit, 0.0)
+            tail = tail_power(logit)
+            tiles = [slice(lane, lane + 128) for lane in range(0, columns, 128)]
+            row_tail = functools.reduce(both_tails, [tail[:, tile] for tile in tiles])
+            total[at, :] += log_tail(row_tail) + sum(above[:, tile] for tile in tiles)
+            for g in range(0, step, 8):
+                group = tail[g : g + 8, :]
+                column_tail = group if column_tail is None else both_tails(column_tail, group)
+            image_total += jnp.sum(above.reshape(step // 8, 8, columns), axis=0)
+            if r % 64 or r + step == span:
+                image_total += log_tail(column_tail)
+                column_tail = None
         summed = jnp.sum(image_total, axis=0, keepdims=True)
         for j in range(columns // 128):
             row = (high * 2 + ((j // 2) ^ low)) * 4 + owner * 2 + j % 2
             lanes = summed[:, j * 128 : (j + 1) * 128]
-            image_sums[pl.ds(row, 1), :] = lanes
-
+            if part == 0:
+                image_sums[pl.ds(row, 1), :] = lanes
+            else:
+                image_sums[pl.ds(row, 1), :] += lanes
+
+    steps = [(block, part) for block in range(4) for part in range(parts)]
     buffers = (even, odd)
-    for block in range(5):
-        if block < 4:
-            if first:
-                scale_block(block)
-            product(block, buffers[block % 2])
-        if block > 0:
-            losses(block - 1, buffers[(block - 1) % 2])
+    for n, step in enumerate(steps + [None]):
+        if step is not None:
+            if first and step[1] == 0:
+                scale_block(step[0])
+            product(*step, buffers[n % 2])
+        if n > 0:
+            losses(*steps[n - 1], buffers[(n - 1) % 2])
 
     text_sums[...] = jnp.zeros_like(text_sums) if first else before_text[...]
     for i, planes in enumerate((0, 1, 7, 2, 6) if first else (3, 5, 4)):
@@ -260,10 +288,11 @@
     features, columns = operands[0].shape[-2:]
     sums = jax.ShapeDtypeStruct((16, 128), jnp.float32)
     outs = [sums, sums]
+    span = rows // (4 if first else 3)
     buffers = [
         pltpu.VMEM((rows, depth), jnp.bfloat16),
-        pltpu.VMEM((rows, columns), jnp.float32),
-        pltpu.VMEM((rows, columns), jnp.float32),
+        pltpu.VMEM((span, columns), jnp.float32),
+        pltpu.VMEM((span, columns), jnp.float32),
         pltpu.VMEM((rows, 128), jnp.float32),
         pltpu.VMEM((rows, 128), jnp.float32),
     ]
@@ -394,15 +423,14 @@
     up1, down1 = send_z(text, 1), send_z(text, -1)
     up2, down2 = send_z(up1, 1), send_z(down1, -1)
     up3, down3 = send_z(up2, 1), send_z(down2, -1)
-    middle = text.shape[0] // 2
-    up4, down4 = send_z(up3[:middle], 1), send_z(down3[middle:], -1)
+    down4 = send_z(down3, -1)
 
     scalars = (sharpness_factors, offset_couple, place)
     image_sums, text_sums, image, scale = pair_sums(
         *scalars, (text, up1, down1, up2, down2), (line, one, two_low, two_high, three), True
     )
     keep, give = pair_sums(
-        *scalars, (up3, down3, up4, down4), (image, scale, image_sums, text_sums), False
+        *scalars, (up3, down3, down4), (image, scale, image_sums, text_sums), False
     )
     return tuple(reduce_sums(place, keep, give))
 

time: 92.5 us -> 91.3 us (0.987)
  starting transfers between devices: 34.7 us -> 35.9 us
    ppermute x18 -> x17, starting transfers between devices: 30.9 us -> 32.2 us  [send(): return lax.ppermute(value, AXES, pairs)]
    ppermute x18 -> x17, waiting for transfers between devices: 18.9 us -> 18.5 us  [send(): return lax.ppermute(value, AXES, pairs)]
  transfers between devices with their start and end apart: 19 -> 18, of which waited for: 10 -> 8; matrix products, arithmetic and copies ran while one was open for 1% -> 1% of each run, Pallas kernels for 9% -> 9%
where the time goes in v2:
time: 91.3 us; the launch traced here: 91.1 us
  starting transfers between devices  35.9 us (39%)
  waiting for transfers between devices  21.7 us (24%)
  Pallas kernels  16.7 us (18%)
  blocking collectives  14.7 us (16%)
  other arithmetic  1.25 us (1%)
    ppermute x17, starting transfers between devices, send(): return lax.ppermute(value, AXES, pairs)  32.2 us
    ppermute x17, waiting for transfers between devices, send(): return lax.ppermute(value, AXES, pairs)  18.5 us
    all_to_all x1, blocking collectives, exchange(): lax.all_to_all(value, AXES, 0, 0, axis_index_groups=groups, tiled=True)  14.7 us
    pallas_call x2, Pallas kernels, pair_sums(): pl.pallas_call(functools.partial(pair_kernel, texts=len(texts), first=fir...  12 us
    all_to_all x1, starting transfers between devices, exchange(): lax.all_to_all(value, AXES, 0, 0, axis_index_groups=groups, tiled=True)  3.71 us
    all_to_all x1, waiting for transfers between devices, exchange(): lax.all_to_all(value, AXES, 0, 0, axis_index_groups=groups, tiled=True)  3.17 us
    pallas_call x1, Pallas kernels, start(): pl.pallas_call(start_kernel, in_specs=[VMEM] * 4, out_specs=[VMEM] * 3, o...  2.07 us
  transfers between devices with their start and end apart: 18, of which 8 were waited for; matrix products, arithmetic and copies ran while one was open for 1% of the time, Pallas kernels for 9%

profile of v2, /device:TPU:1, one launch (start us, length us, event | category | flops | bytes accessed | tf_op | source)
XLA Modules:
  0.0 91.1 jit_solution(1937270097987817294)
XLA Ops:
  0.6 2.1 %shard_map.77 = (bf16[144,512]{1,0:T(8,128)(2,1)}, bf16[144,512]{1,0:T(8,128)(2,1)}, bf16[16,80,128]{2,1,0:T(8,128)(2,1)}) custom-call(bf16[144,512]{1,0:T(8,128)(2,1)} %p0.1, bf16[144,512]{1,0:T(8,128)(2,1)} %p1.1, bf16[144,512]{1,0:T(8,128)(2,1)} %c0.1, bf16[144,512]{1,0:T(8,128)(2,1)} %c1.1), custom_call_target="tpu_custom_call" | custom-call | tf_op jit(solution)/shard_map/pallas_call | solution.py:102
  2.7 3.2 %collective-permute-start.7 = (bf16[144,512]{1,0:T(8,128)(2,1)}, bf16[144,512]{1,0:T(8,128)(2,1)S(1)}, u32[]{:S(2)}, u32[]{:S(2)}) collective-permute-start(bf16[144,512]{1,0:T(8,128)(2,1)} %get-tuple-element.17), channel_id=1, source_target_pairs={{0,8},{1,9},{2,10},{3,11},{4,12},{5,13},{6,14},{7,15},{8,0},{9,1},... | collective-permute-start | bytes 442376 | tf_op jit(solution)/shard_map/ppermute | solution.py:32
  5.9 3.7 %all-to-all-start = ((bf16[16,80,128]{2,1,0:T(8,128)(2,1)}), bf16[16,80,128]{2,1,0:T(8,128)(2,1)S(1)}, u32[]{:S(2)}, u32[]{:S(2)}) async-start(bf16[16,80,128]{2,1,0:T(8,128)(2,1)} %get-tuple-element.15), calls=%async_computation | async-start | bytes 655360 | tf_op jit(solution)/shard_map/all_to_all | solution.py:68
  9.7 0.0 collective-permute-done.7
  9.7 1.0 %maximum_select_fusion = bf16[2,144,512]{2,1,0:T(8,128)(2,1)S(1)} fusion(bf16[1,144,512]{2,1,0:T(8,128)(2,1)S(1)} %bitcast.15, bf16[1,144,512]{2,1,0:T(8,128)(2,1)} %bitcast.14, pred[]{:T(512)S(6)} %eq.6), kind=kLoop, calls=%fused_computation.1 | loop fusion | flops 442368 | bytes 589825 | tf_op jit(solution)/shard_map/jit(_where)/select_n | solution.py:412
  10.7 2.9 %collective-permute-start.10 = (bf16[2,144,512]{2,1,0:T(8,128)(2,1)S(1)}, bf16[2,144,512]{2,1,0:T(8,128)(2,1)S(1)}, u32[]{:S(2)}, u32[]{:S(2)}) collective-permute-start(bf16[2,144,512]{2,1,0:T(8,128)(2,1)S(1)} %maximum_select_fusion), channel_id=1, source_target_pairs={{0,3},{1,2},{2,1},{3,0},{4,7},{5,6},{6,5},{7,4},{8,140},{9,141},{1... | collective-permute-start | bytes 884744 | tf_op jit(solution)/shard_map/ppermute | solution.py:32
  13.6 0.0 collective-permute-start.8
  13.6 1.3 %collective-permute-start.9 = (bf16[2,144,512]{2,1,0:T(8,128)(2,1)S(1)}, bf16[2,144,512]{2,1,0:T(8,128)(2,1)S(1)}, u32[]{:S(2)}, u32[]{:S(2)}) collective-permute-start(bf16[2,144,512]{2,1,0:T(8,128)(2,1)S(1)} %maximum_select_fusion), channel_id=1, source_target_pairs={{0,2},{1,3},{2,0},{3,1},{4,6},{5,7},{6,4},{7,5},{8,136},{9,137},{1... | collective-permute-start | bytes 884744 | tf_op jit(solution)/shard_map/ppermute | solution.py:32
  14.9 0.1 pad_add_fusion.place
  15.0 3.2 %all-to-all-done.in_ref = bf16[16,80,128]{2,1,0:T(8,128)(2,1)S(1)} async-done(((bf16[16,80,128]{2,1,0:T(8,128)(2,1)}), bf16[16,80,128]{2,1,0:T(8,128)(2,1)S(1)}, u32[]{:S(2)}, u32[]{:S(2)}) %all-to-all-start) | async-done | bytes 327712 | tf_op jit(solution)/shard_map/all_to_all | solution.py:68
  18.1 0.8 shard_map.78.refs_0_
  19.0 0.0 collective-permute-done.10
  19.0 1.4 %collective-permute-done.8 = bf16[2,144,512]{2,1,0:T(8,128)(2,1)S(1)} collective-permute-done((bf16[2,144,512]{2,1,0:T(8,128)(2,1)S(1)}, bf16[2,144,512]{2,1,0:T(8,128)(2,1)S(1)}, u32[]{:S(2)}, u32[]{:S(2)}) %collective-permute-start.8) | collective-permute-done | bytes 294944 | tf_op jit(solution)/shard_map/ppermute | solution.py:32
  20.4 4.1 %collective-permute-done.9 = bf16[2,144,512]{2,1,0:T(8,128)(2,1)S(1)} collective-permute-done((bf16[2,144,512]{2,1,0:T(8,128)(2,1)S(1)}, bf16[2,144,512]{2,1,0:T(8,128)(2,1)S(1)}, u32[]{:S(2)}, u32[]{:S(2)}) %collective-permute-start.9) | collective-permute-done | bytes 294944 | tf_op jit(solution)/shard_map/ppermute | solution.py:32
  24.5 0.1 pad_maximum_fusion.refs_5_
  24.7 0.0 copy-start
  24.7 0.0 copy-start.1
  24.7 1.5 %collective-permute-start.12 = (bf16[4,2,144,512]{3,2,1,0:T(8,128)(2,1)S(1)}, bf16[4,2,144,512]{3,2,1,0:T(8,128)(2,1)S(1)}, u32[]{:S(2)}, u32[]{:S(2)}) collective-permute-start(bf16[4,2,144,512]{3,2,1,0:T(8,128)(2,1)S(1)} %pad_maximum_fusion.refs_5_), channel_id=1, source_target_pairs={{0,132},{1,133},{2,134},{3,135},{4,128},{5,129},{6,130},{7,131},{8... | collective-permute-start | bytes 3538952 | tf_op jit(solution)/shard_map/ppermute | solution.py:32
  26.2 0.0 collective-permute-start.11
  26.2 5.6 %collective-permute-start.3 = (bf16[128,1152]{1,0:T(8,128)(2,1)S(1)}, bf16[128,1152]{1,0:T(8,128)(2,1)S(1)}, u32[]{:S(2)}, u32[]{:S(2)}) collective-permute-start(bf16[128,1152]{1,0:T(8,128)(2,1)S(1)} %shard_map.78.refs_0_), channel_id=1, source_target_pairs={{0,112},{1,113},{2,114},{3,115},{4,116},{5,117},{6,118},{7,119},{8... | collective-permute-start | bytes 884744 | tf_op jit(solution)/shard_map/ppermute | solution.py:32
  31.7 0.0 collective-permute-start
  31.7 5.1 %collective-permute-done.3.refs_2_ = bf16[128,1152]{1,0:T(8,128)(2,1)S(1)} collective-permute-done((bf16[128,1152]{1,0:T(8,128)(2,1)S(1)}, bf16[128,1152]{1,0:T(8,128)(2,1)S(1)}, u32[]{:S(2)}, u32[]{:S(2)}) %collective-permute-start.3) | collective-permute-done | bytes 294944 | tf_op jit(solution)/shard_map/ppermute | solution.py:32
  36.8 3.4 %collective-permute-start.4 = (bf16[128,1152]{1,0:T(8,128)(2,1)S(1)}, bf16[128,1152]{1,0:T(8,128)(2,1)S(1)}, u32[]{:S(2)}, u32[]{:S(2)}) collective-permute-start(bf16[128,1152]{1,0:T(8,128)(2,1)S(1)} %collective-permute-done.3.refs_2_), channel_id=1, source_target_pairs={{0,112},{1,113},{2,114},{3,115},{4,116},{5,117},{6,118},{7,119},{8... | collective-permute-start | bytes 884744 | tf_op jit(solution)/shard_map/ppermute | solution.py:32
  40.2 1.1 %collective-permute-done.12.refs_9_ = bf16[4,2,144,512]{3,2,1,0:T(8,128)(2,1)S(1)} collective-permute-done((bf16[4,2,144,512]{3,2,1,0:T(8,128)(2,1)S(1)}, bf16[4,2,144,512]{3,2,1,0:T(8,128)(2,1)S(1)}, u32[]{:S(2)}, u32[]{:S(2)}) %collective-permute-start.12) | collective-permute-done | bytes 1179680 | tf_op jit(solution)/shard_map/ppermute | solution.py:32
  41.4 1.8 %collective-permute-start.13 = (bf16[2,2,144,512]{3,2,1,0:T(8,128)(2,1)S(1)}, bf16[2,2,144,512]{3,2,1,0:T(8,128)(2,1)S(1)}, u32[]{:S(2)}, u32[]{:S(2)}) collective-permute-start(bf16[2,2,144,512]{3,2,1,0:T(8,128)(2,1)S(1)} %slice.8), channel_id=1, source_target_pairs={{0,4},{1,5},{2,6},{3,7},{4,0},{5,1},{6,2},{7,3},{8,9},{9,8},{10,11... | collective-permute-start | bytes 1769480 | tf_op jit(solution)/shard_map/ppermute | solution.py:32
  43.1 0.0 collective-permute-done.11.refs_6_
  43.2 1.5 %collective-permute-start.14 = (bf16[2,2,144,512]{3,2,1,0:T(8,128)(2,1)S(1)}, bf16[2,2,144,512]{3,2,1,0:T(8,128)(2,1)S(1)}, u32[]{:S(2)}, u32[]{:S(2)}) collective-permute-start(bf16[2,2,144,512]{3,2,1,0:T(8,128)(2,1)S(1)} %slice.9), channel_id=1, source_target_pairs={{0,132},{1,133},{2,134},{3,135},{4,128},{5,129},{6,130},{7,131},{8... | collective-permute-start | bytes 1769480 | tf_op jit(solution)/shard_map/ppermute | solution.py:32
  44.7 0.0 collective-permute-done.refs_1_
  44.7 0.0 collective-permute-start.1
  44.7 0.0 collective-permute-done.4.refs_4_
  44.7 3.9 %collective-permute-start.5 = (bf16[128,1152]{1,0:T(8,128)(2,1)S(1)}, bf16[128,1152]{1,0:T(8,128)(2,1)S(1)}, u32[]{:S(2)}, u32[]{:S(2)}) collective-permute-start(bf16[128,1152]{1,0:T(8,128)(2,1)S(1)} %collective-permute-done.4.refs_4_), channel_id=1, source_target_pairs={{0,112},{1,113},{2,114},{3,115},{4,116},{5,117},{6,118},{7,119},{8... | collective-permute-start | bytes 884744 | tf_op jit(solution)/shard_map/ppermute | solution.py:32
  48.7 5.2 %collective-permute-done.1.refs_3_ = bf16[128,1152]{1,0:T(8,128)(2,1)S(1)} collective-permute-done((bf16[128,1152]{1,0:T(8,128)(2,1)S(1)}, bf16[128,1152]{1,0:T(8,128)(2,1)S(1)}, u32[]{:S(2)}, u32[]{:S(2)}) %collective-permute-start.1) | collective-permute-done | bytes 294944 | tf_op jit(solution)/shard_map/ppermute | solution.py:32
  53.8 0.0 collective-permute-start.2
  53.8 0.0 collective-permute-done.5.refs_1_
  53.8 2.7 %collective-permute-start.6 = (bf16[128,1152]{1,0:T(8,128)(2,1)S(1)}, bf16[128,1152]{1,0:T(8,128)(2,1)S(1)}, u32[]{:S(2)}, u32[]{:S(2)}) collective-permute-start(bf16[128,1152]{1,0:T(8,128)(2,1)S(1)} %collective-permute-done.5.refs_1_), channel_id=1, source_target_pairs={{0,112},{1,113},{2,114},{3,115},{4,116},{5,117},{6,118},{7,119},{8... | collective-permute-start | bytes 884744 | tf_op jit(solution)/shard_map/ppermute | solution.py:32
  56.5 0.0 collective-permute-done.13.refs_7_
  56.5 0.0 collective-permute-done.14.refs_8_
  56.5 7.7 %shard_map.79 = (f32[16,128]{1,0:T(8,128)S(1)}, f32[16,128]{1,0:T(8,128)S(1)}, bf16[4,2,4,144,512]{4,3,2,1,0:T(8,128)(2,1)S(1)}, f32[4,1,512]{2,1,0:T(1,128)S(1)}) custom-call(f32[2]{0:T(128)S(1)} %copy-done, f32[2]{0:T(128)S(1)} %copy-done.1, s32[4]{0:T(128)S(1)} %pad_add_fusion.place, bf16[128,1152]{1,0:T(8,128)(2,1)S(1)} %shard_map.78.refs_0_, ...), custom_call_target="tpu_custom_call" | custom-call | flops 3019898880 | bytes 6193152 | tf_op jit(solution)/shard_map/pallas_call | solution.py:307
  64.3 0.0 collective-permute-done.2.refs_0_
  64.3 0.0 collective-permute-done.6.refs_2_
  64.3 4.2 %shard_map.80 = (f32[16,128]{1,0:T(8,128)S(1)}, f32[16,128]{1,0:T(8,128)S(1)}) custom-call(f32[2]{0:T(128)S(1)} %copy-done, f32[2]{0:T(128)S(1)} %copy-done.1, s32[4]{0:T(128)S(1)} %pad_add_fusion.place, bf16[128,1152]{1,0:T(8,128)(2,1)S(1)} %collective-permute-done.2.refs_0_, bf16[128,1152]{1,0:T(8,128)(2,1)S(1)} %collective-permute-done.5.refs_1_, ...), custom_call_target="tpu_custom_call" | custom-call | flops 1811939328 | bytes 5603328 | tf_op jit(solution)/shard_map/pallas_call | solution.py:307
  68.5 3.3 %collective-permute-start.15 = (f32[16,128]{1,0:T(8,128)S(1)}, f32[16,128]{1,0:T(8,128)S(1)}, u32[]{:S(2)}, u32[]{:S(2)}) collective-permute-start(f32[16,128]{1,0:T(8,128)S(1)} %get-tuple-element.27), channel_id=1, source_target_pairs={{0,8},{1,9},{2,10},{3,11},{4,12},{5,13},{6,14},{7,15},{8,0},{9,1},... | collective-permute-start | bytes 24584 | tf_op jit(solution)/shard_map/ppermute | solution.py:32
  71.8 0.8 collective-permute-done.15.got_ref
  72.6 0.6 shard_map.81
  73.2 14.7 %all_to_all.10.mine_ref = f32[16,2,128]{2,1,0:T(2,128)S(1)} all-to-all(f32[16,2,128]{2,1,0:T(2,128)S(1)} %shard_map.81), channel_id=1, replica_groups={{0,1,2,3,4,5,6,7,128,129,130,131,132,133,134,135},{8,136,24,152,40,168,..., dimensions={0} | all-to-all | bytes 32768 | tf_op jit(solution)/shard_map/all_to_all | solution.py:68
  88.0 1.1 %collective-permute-start.16 = (f32[16,2,128]{2,1,0:T(2,128)S(1)}, f32[16,2,128]{2,1,0:T(2,128)S(1)}, u32[]{:S(2)}, u32[]{:S(2)}) collective-permute-start(f32[16,2,128]{2,1,0:T(2,128)S(1)} %all_to_all.10.mine_ref), channel_id=1, source_target_pairs={{0,8},{1,9},{2,10},{3,11},{4,12},{5,13},{6,14},{7,15},{8,0},{9,1},... | collective-permute-start | bytes 49160 | tf_op jit(solution)/shard_map/ppermute | solution.py:32
  89.0 0.8 collective-permute-done.16.got_ref
  89.9 1.2 %shard_map.82 = (f32[2,64]{1,0:T(2,128)}, f32[2,64]{1,0:T(2,128)}) custom-call(s32[4]{0:T(128)S(1)} %pad_add_fusion.place, f32[16,2,128]{2,1,0:T(2,128)S(1)} %all_to_all.10.mine_ref, f32[16,2,128]{2,1,0:T(2,128)S(1)} %collective-permute-done.16.got_ref), custom_call_target="tpu_custom_call" | custom-call | tf_op jit(solution)/shard_map/pallas_call | solution.py:367
  (4 shorter events, 0.1 us)
Async XLA Ops:
  2.7 7.0 %collective-permute-start.7 = (bf16[144,512]{1,0:T(8,128)(2,1)}, bf16[144,512]{1,0:T(8,128)(2,1)S(1)}, u32[]{:S(2)}, u32[]{:S(2)}) collective-permute-start(bf16[144,512]{1,0:T(8,128)(2,1)} %get-tuple-element.17), channel_id=1, source_target_pairs={{0,8},{1,9},{2,10},{3,11},{4,12},{5,13},{6,14},{7,15},{8,0},{9,1},... | collective-permute-start | bytes 442376 | tf_op jit(solution)/shard_map/ppermute | solution.py:32
  5.9 12.2 %all-to-all-start = ((bf16[16,80,128]{2,1,0:T(8,128)(2,1)}), bf16[16,80,128]{2,1,0:T(8,128)(2,1)S(1)}, u32[]{:S(2)}, u32[]{:S(2)}) async-start(bf16[16,80,128]{2,1,0:T(8,128)(2,1)} %get-tuple-element.15), calls=%async_computation | async-start | bytes 655360 | tf_op jit(solution)/shard_map/all_to_all | solution.py:68
  10.7 8.3 %collective-permute-start.10 = (bf16[2,144,512]{2,1,0:T(8,128)(2,1)S(1)}, bf16[2,144,512]{2,1,0:T(8,128)(2,1)S(1)}, u32[]{:S(2)}, u32[]{:S(2)}) collective-permute-start(bf16[2,144,512]{2,1,0:T(8,128)(2,1)S(1)} %maximum_select_fusion), channel_id=1, source_target_pairs={{0,3},{1,2},{2,1},{3,0},{4,7},{5,6},{6,5},{7,4},{8,140},{9,141},{1... | collective-permute-start | bytes 884744 | tf_op jit(solution)/shard_map/ppermute | solution.py:32
  13.6 6.8 %collective-permute-start.8 = (bf16[2,144,512]{2,1,0:T(8,128)(2,1)S(1)}, bf16[2,144,512]{2,1,0:T(8,128)(2,1)S(1)}, u32[]{:S(2)}, u32[]{:S(2)}) collective-permute-start(bf16[2,144,512]{2,1,0:T(8,128)(2,1)S(1)} %maximum_select_fusion), channel_id=1, source_target_pairs={{0,1},{1,0},{2,3},{3,2},{4,5},{5,4},{6,7},{7,6},{8,12},{9,13},{10,... | collective-permute-start | bytes 884744 | tf_op jit(solution)/shard_map/ppermute | solution.py:32
  13.6 10.9 %collective-permute-start.9 = (bf16[2,144,512]{2,1,0:T(8,128)(2,1)S(1)}, bf16[2,144,512]{2,1,0:T(8,128)(2,1)S(1)}, u32[]{:S(2)}, u32[]{:S(2)}) collective-permute-start(bf16[2,144,512]{2,1,0:T(8,128)(2,1)S(1)} %maximum_select_fusion), channel_id=1, source_target_pairs={{0,2},{1,3},{2,0},{3,1},{4,6},{5,7},{6,4},{7,5},{8,136},{9,137},{1... | collective-permute-start | bytes 884744 | tf_op jit(solution)/shard_map/ppermute | solution.py:32
  24.7 31.9 %copy-start = (f32[2]{0:T(128)S(1)}, f32[2]{0:T(128)}, u32[]{:S(2)}) copy-start(f32[2]{0:T(128)} %sharpness.3) | copy-start | bytes 28
  24.7 31.9 %copy-start.1 = (f32[2]{0:T(128)S(1)}, f32[2]{0:T(128)}, u32[]{:S(2)}) copy-start(f32[2]{0:T(128)} %offsets.3) | copy-start | bytes 28
  24.7 16.6 %collective-permute-start.12 = (bf16[4,2,144,512]{3,2,1,0:T(8,128)(2,1)S(1)}, bf16[4,2,144,512]{3,2,1,0:T(8,128)(2,1)S(1)}, u32[]{:S(2)}, u32[]{:S(2)}) collective-permute-start(bf16[4,2,144,512]{3,2,1,0:T(8,128)(2,1)S(1)} %pad_maximum_fusion.refs_5_), channel_id=1, source_target_pairs={{0,132},{1,133},{2,134},{3,135},{4,128},{5,129},{6,130},{7,131},{8... | collective-permute-start | bytes 3538952 | tf_op jit(solution)/shard_map/ppermute | solution.py:32
  26.2 17.0 %collective-permute-start.11 = (bf16[4,2,144,512]{3,2,1,0:T(8,128)(2,1)S(1)}, bf16[4,2,144,512]{3,2,1,0:T(8,128)(2,1)S(1)}, u32[]{:S(2)}, u32[]{:S(2)}) collective-permute-start(bf16[4,2,144,512]{3,2,1,0:T(8,128)(2,1)S(1)} %pad_maximum_fusion.refs_5_), channel_id=1, source_target_pairs={{0,4},{1,5},{2,6},{3,7},{4,0},{5,1},{6,2},{7,3},{8,9},{9,8},{10,11... | collective-permute-start | bytes 3538952 | tf_op jit(solution)/shard_map/ppermute | solution.py:32
  26.2 10.7 %collective-permute-start.3 = (bf16[128,1152]{1,0:T(8,128)(2,1)S(1)}, bf16[128,1152]{1,0:T(8,128)(2,1)S(1)}, u32[]{:S(2)}, u32[]{:S(2)}) collective-permute-start(bf16[128,1152]{1,0:T(8,128)(2,1)S(1)} %shard_map.78.refs_0_), channel_id=1, source_target_pairs={{0,112},{1,113},{2,114},{3,115},{4,116},{5,117},{6,118},{7,119},{8... | collective-permute-start | bytes 884744 | tf_op jit(solution)/shard_map/ppermute | solution.py:32
  31.7 13.0 %collective-permute-start = (bf16[128,1152]{1,0:T(8,128)(2,1)S(1)}, bf16[128,1152]{1,0:T(8,128)(2,1)S(1)}, u32[]{:S(2)}, u32[]{:S(2)}) collective-permute-start(bf16[128,1152]{1,0:T(8,128)(2,1)S(1)} %shard_map.78.refs_0_), channel_id=1, source_target_pairs={{0,16},{1,17},{2,18},{3,19},{4,20},{5,21},{6,22},{7,23},{8,24},{9,... | collective-permute-start | bytes 884744 | tf_op jit(solution)/shard_map/ppermute | solution.py:32
  36.8 7.9 %collective-permute-start.4 = (bf16[128,1152]{1,0:T(8,128)(2,1)S(1)}, bf16[128,1152]{1,0:T(8,128)(2,1)S(1)}, u32[]{:S(2)}, u32[]{:S(2)}) collective-permute-start(bf16[128,1152]{1,0:T(8,128)(2,1)S(1)} %collective-permute-done.3.refs_2_), channel_id=1, source_target_pairs={{0,112},{1,113},{2,114},{3,115},{4,116},{5,117},{6,118},{7,119},{8... | collective-permute-start | bytes 884744 | tf_op jit(solution)/shard_map/ppermute | solution.py:32
  41.4 15.1 %collective-permute-start.13 = (bf16[2,2,144,512]{3,2,1,0:T(8,128)(2,1)S(1)}, bf16[2,2,144,512]{3,2,1,0:T(8,128)(2,1)S(1)}, u32[]{:S(2)}, u32[]{:S(2)}) collective-permute-start(bf16[2,2,144,512]{3,2,1,0:T(8,128)(2,1)S(1)} %slice.8), channel_id=1, source_target_pairs={{0,4},{1,5},{2,6},{3,7},{4,0},{5,1},{6,2},{7,3},{8,9},{9,8},{10,11... | collective-permute-start | bytes 1769480 | tf_op jit(solution)/shard_map/ppermute | solution.py:32
  43.2 13.3 %collective-permute-start.14 = (bf16[2,2,144,512]{3,2,1,0:T(8,128)(2,1)S(1)}, bf16[2,2,144,512]{3,2,1,0:T(8,128)(2,1)S(1)}, u32[]{:S(2)}, u32[]{:S(2)}) collective-permute-start(bf16[2,2,144,512]{3,2,1,0:T(8,128)(2,1)S(1)} %slice.9), channel_id=1, source_target_pairs={{0,132},{1,133},{2,134},{3,135},{4,128},{5,129},{6,130},{7,131},{8... | collective-permute-start | bytes 1769480 | tf_op jit(solution)/shard_map/ppermute | solution.py:32
  44.7 9.1 %collective-permute-start.1 = (bf16[128,1152]{1,0:T(8,128)(2,1)S(1)}, bf16[128,1152]{1,0:T(8,128)(2,1)S(1)}, u32[]{:S(2)}, u32[]{:S(2)}) collective-permute-start(bf16[128,1152]{1,0:T(8,128)(2,1)S(1)} %collective-permute-done.refs_1_), channel_id=1, source_target_pairs={{0,16},{1,17},{2,18},{3,19},{4,20},{5,21},{6,22},{7,23},{8,24},{9,... | collective-permute-start | bytes 884744 | tf_op jit(solution)/shard_map/ppermute | solution.py:32
  44.7 9.1 %collective-permute-start.5 = (bf16[128,1152]{1,0:T(8,128)(2,1)S(1)}, bf16[128,1152]{1,0:T(8,128)(2,1)S(1)}, u32[]{:S(2)}, u32[]{:S(2)}) collective-permute-start(bf16[128,1152]{1,0:T(8,128)(2,1)S(1)} %collective-permute-done.4.refs_4_), channel_id=1, source_target_pairs={{0,112},{1,113},{2,114},{3,115},{4,116},{5,117},{6,118},{7,119},{8... | collective-permute-start | bytes 884744 | tf_op jit(solution)/shard_map/ppermute | solution.py:32
  53.8 10.4 %collective-permute-start.2 = (bf16[128,1152]{1,0:T(8,128)(2,1)S(1)}, bf16[128,1152]{1,0:T(8,128)(2,1)S(1)}, u32[]{:S(2)}, u32[]{:S(2)}) collective-permute-start(bf16[128,1152]{1,0:T(8,128)(2,1)S(1)} %collective-permute-done.1.refs_3_), channel_id=1, source_target_pairs={{0,16},{1,17},{2,18},{3,19},{4,20},{5,21},{6,22},{7,23},{8,24},{9,... | collective-permute-start | bytes 884744 | tf_op jit(solution)/shard_map/ppermute | solution.py:32
  53.8 10.4 %collective-permute-start.6 = (bf16[128,1152]{1,0:T(8,128)(2,1)S(1)}, bf16[128,1152]{1,0:T(8,128)(2,1)S(1)}, u32[]{:S(2)}, u32[]{:S(2)}) collective-permute-start(bf16[128,1152]{1,0:T(8,128)(2,1)S(1)} %collective-permute-done.5.refs_1_), channel_id=1, source_target_pairs={{0,112},{1,113},{2,114},{3,115},{4,116},{5,117},{6,118},{7,119},{8... | collective-permute-start | bytes 884744 | tf_op jit(solution)/shard_map/ppermute | solution.py:32
  68.5 4.1 %collective-permute-start.15 = (f32[16,128]{1,0:T(8,128)S(1)}, f32[16,128]{1,0:T(8,128)S(1)}, u32[]{:S(2)}, u32[]{:S(2)}) collective-permute-start(f32[16,128]{1,0:T(8,128)S(1)} %get-tuple-element.27), channel_id=1, source_target_pairs={{0,8},{1,9},{2,10},{3,11},{4,12},{5,13},{6,14},{7,15},{8,0},{9,1},... | collective-permute-start | bytes 24584 | tf_op jit(solution)/shard_map/ppermute | solution.py:32
  88.0 1.9 %collective-permute-start.16 = (f32[16,2,128]{2,1,0:T(2,128)S(1)}, f32[16,2,128]{2,1,0:T(2,128)S(1)}, u32[]{:S(2)}, u32[]{:S(2)}) collective-permute-start(f32[16,2,128]{2,1,0:T(2,128)S(1)} %all_to_all.10.mine_ref), channel_id=1, source_target_pairs={{0,8},{1,9},{2,10},{3,11},{4,12},{5,13},{6,14},{7,15},{8,0},{9,1},... | collective-permute-start | bytes 49160 | tf_op jit(solution)/shard_map/ppermute | solution.py:32

commit v3 on v2

--- a/solution.py
+++ b/solution.py
@@ -81,13 +81,10 @@
 FOLD = 80
 
 
-def start_kernel(p0, p1, c0, c1, own_ref, give_ref, out_ref):
-    core = lax.axis_index("wide") % CORES
-    give_ref[...] = jnp.where(core == 0, p1[...], p0[...])
-    own_ref[...] = jnp.where(core == 0, p0[...], p1[...])
-    features, block = c0.shape
+def shares_kernel(learner_ref, refer_ref, out_ref):
+    features, block = learner_ref.shape
     share = block // NARROW
-    for model, ref in enumerate((c0, c1)):
+    for model, ref in enumerate((learner_ref, refer_ref)):
         for n in range(NARROW):
             piece = ref[:, n * share : (n + 1) * share]
             rest = jnp.concatenate(
@@ -96,20 +93,17 @@
             out_ref[model * NARROW + n] = jnp.concatenate([piece[:FOLD], rest], axis=1)
 
 
-def start(pictures, captions):
-    features, block = captions[0].shape
-    dtype = captions[0].dtype
+def text_shares(learner, refer):
+    _, block = learner.shape
     return pl.pallas_call(
-        start_kernel,
-        in_specs=[VMEM] * 4,
-        out_specs=[VMEM] * 3,
-        out_shape=[
-            jax.ShapeDtypeStruct((features, block), dtype),
-            jax.ShapeDtypeStruct((features, block), dtype),
-            jax.ShapeDtypeStruct((CORES * NARROW, FOLD, 2 * block // NARROW), dtype),
-        ],
+        shares_kernel,
+        in_specs=[VMEM, VMEM],
+        out_specs=VMEM,
+        out_shape=jax.ShapeDtypeStruct(
+            (CORES * NARROW, FOLD, 2 * block // NARROW), learner.dtype
+        ),
         compiler_params=pltpu.CompilerParams(vmem_limit_bytes=LARGE),
-    )(*pictures, *captions)
+    )(learner, refer)
 
 
 def rows_kernel(place, in_ref, out_ref):
@@ -288,7 +282,7 @@
     features, columns = operands[0].shape[-2:]
     sums = jax.ShapeDtypeStruct((16, 128), jnp.float32)
     outs = [sums, sums]
-    span = rows // (4 if first else 3)
+    span = rows // (2 if first else 3)
     buffers = [
         pltpu.VMEM((rows, depth), jnp.bfloat16),
         pltpu.VMEM((span, columns), jnp.float32),
@@ -400,21 +394,19 @@
     place = jnp.stack([narrow, wide // (Z * CORES), core, wide // CORES % Z]).astype(jnp.int32)
     learner = core == 0
 
-    own_pictures, pictures, shares = start(
-        (student_picture_vectors, teacher_picture_vectors),
-        (student_caption_vectors, teacher_caption_vectors),
-    )
+    pictures = jnp.where(learner, teacher_picture_vectors, student_picture_vectors)
+    other_pictures = send_core(pictures)
+    shares = text_shares(student_caption_vectors, teacher_caption_vectors)
+    both = jnp.where(
+        learner,
+        jnp.stack([student_picture_vectors, other_pictures]),
+        jnp.stack([other_pictures, teacher_picture_vectors]),
+    )
+    both, shares = lax.optimization_barrier((both, shares))
+    ring = [both] + [send_first(both, d) for d in (1, 2, 3)]
 
     by_row = groups_by(lambda hi, z, c, lo, x: (hi, z), lambda hi, z, c, lo, x: (c, lo, x))
     text = text_rows(place, exchange(shares, by_row), features)
-
-    other_pictures = send_core(pictures)
-    both = jnp.where(
-        learner,
-        jnp.stack([own_pictures, other_pictures]),
-        jnp.stack([other_pictures, own_pictures]),
-    )
-    ring = [both] + [send_first(both, d) for d in (1, 2, 3)]
     _, *ring = lax.optimization_barrier((text, *ring))
     line = jnp.stack(ring)
     one, three = send_second(line, 1), send_second(line, 3)

time: 91.3 us -> 90.9 us (level)
    ppermute x17, waiting for transfers between devices: 18.5 us -> 17.2 us  [send(): return lax.ppermute(value, AXES, pairs)]
    all_to_all x1, waiting for transfers between devices: 3.17 us -> 4.3 us  [exchange(): lax.all_to_all(value, AXES, 0, 0, axis_index_groups=groups, tiled=True)]
  transfers between devices with their start and end apart: 18 -> 18, of which waited for: 8 -> 8; matrix products, arithmetic and copies ran while one was open for 1% -> 0% of each run, Pallas kernels for 9% -> 11%
where the time goes in v3:
time: 90.9 us; the launch traced here: 90.7 us
  starting transfers between devices  36.5 us (40%)
  waiting for transfers between devices  21.5 us (24%)
  Pallas kernels  16.1 us (18%)
  blocking collectives  14.5 us (16%)
  other arithmetic  1.27 us (1%)
    ppermute x17, starting transfers between devices, send(): return lax.ppermute(value, AXES, pairs)  32.8 us
    ppermute x17, waiting for transfers between devices, send(): return lax.ppermute(value, AXES, pairs)  17.2 us
    all_to_all x1, blocking collectives, exchange(): lax.all_to_all(value, AXES, 0, 0, axis_index_groups=groups, tiled=True)  14.5 us
    pallas_call x2, Pallas kernels, pair_sums(): pl.pallas_call(functools.partial(pair_kernel, texts=len(texts), first=fir...  11.6 us
    all_to_all x1, waiting for transfers between devices, exchange(): lax.all_to_all(value, AXES, 0, 0, axis_index_groups=groups, tiled=True)  4.3 us
    all_to_all x1, starting transfers between devices, exchange(): lax.all_to_all(value, AXES, 0, 0, axis_index_groups=groups, tiled=True)  3.72 us
    pallas_call x1, Pallas kernels, text_shares(): pl.pallas_call(shares_kernel, in_specs=[VMEM, VMEM], out_specs=VMEM, out_...  1.86 us
  transfers between devices with their start and end apart: 18, of which 8 were waited for; matrix products, arithmetic and copies ran while one was open for 0% of the time, Pallas kernels for 11%

profile of v3, /device:TPU:1, one launch (start us, length us, event | category | flops | bytes accessed | tf_op | source)
XLA Modules:
  0.0 90.7 jit_solution(15978740268140622944)
XLA Ops:
  0.7 1.0 %broadcast_select_fusion = bf16[144,512]{1,0:T(8,128)(2,1)S(1)} fusion(bf16[144,512]{1,0:T(8,128)(2,1)} %param.8, bf16[144,512]{1,0:T(8,128)(2,1)} %param.6, pred[]{:T(512)S(6)} %eq.6), kind=kLoop, calls=%fused_computation.2 | loop fusion | flops 73728 | bytes 442369 | tf_op jit(solution)/shard_map/jit(_where)/select_n | solution.py:397
  1.7 3.3 %collective-permute-start = (bf16[144,512]{1,0:T(8,128)(2,1)S(1)}, bf16[144,512]{1,0:T(8,128)(2,1)S(1)}, u32[]{:S(2)}, u32[]{:S(2)}) collective-permute-start(bf16[144,512]{1,0:T(8,128)(2,1)S(1)} %broadcast_select_fusion), channel_id=1, source_target_pairs={{0,8},{1,9},{2,10},{3,11},{4,12},{5,13},{6,14},{7,15},{8,0},{9,1},... | collective-permute-start | bytes 442376 | tf_op jit(solution)/shard_map/ppermute | solution.py:32
  5.0 1.9 %shard_map.77 = bf16[16,80,128]{2,1,0:T(8,128)(2,1)} custom-call(bf16[144,512]{1,0:T(8,128)(2,1)} %learner_ref.1, bf16[144,512]{1,0:T(8,128)(2,1)} %refer_ref.1), custom_call_target="tpu_custom_call" | custom-call | tf_op jit(solution)/shard_map/pallas_call | solution.py:98
  6.9 0.0 collective-permute-done
  6.9 3.7 %all-to-all-start = ((bf16[16,80,128]{2,1,0:T(8,128)(2,1)}), bf16[16,80,128]{2,1,0:T(8,128)(2,1)S(1)}, u32[]{:S(2)}, u32[]{:S(2)}) async-start(bf16[16,80,128]{2,1,0:T(8,128)(2,1)} %shard_map.77), calls=%async_computation | async-start | bytes 655360 | tf_op jit(solution)/shard_map/all_to_all | solution.py:68
  10.6 2.8 %collective-permute-start.10 = (bf16[2,144,512]{2,1,0:T(8,128)(2,1)S(1)}, bf16[2,144,512]{2,1,0:T(8,128)(2,1)S(1)}, u32[]{:S(2)}, u32[]{:S(2)}) collective-permute-start(bf16[2,144,512]{2,1,0:T(8,128)(2,1)S(1)} %maximum_select_fusion), channel_id=1, source_target_pairs={{0,3},{1,2},{2,1},{3,0},{4,7},{5,6},{6,5},{7,4},{8,140},{9,141},{1... | collective-permute-start | bytes 884744 | tf_op jit(solution)/shard_map/ppermute | solution.py:32
  13.5 0.0 collective-permute-start.8
  13.5 1.3 %collective-permute-start.9 = (bf16[2,144,512]{2,1,0:T(8,128)(2,1)S(1)}, bf16[2,144,512]{2,1,0:T(8,128)(2,1)S(1)}, u32[]{:S(2)}, u32[]{:S(2)}) collective-permute-start(bf16[2,144,512]{2,1,0:T(8,128)(2,1)S(1)} %maximum_select_fusion), channel_id=1, source_target_pairs={{0,2},{1,3},{2,0},{3,1},{4,6},{5,7},{6,4},{7,5},{8,136},{9,137},{1... | collective-permute-start | bytes 884744 | tf_op jit(solution)/shard_map/ppermute | solution.py:32
  14.7 0.1 pad_add_fusion.place
  14.8 4.3 %all-to-all-done.in_ref = bf16[16,80,128]{2,1,0:T(8,128)(2,1)S(1)} async-done(((bf16[16,80,128]{2,1,0:T(8,128)(2,1)}), bf16[16,80,128]{2,1,0:T(8,128)(2,1)S(1)}, u32[]{:S(2)}, u32[]{:S(2)}) %all-to-all-start) | async-done | bytes 327712 | tf_op jit(solution)/shard_map/all_to_all | solution.py:68
  19.1 0.8 shard_map.78.refs_0_
  20.0 0.0 collective-permute-done.10
  20.0 1.4 %collective-permute-done.8 = bf16[2,144,512]{2,1,0:T(8,128)(2,1)S(1)} collective-permute-done((bf16[2,144,512]{2,1,0:T(8,128)(2,1)S(1)}, bf16[2,144,512]{2,1,0:T(8,128)(2,1)S(1)}, u32[]{:S(2)}, u32[]{:S(2)}) %collective-permute-start.8) | collective-permute-done | bytes 294944 | tf_op jit(solution)/shard_map/ppermute | solution.py:32
  21.3 3.5 %collective-permute-done.9 = bf16[2,144,512]{2,1,0:T(8,128)(2,1)S(1)} collective-permute-done((bf16[2,144,512]{2,1,0:T(8,128)(2,1)S(1)}, bf16[2,144,512]{2,1,0:T(8,128)(2,1)S(1)}, u32[]{:S(2)}, u32[]{:S(2)}) %collective-permute-start.9) | collective-permute-done | bytes 294944 | tf_op jit(solution)/shard_map/ppermute | solution.py:32
  24.8 0.1 pad_maximum_fusion.refs_5_
  24.9 0.0 copy-start
  25.0 0.0 copy-start.1
  25.0 2.1 %collective-permute-start.12 = (bf16[4,2,144,512]{3,2,1,0:T(8,128)(2,1)S(1)}, bf16[4,2,144,512]{3,2,1,0:T(8,128)(2,1)S(1)}, u32[]{:S(2)}, u32[]{:S(2)}) collective-permute-start(bf16[4,2,144,512]{3,2,1,0:T(8,128)(2,1)S(1)} %pad_maximum_fusion.refs_5_), channel_id=1, source_target_pairs={{0,132},{1,133},{2,134},{3,135},{4,128},{5,129},{6,130},{7,131},{8... | collective-permute-start | bytes 3538952 | tf_op jit(solution)/shard_map/ppermute | solution.py:32
  27.1 0.0 collective-permute-start.11
  27.1 5.6 %collective-permute-start.4 = (bf16[128,1152]{1,0:T(8,128)(2,1)S(1)}, bf16[128,1152]{1,0:T(8,128)(2,1)S(1)}, u32[]{:S(2)}, u32[]{:S(2)}) collective-permute-start(bf16[128,1152]{1,0:T(8,128)(2,1)S(1)} %shard_map.78.refs_0_), channel_id=1, source_target_pairs={{0,112},{1,113},{2,114},{3,115},{4,116},{5,117},{6,118},{7,119},{8... | collective-permute-start | bytes 884744 | tf_op jit(solution)/shard_map/ppermute | solution.py:32
  32.7 0.0 collective-permute-start.1
  32.7 5.0 %collective-permute-done.4.refs_2_ = bf16[128,1152]{1,0:T(8,128)(2,1)S(1)} collective-permute-done((bf16[128,1152]{1,0:T(8,128)(2,1)S(1)}, bf16[128,1152]{1,0:T(8,128)(2,1)S(1)}, u32[]{:S(2)}, u32[]{:S(2)}) %collective-permute-start.4) | collective-permute-done | bytes 294944 | tf_op jit(solution)/shard_map/ppermute | solution.py:32
  37.7 3.4 %collective-permute-start.5 = (bf16[128,1152]{1,0:T(8,128)(2,1)S(1)}, bf16[128,1152]{1,0:T(8,128)(2,1)S(1)}, u32[]{:S(2)}, u32[]{:S(2)}) collective-permute-start(bf16[128,1152]{1,0:T(8,128)(2,1)S(1)} %collective-permute-done.4.refs_2_), channel_id=1, source_target_pairs={{0,112},{1,113},{2,114},{3,115},{4,116},{5,117},{6,118},{7,119},{8... | collective-permute-start | bytes 884744 | tf_op jit(solution)/shard_map/ppermute | solution.py:32
  41.1 0.5 collective-permute-done.12.refs_9_
  41.7 2.4 %collective-permute-start.13 = (bf16[2,2,144,512]{3,2,1,0:T(8,128)(2,1)S(1)}, bf16[2,2,144,512]{3,2,1,0:T(8,128)(2,1)S(1)}, u32[]{:S(2)}, u32[]{:S(2)}) collective-permute-start(bf16[2,2,144,512]{3,2,1,0:T(8,128)(2,1)S(1)} %slice.8), channel_id=1, source_target_pairs={{0,4},{1,5},{2,6},{3,7},{4,0},{5,1},{6,2},{7,3},{8,9},{9,8},{10,11... | collective-permute-start | bytes 1769480 | tf_op jit(solution)/shard_map/ppermute | solution.py:32
  44.1 0.0 collective-permute-done.11.refs_6_
  44.1 1.0 %collective-permute-start.14 = (bf16[2,2,144,512]{3,2,1,0:T(8,128)(2,1)S(1)}, bf16[2,2,144,512]{3,2,1,0:T(8,128)(2,1)S(1)}, u32[]{:S(2)}, u32[]{:S(2)}) collective-permute-start(bf16[2,2,144,512]{3,2,1,0:T(8,128)(2,1)S(1)} %slice.9), channel_id=1, source_target_pairs={{0,132},{1,133},{2,134},{3,135},{4,128},{5,129},{6,130},{7,131},{8... | collective-permute-start | bytes 1769480 | tf_op jit(solution)/shard_map/ppermute | solution.py:32
  45.1 0.0 collective-permute-done.1.refs_1_
  45.1 0.3 collective-permute-start.2
  45.4 0.0 collective-permute-done.5.refs_4_
  45.4 4.2 %collective-permute-start.6 = (bf16[128,1152]{1,0:T(8,128)(2,1)S(1)}, bf16[128,1152]{1,0:T(8,128)(2,1)S(1)}, u32[]{:S(2)}, u32[]{:S(2)}) collective-permute-start(bf16[128,1152]{1,0:T(8,128)(2,1)S(1)} %collective-permute-done.5.refs_4_), channel_id=1, source_target_pairs={{0,112},{1,113},{2,114},{3,115},{4,116},{5,117},{6,118},{7,119},{8... | collective-permute-start | bytes 884744 | tf_op jit(solution)/shard_map/ppermute | solution.py:32
  49.6 5.1 %collective-permute-done.2.refs_3_ = bf16[128,1152]{1,0:T(8,128)(2,1)S(1)} collective-permute-done((bf16[128,1152]{1,0:T(8,128)(2,1)S(1)}, bf16[128,1152]{1,0:T(8,128)(2,1)S(1)}, u32[]{:S(2)}, u32[]{:S(2)}) %collective-permute-start.2) | collective-permute-done | bytes 294944 | tf_op jit(solution)/shard_map/ppermute | solution.py:32
  54.7 0.0 collective-permute-start.3
  54.7 0.0 collective-permute-done.6.refs_1_
  54.7 2.7 %collective-permute-start.7 = (bf16[128,1152]{1,0:T(8,128)(2,1)S(1)}, bf16[128,1152]{1,0:T(8,128)(2,1)S(1)}, u32[]{:S(2)}, u32[]{:S(2)}) collective-permute-start(bf16[128,1152]{1,0:T(8,128)(2,1)S(1)} %collective-permute-done.6.refs_1_), channel_id=1, source_target_pairs={{0,112},{1,113},{2,114},{3,115},{4,116},{5,117},{6,118},{7,119},{8... | collective-permute-start | bytes 884744 | tf_op jit(solution)/shard_map/ppermute | solution.py:32
  57.4 0.0 collective-permute-done.13.refs_7_
  57.4 0.0 collective-permute-done.14.refs_8_
  57.4 7.4 %shard_map.79 = (f32[16,128]{1,0:T(8,128)S(1)}, f32[16,128]{1,0:T(8,128)S(1)}, bf16[4,2,4,144,512]{4,3,2,1,0:T(8,128)(2,1)S(1)}, f32[4,1,512]{2,1,0:T(1,128)S(1)}) custom-call(f32[2]{0:T(128)S(1)} %copy-done, f32[2]{0:T(128)S(1)} %copy-done.1, s32[4]{0:T(128)S(1)} %pad_add_fusion.place, bf16[128,1152]{1,0:T(8,128)(2,1)S(1)} %shard_map.78.refs_0_, ...), custom_call_target="tpu_custom_call" | custom-call | flops 3019898880 | bytes 6193152 | tf_op jit(solution)/shard_map/pallas_call | solution.py:301
  64.8 0.0 collective-permute-done.3.refs_0_
  64.8 0.0 collective-permute-done.7.refs_2_
  64.8 4.2 %shard_map.80 = (f32[16,128]{1,0:T(8,128)S(1)}, f32[16,128]{1,0:T(8,128)S(1)}) custom-call(f32[2]{0:T(128)S(1)} %copy-done, f32[2]{0:T(128)S(1)} %copy-done.1, s32[4]{0:T(128)S(1)} %pad_add_fusion.place, bf16[128,1152]{1,0:T(8,128)(2,1)S(1)} %collective-permute-done.3.refs_0_, bf16[128,1152]{1,0:T(8,128)(2,1)S(1)} %collective-permute-done.6.refs_1_, ...), custom_call_target="tpu_custom_call" | custom-call | flops 1811939328 | bytes 5603328 | tf_op jit(solution)/shard_map/pallas_call | solution.py:301
  69.0 3.3 %collective-permute-start.15 = (f32[16,128]{1,0:T(8,128)S(1)}, f32[16,128]{1,0:T(8,128)S(1)}, u32[]{:S(2)}, u32[]{:S(2)}) collective-permute-start(f32[16,128]{1,0:T(8,128)S(1)} %get-tuple-element.25), channel_id=1, source_target_pairs={{0,8},{1,9},{2,10},{3,11},{4,12},{5,13},{6,14},{7,15},{8,0},{9,1},... | collective-permute-start | bytes 24584 | tf_op jit(solution)/shard_map/ppermute | solution.py:32
  72.4 0.8 collective-permute-done.15.got_ref
  73.2 0.6 shard_map.81
  73.8 14.5 %all_to_all.10.mine_ref = f32[16,2,128]{2,1,0:T(2,128)S(1)} all-to-all(f32[16,2,128]{2,1,0:T(2,128)S(1)} %shard_map.81), channel_id=1, replica_groups={{0,1,2,3,4,5,6,7,128,129,130,131,132,133,134,135},{8,136,24,152,40,168,..., dimensions={0} | all-to-all | bytes 32768 | tf_op jit(solution)/shard_map/all_to_all | solution.py:68
  88.3 0.3 collective-permute-start.16
  88.7 0.8 collective-permute-done.16.got_ref
  89.5 1.2 %shard_map.82 = (f32[2,64]{1,0:T(2,128)}, f32[2,64]{1,0:T(2,128)}) custom-call(s32[4]{0:T(128)S(1)} %pad_add_fusion.place, f32[16,2,128]{2,1,0:T(2,128)S(1)} %all_to_all.10.mine_ref, f32[16,2,128]{2,1,0:T(2,128)S(1)} %collective-permute-done.16.got_ref), custom_call_target="tpu_custom_call" | custom-call | tf_op jit(solution)/shard_map/pallas_call | solution.py:361
  (9 shorter events, 0.1 us)
Async XLA Ops:
  0.6 6.2 %copy-start.3 = (bf16[144,512]{1,0:T(8,128)(2,1)S(1)}, bf16[144,512]{1,0:T(8,128)(2,1)}, u32[]{:S(2)}) copy-start(bf16[144,512]{1,0:T(8,128)(2,1)} %param.6) | copy-start | bytes 442372
  0.6 6.2 %copy-start.2 = (bf16[144,512]{1,0:T(8,128)(2,1)S(1)}, bf16[144,512]{1,0:T(8,128)(2,1)}, u32[]{:S(2)}) copy-start(bf16[144,512]{1,0:T(8,128)(2,1)} %param.8) | copy-start | bytes 442372
  1.7 5.2 %collective-permute-start = (bf16[144,512]{1,0:T(8,128)(2,1)S(1)}, bf16[144,512]{1,0:T(8,128)(2,1)S(1)}, u32[]{:S(2)}, u32[]{:S(2)}) collective-permute-start(bf16[144,512]{1,0:T(8,128)(2,1)S(1)} %broadcast_select_fusion), channel_id=1, source_target_pairs={{0,8},{1,9},{2,10},{3,11},{4,12},{5,13},{6,14},{7,15},{8,0},{9,1},... | collective-permute-start | bytes 442376 | tf_op jit(solution)/shard_map/ppermute | solution.py:32
  6.9 12.2 %all-to-all-start = ((bf16[16,80,128]{2,1,0:T(8,128)(2,1)}), bf16[16,80,128]{2,1,0:T(8,128)(2,1)S(1)}, u32[]{:S(2)}, u32[]{:S(2)}) async-start(bf16[16,80,128]{2,1,0:T(8,128)(2,1)} %shard_map.77), calls=%async_computation | async-start | bytes 655360 | tf_op jit(solution)/shard_map/all_to_all | solution.py:68
  10.6 9.3 %collective-permute-start.10 = (bf16[2,144,512]{2,1,0:T(8,128)(2,1)S(1)}, bf16[2,144,512]{2,1,0:T(8,128)(2,1)S(1)}, u32[]{:S(2)}, u32[]{:S(2)}) collective-permute-start(bf16[2,144,512]{2,1,0:T(8,128)(2,1)S(1)} %maximum_select_fusion), channel_id=1, source_target_pairs={{0,3},{1,2},{2,1},{3,0},{4,7},{5,6},{6,5},{7,4},{8,140},{9,141},{1... | collective-permute-start | bytes 884744 | tf_op jit(solution)/shard_map/ppermute | solution.py:32
  13.5 7.9 %collective-permute-start.8 = (bf16[2,144,512]{2,1,0:T(8,128)(2,1)S(1)}, bf16[2,144,512]{2,1,0:T(8,128)(2,1)S(1)}, u32[]{:S(2)}, u32[]{:S(2)}) collective-permute-start(bf16[2,144,512]{2,1,0:T(8,128)(2,1)S(1)} %maximum_select_fusion), channel_id=1, source_target_pairs={{0,1},{1,0},{2,3},{3,2},{4,5},{5,4},{6,7},{7,6},{8,12},{9,13},{10,... | collective-permute-start | bytes 884744 | tf_op jit(solution)/shard_map/ppermute | solution.py:32
  13.5 11.3 %collective-permute-start.9 = (bf16[2,144,512]{2,1,0:T(8,128)(2,1)S(1)}, bf16[2,144,512]{2,1,0:T(8,128)(2,1)S(1)}, u32[]{:S(2)}, u32[]{:S(2)}) collective-permute-start(bf16[2,144,512]{2,1,0:T(8,128)(2,1)S(1)} %maximum_select_fusion), channel_id=1, source_target_pairs={{0,2},{1,3},{2,0},{3,1},{4,6},{5,7},{6,4},{7,5},{8,136},{9,137},{1... | collective-permute-start | bytes 884744 | tf_op jit(solution)/shard_map/ppermute | solution.py:32
  24.9 32.5 %copy-start = (f32[2]{0:T(128)S(1)}, f32[2]{0:T(128)}, u32[]{:S(2)}) copy-start(f32[2]{0:T(128)} %sharpness.3) | copy-start | bytes 28
  25.0 32.4 %copy-start.1 = (f32[2]{0:T(128)S(1)}, f32[2]{0:T(128)}, u32[]{:S(2)}) copy-start(f32[2]{0:T(128)} %offsets.3) | copy-start | bytes 28
  25.0 16.6 %collective-permute-start.12 = (bf16[4,2,144,512]{3,2,1,0:T(8,128)(2,1)S(1)}, bf16[4,2,144,512]{3,2,1,0:T(8,128)(2,1)S(1)}, u32[]{:S(2)}, u32[]{:S(2)}) collective-permute-start(bf16[4,2,144,512]{3,2,1,0:T(8,128)(2,1)S(1)} %pad_maximum_fusion.refs_5_), channel_id=1, source_target_pairs={{0,132},{1,133},{2,134},{3,135},{4,128},{5,129},{6,130},{7,131},{8... | collective-permute-start | bytes 3538952 | tf_op jit(solution)/shard_map/ppermute | solution.py:32
  27.1 17.0 %collective-permute-start.11 = (bf16[4,2,144,512]{3,2,1,0:T(8,128)(2,1)S(1)}, bf16[4,2,144,512]{3,2,1,0:T(8,128)(2,1)S(1)}, u32[]{:S(2)}, u32[]{:S(2)}) collective-permute-start(bf16[4,2,144,512]{3,2,1,0:T(8,128)(2,1)S(1)} %pad_maximum_fusion.refs_5_), channel_id=1, source_target_pairs={{0,4},{1,5},{2,6},{3,7},{4,0},{5,1},{6,2},{7,3},{8,9},{9,8},{10,11... | collective-permute-start | bytes 3538952 | tf_op jit(solution)/shard_map/ppermute | solution.py:32
  27.1 10.6 %collective-permute-start.4 = (bf16[128,1152]{1,0:T(8,128)(2,1)S(1)}, bf16[128,1152]{1,0:T(8,128)(2,1)S(1)}, u32[]{:S(2)}, u32[]{:S(2)}) collective-permute-start(bf16[128,1152]{1,0:T(8,128)(2,1)S(1)} %shard_map.78.refs_0_), channel_id=1, source_target_pairs={{0,112},{1,113},{2,114},{3,115},{4,116},{5,117},{6,118},{7,119},{8... | collective-permute-start | bytes 884744 | tf_op jit(solution)/shard_map/ppermute | solution.py:32
  32.7 12.4 %collective-permute-start.1 = (bf16[128,1152]{1,0:T(8,128)(2,1)S(1)}, bf16[128,1152]{1,0:T(8,128)(2,1)S(1)}, u32[]{:S(2)}, u32[]{:S(2)}) collective-permute-start(bf16[128,1152]{1,0:T(8,128)(2,1)S(1)} %shard_map.78.refs_0_), channel_id=1, source_target_pairs={{0,16},{1,17},{2,18},{3,19},{4,20},{5,21},{6,22},{7,23},{8,24},{9,... | collective-permute-start | bytes 884744 | tf_op jit(solution)/shard_map/ppermute | solution.py:32
  37.7 7.7 %collective-permute-start.5 = (bf16[128,1152]{1,0:T(8,128)(2,1)S(1)}, bf16[128,1152]{1,0:T(8,128)(2,1)S(1)}, u32[]{:S(2)}, u32[]{:S(2)}) collective-permute-start(bf16[128,1152]{1,0:T(8,128)(2,1)S(1)} %collective-permute-done.4.refs_2_), channel_id=1, source_target_pairs={{0,112},{1,113},{2,114},{3,115},{4,116},{5,117},{6,118},{7,119},{8... | collective-permute-start | bytes 884744 | tf_op jit(solution)/shard_map/ppermute | solution.py:32
  41.7 15.7 %collective-permute-start.13 = (bf16[2,2,144,512]{3,2,1,0:T(8,128)(2,1)S(1)}, bf16[2,2,144,512]{3,2,1,0:T(8,128)(2,1)S(1)}, u32[]{:S(2)}, u32[]{:S(2)}) collective-permute-start(bf16[2,2,144,512]{3,2,1,0:T(8,128)(2,1)S(1)} %slice.8), channel_id=1, source_target_pairs={{0,4},{1,5},{2,6},{3,7},{4,0},{5,1},{6,2},{7,3},{8,9},{9,8},{10,11... | collective-permute-start | bytes 1769480 | tf_op jit(solution)/shard_map/ppermute | solution.py:32
  44.1 13.3 %collective-permute-start.14 = (bf16[2,2,144,512]{3,2,1,0:T(8,128)(2,1)S(1)}, bf16[2,2,144,512]{3,2,1,0:T(8,128)(2,1)S(1)}, u32[]{:S(2)}, u32[]{:S(2)}) collective-permute-start(bf16[2,2,144,512]{3,2,1,0:T(8,128)(2,1)S(1)} %slice.9), channel_id=1, source_target_pairs={{0,132},{1,133},{2,134},{3,135},{4,128},{5,129},{6,130},{7,131},{8... | collective-permute-start | bytes 1769480 | tf_op jit(solution)/shard_map/ppermute | solution.py:32
  45.1 9.6 %collective-permute-start.2 = (bf16[128,1152]{1,0:T(8,128)(2,1)S(1)}, bf16[128,1152]{1,0:T(8,128)(2,1)S(1)}, u32[]{:S(2)}, u32[]{:S(2)}) collective-permute-start(bf16[128,1152]{1,0:T(8,128)(2,1)S(1)} %collective-permute-done.1.refs_1_), channel_id=1, source_target_pairs={{0,16},{1,17},{2,18},{3,19},{4,20},{5,21},{6,22},{7,23},{8,24},{9,... | collective-permute-start | bytes 884744 | tf_op jit(solution)/shard_map/ppermute | solution.py:32
  45.4 9.4 %collective-permute-start.6 = (bf16[128,1152]{1,0:T(8,128)(2,1)S(1)}, bf16[128,1152]{1,0:T(8,128)(2,1)S(1)}, u32[]{:S(2)}, u32[]{:S(2)}) collective-permute-start(bf16[128,1152]{1,0:T(8,128)(2,1)S(1)} %collective-permute-done.5.refs_4_), channel_id=1, source_target_pairs={{0,112},{1,113},{2,114},{3,115},{4,116},{5,117},{6,118},{7,119},{8... | collective-permute-start | bytes 884744 | tf_op jit(solution)/shard_map/ppermute | solution.py:32
  54.7 10.1 %collective-permute-start.3 = (bf16[128,1152]{1,0:T(8,128)(2,1)S(1)}, bf16[128,1152]{1,0:T(8,128)(2,1)S(1)}, u32[]{:S(2)}, u32[]{:S(2)}) collective-permute-start(bf16[128,1152]{1,0:T(8,128)(2,1)S(1)} %collective-permute-done.2.refs_3_), channel_id=1, source_target_pairs={{0,16},{1,17},{2,18},{3,19},{4,20},{5,21},{6,22},{7,23},{8,24},{9,... | collective-permute-start | bytes 884744 | tf_op jit(solution)/shard_map/ppermute | solution.py:32
  54.7 10.1 %collective-permute-start.7 = (bf16[128,1152]{1,0:T(8,128)(2,1)S(1)}, bf16[128,1152]{1,0:T(8,128)(2,1)S(1)}, u32[]{:S(2)}, u32[]{:S(2)}) collective-permute-start(bf16[128,1152]{1,0:T(8,128)(2,1)S(1)} %collective-permute-done.6.refs_1_), channel_id=1, source_target_pairs={{0,112},{1,113},{2,114},{3,115},{4,116},{5,117},{6,118},{7,119},{8... | collective-permute-start | bytes 884744 | tf_op jit(solution)/shard_map/ppermute | solution.py:32
  69.0 4.2 %collective-permute-start.15 = (f32[16,128]{1,0:T(8,128)S(1)}, f32[16,128]{1,0:T(8,128)S(1)}, u32[]{:S(2)}, u32[]{:S(2)}) collective-permute-start(f32[16,128]{1,0:T(8,128)S(1)} %get-tuple-element.25), channel_id=1, source_target_pairs={{0,8},{1,9},{2,10},{3,11},{4,12},{5,13},{6,14},{7,15},{8,0},{9,1},... | collective-permute-start | bytes 24584 | tf_op jit(solution)/shard_map/ppermute | solution.py:32
  88.3 1.2 %collective-permute-start.16 = (f32[16,2,128]{2,1,0:T(2,128)S(1)}, f32[16,2,128]{2,1,0:T(2,128)S(1)}, u32[]{:S(2)}, u32[]{:S(2)}) collective-permute-start(f32[16,2,128]{2,1,0:T(2,128)S(1)} %all_to_all.10.mine_ref), channel_id=1, source_target_pairs={{0,8},{1,9},{2,10},{3,11},{4,12},{5,13},{6,14},{7,15},{8,0},{9,1},... | collective-permute-start | bytes 49160 | tf_op jit(solution)/shard_map/ppermute | solution.py:32

commit v4 on v3

--- a/solution.py
+++ b/solution.py
@@ -126,6 +126,7 @@
         out_specs=VMEM,
         out_shape=jax.ShapeDtypeStruct((shares.shape[2], NARROW * features), shares.dtype),
         compiler_params=SMALL,
+        cost_estimate=pl.CostEstimate(flops=0, bytes_accessed=4096, transcendentals=0),
     )(place, shares)
 
 

time: 90.9 us -> 90.9 us (level)
  no operation moved by 1% of the time
where the time goes in v4:
time: 90.9 us; the launch traced here: 90.7 us
  starting transfers between devices  36.5 us (40%)
  waiting for transfers between devices  21.5 us (24%)
  Pallas kernels  16.1 us (18%)
  blocking collectives  14.5 us (16%)
  other arithmetic  1.27 us (1%)
    ppermute x17, starting transfers between devices, send(): return lax.ppermute(value, AXES, pairs)  32.8 us
    ppermute x17, waiting for transfers between devices, send(): return lax.ppermute(value, AXES, pairs)  17.2 us
    all_to_all x1, blocking collectives, exchange(): lax.all_to_all(value, AXES, 0, 0, axis_index_groups=groups, tiled=True)  14.5 us
    pallas_call x2, Pallas kernels, pair_sums(): pl.pallas_call(functools.partial(pair_kernel, texts=len(texts), first=fir...  11.6 us
    all_to_all x1, waiting for transfers between devices, exchange(): lax.all_to_all(value, AXES, 0, 0, axis_index_groups=groups, tiled=True)  4.3 us
    all_to_all x1, starting transfers between devices, exchange(): lax.all_to_all(value, AXES, 0, 0, axis_index_groups=groups, tiled=True)  3.72 us
    pallas_call x1, Pallas kernels, text_shares(): pl.pallas_call(shares_kernel, in_specs=[VMEM, VMEM], out_specs=VMEM, out_...  1.86 us
  transfers between devices with their start and end apart: 18, of which 8 were waited for; matrix products, arithmetic and copies ran while one was open for 0% of the time, Pallas kernels for 11%

profile of v4, /device:TPU:1, one launch (start us, length us, event | category | flops | bytes accessed | tf_op | source)
XLA Modules:
  0.0 90.7 jit_solution(15978740268140622944)
XLA Ops:
  0.7 1.0 %broadcast_select_fusion = bf16[144,512]{1,0:T(8,128)(2,1)S(1)} fusion(bf16[144,512]{1,0:T(8,128)(2,1)} %param.8, bf16[144,512]{1,0:T(8,128)(2,1)} %param.6, pred[]{:T(512)S(6)} %eq.6), kind=kLoop, calls=%fused_computation.2 | loop fusion | flops 73728 | bytes 442369 | tf_op jit(solution)/shard_map/jit(_where)/select_n | solution.py:398
  1.7 3.3 %collective-permute-start = (bf16[144,512]{1,0:T(8,128)(2,1)S(1)}, bf16[144,512]{1,0:T(8,128)(2,1)S(1)}, u32[]{:S(2)}, u32[]{:S(2)}) collective-permute-start(bf16[144,512]{1,0:T(8,128)(2,1)S(1)} %broadcast_select_fusion), channel_id=1, source_target_pairs={{0,8},{1,9},{2,10},{3,11},{4,12},{5,13},{6,14},{7,15},{8,0},{9,1},... | collective-permute-start | bytes 442376 | tf_op jit(solution)/shard_map/ppermute | solution.py:32
  5.0 1.9 %shard_map.77 = bf16[16,80,128]{2,1,0:T(8,128)(2,1)} custom-call(bf16[144,512]{1,0:T(8,128)(2,1)} %learner_ref.1, bf16[144,512]{1,0:T(8,128)(2,1)} %refer_ref.1), custom_call_target="tpu_custom_call" | custom-call | tf_op jit(solution)/shard_map/pallas_call | solution.py:98
  6.9 0.0 collective-permute-done
  6.9 3.7 %all-to-all-start = ((bf16[16,80,128]{2,1,0:T(8,128)(2,1)}), bf16[16,80,128]{2,1,0:T(8,128)(2,1)S(1)}, u32[]{:S(2)}, u32[]{:S(2)}) async-start(bf16[16,80,128]{2,1,0:T(8,128)(2,1)} %shard_map.77), calls=%async_computation | async-start | bytes 655360 | tf_op jit(solution)/shard_map/all_to_all | solution.py:68
  10.6 2.8 %collective-permute-start.10 = (bf16[2,144,512]{2,1,0:T(8,128)(2,1)S(1)}, bf16[2,144,512]{2,1,0:T(8,128)(2,1)S(1)}, u32[]{:S(2)}, u32[]{:S(2)}) collective-permute-start(bf16[2,144,512]{2,1,0:T(8,128)(2,1)S(1)} %maximum_select_fusion), channel_id=1, source_target_pairs={{0,3},{1,2},{2,1},{3,0},{4,7},{5,6},{6,5},{7,4},{8,140},{9,141},{1... | collective-permute-start | bytes 884744 | tf_op jit(solution)/shard_map/ppermute | solution.py:32
  13.5 0.0 collective-permute-start.8
  13.5 1.3 %collective-permute-start.9 = (bf16[2,144,512]{2,1,0:T(8,128)(2,1)S(1)}, bf16[2,144,512]{2,1,0:T(8,128)(2,1)S(1)}, u32[]{:S(2)}, u32[]{:S(2)}) collective-permute-start(bf16[2,144,512]{2,1,0:T(8,128)(2,1)S(1)} %maximum_select_fusion), channel_id=1, source_target_pairs={{0,2},{1,3},{2,0},{3,1},{4,6},{5,7},{6,4},{7,5},{8,136},{9,137},{1... | collective-permute-start | bytes 884744 | tf_op jit(solution)/shard_map/ppermute | solution.py:32
  14.7 0.1 pad_add_fusion.place
  14.8 4.3 %all-to-all-done.in_ref = bf16[16,80,128]{2,1,0:T(8,128)(2,1)S(1)} async-done(((bf16[16,80,128]{2,1,0:T(8,128)(2,1)}), bf16[16,80,128]{2,1,0:T(8,128)(2,1)S(1)}, u32[]{:S(2)}, u32[]{:S(2)}) %all-to-all-start) | async-done | bytes 327712 | tf_op jit(solution)/shard_map/all_to_all | solution.py:68
  19.1 0.8 shard_map.78.refs_0_
  20.0 0.0 collective-permute-done.10
  20.0 1.4 %collective-permute-done.8 = bf16[2,144,512]{2,1,0:T(8,128)(2,1)S(1)} collective-permute-done((bf16[2,144,512]{2,1,0:T(8,128)(2,1)S(1)}, bf16[2,144,512]{2,1,0:T(8,128)(2,1)S(1)}, u32[]{:S(2)}, u32[]{:S(2)}) %collective-permute-start.8) | collective-permute-done | bytes 294944 | tf_op jit(solution)/shard_map/ppermute | solution.py:32
  21.3 3.5 %collective-permute-done.9 = bf16[2,144,512]{2,1,0:T(8,128)(2,1)S(1)} collective-permute-done((bf16[2,144,512]{2,1,0:T(8,128)(2,1)S(1)}, bf16[2,144,512]{2,1,0:T(8,128)(2,1)S(1)}, u32[]{:S(2)}, u32[]{:S(2)}) %collective-permute-start.9) | collective-permute-done | bytes 294944 | tf_op jit(solution)/shard_map/ppermute | solution.py:32
  24.8 0.1 pad_maximum_fusion.refs_5_
  24.9 0.0 copy-start
  25.0 0.0 copy-start.1
  25.0 2.1 %collective-permute-start.12 = (bf16[4,2,144,512]{3,2,1,0:T(8,128)(2,1)S(1)}, bf16[4,2,144,512]{3,2,1,0:T(8,128)(2,1)S(1)}, u32[]{:S(2)}, u32[]{:S(2)}) collective-permute-start(bf16[4,2,144,512]{3,2,1,0:T(8,128)(2,1)S(1)} %pad_maximum_fusion.refs_5_), channel_id=1, source_target_pairs={{0,132},{1,133},{2,134},{3,135},{4,128},{5,129},{6,130},{7,131},{8... | collective-permute-start | bytes 3538952 | tf_op jit(solution)/shard_map/ppermute | solution.py:32
  27.1 0.0 collective-permute-start.11
  27.1 5.6 %collective-permute-start.4 = (bf16[128,1152]{1,0:T(8,128)(2,1)S(1)}, bf16[128,1152]{1,0:T(8,128)(2,1)S(1)}, u32[]{:S(2)}, u32[]{:S(2)}) collective-permute-start(bf16[128,1152]{1,0:T(8,128)(2,1)S(1)} %shard_map.78.refs_0_), channel_id=1, source_target_pairs={{0,112},{1,113},{2,114},{3,115},{4,116},{5,117},{6,118},{7,119},{8... | collective-permute-start | bytes 884744 | tf_op jit(solution)/shard_map/ppermute | solution.py:32
  32.7 0.0 collective-permute-start.1
  32.7 5.0 %collective-permute-done.4.refs_2_ = bf16[128,1152]{1,0:T(8,128)(2,1)S(1)} collective-permute-done((bf16[128,1152]{1,0:T(8,128)(2,1)S(1)}, bf16[128,1152]{1,0:T(8,128)(2,1)S(1)}, u32[]{:S(2)}, u32[]{:S(2)}) %collective-permute-start.4) | collective-permute-done | bytes 294944 | tf_op jit(solution)/shard_map/ppermute | solution.py:32
  37.7 3.4 %collective-permute-start.5 = (bf16[128,1152]{1,0:T(8,128)(2,1)S(1)}, bf16[128,1152]{1,0:T(8,128)(2,1)S(1)}, u32[]{:S(2)}, u32[]{:S(2)}) collective-permute-start(bf16[128,1152]{1,0:T(8,128)(2,1)S(1)} %collective-permute-done.4.refs_2_), channel_id=1, source_target_pairs={{0,112},{1,113},{2,114},{3,115},{4,116},{5,117},{6,118},{7,119},{8... | collective-permute-start | bytes 884744 | tf_op jit(solution)/shard_map/ppermute | solution.py:32
  41.1 0.5 collective-permute-done.12.refs_9_
  41.7 2.4 %collective-permute-start.13 = (bf16[2,2,144,512]{3,2,1,0:T(8,128)(2,1)S(1)}, bf16[2,2,144,512]{3,2,1,0:T(8,128)(2,1)S(1)}, u32[]{:S(2)}, u32[]{:S(2)}) collective-permute-start(bf16[2,2,144,512]{3,2,1,0:T(8,128)(2,1)S(1)} %slice.8), channel_id=1, source_target_pairs={{0,4},{1,5},{2,6},{3,7},{4,0},{5,1},{6,2},{7,3},{8,9},{9,8},{10,11... | collective-permute-start | bytes 1769480 | tf_op jit(solution)/shard_map/ppermute | solution.py:32
  44.1 0.0 collective-permute-done.11.refs_6_
  44.1 1.0 %collective-permute-start.14 = (bf16[2,2,144,512]{3,2,1,0:T(8,128)(2,1)S(1)}, bf16[2,2,144,512]{3,2,1,0:T(8,128)(2,1)S(1)}, u32[]{:S(2)}, u32[]{:S(2)}) collective-permute-start(bf16[2,2,144,512]{3,2,1,0:T(8,128)(2,1)S(1)} %slice.9), channel_id=1, source_target_pairs={{0,132},{1,133},{2,134},{3,135},{4,128},{5,129},{6,130},{7,131},{8... | collective-permute-start | bytes 1769480 | tf_op jit(solution)/shard_map/ppermute | solution.py:32
  45.1 0.0 collective-permute-done.1.refs_1_
  45.1 0.3 collective-permute-start.2
  45.4 0.0 collective-permute-done.5.refs_4_
  45.4 4.2 %collective-permute-start.6 = (bf16[128,1152]{1,0:T(8,128)(2,1)S(1)}, bf16[128,1152]{1,0:T(8,128)(2,1)S(1)}, u32[]{:S(2)}, u32[]{:S(2)}) collective-permute-start(bf16[128,1152]{1,0:T(8,128)(2,1)S(1)} %collective-permute-done.5.refs_4_), channel_id=1, source_target_pairs={{0,112},{1,113},{2,114},{3,115},{4,116},{5,117},{6,118},{7,119},{8... | collective-permute-start | bytes 884744 | tf_op jit(solution)/shard_map/ppermute | solution.py:32
  49.6 5.1 %collective-permute-done.2.refs_3_ = bf16[128,1152]{1,0:T(8,128)(2,1)S(1)} collective-permute-done((bf16[128,1152]{1,0:T(8,128)(2,1)S(1)}, bf16[128,1152]{1,0:T(8,128)(2,1)S(1)}, u32[]{:S(2)}, u32[]{:S(2)}) %collective-permute-start.2) | collective-permute-done | bytes 294944 | tf_op jit(solution)/shard_map/ppermute | solution.py:32
  54.7 0.0 collective-permute-start.3
  54.7 0.0 collective-permute-done.6.refs_1_
  54.7 2.7 %collective-permute-start.7 = (bf16[128,1152]{1,0:T(8,128)(2,1)S(1)}, bf16[128,1152]{1,0:T(8,128)(2,1)S(1)}, u32[]{:S(2)}, u32[]{:S(2)}) collective-permute-start(bf16[128,1152]{1,0:T(8,128)(2,1)S(1)} %collective-permute-done.6.refs_1_), channel_id=1, source_target_pairs={{0,112},{1,113},{2,114},{3,115},{4,116},{5,117},{6,118},{7,119},{8... | collective-permute-start | bytes 884744 | tf_op jit(solution)/shard_map/ppermute | solution.py:32
  57.4 0.0 collective-permute-done.13.refs_7_
  57.4 0.0 collective-permute-done.14.refs_8_
  57.4 7.4 %shard_map.79 = (f32[16,128]{1,0:T(8,128)S(1)}, f32[16,128]{1,0:T(8,128)S(1)}, bf16[4,2,4,144,512]{4,3,2,1,0:T(8,128)(2,1)S(1)}, f32[4,1,512]{2,1,0:T(1,128)S(1)}) custom-call(f32[2]{0:T(128)S(1)} %copy-done, f32[2]{0:T(128)S(1)} %copy-done.1, s32[4]{0:T(128)S(1)} %pad_add_fusion.place, bf16[128,1152]{1,0:T(8,128)(2,1)S(1)} %shard_map.78.refs_0_, ...), custom_call_target="tpu_custom_call" | custom-call | flops 3019898880 | bytes 6193152 | tf_op jit(solution)/shard_map/pallas_call | solution.py:302
  64.8 0.0 collective-permute-done.3.refs_0_
  64.8 0.0 collective-permute-done.7.refs_2_
  64.8 4.2 %shard_map.80 = (f32[16,128]{1,0:T(8,128)S(1)}, f32[16,128]{1,0:T(8,128)S(1)}) custom-call(f32[2]{0:T(128)S(1)} %copy-done, f32[2]{0:T(128)S(1)} %copy-done.1, s32[4]{0:T(128)S(1)} %pad_add_fusion.place, bf16[128,1152]{1,0:T(8,128)(2,1)S(1)} %collective-permute-done.3.refs_0_, bf16[128,1152]{1,0:T(8,128)(2,1)S(1)} %collective-permute-done.6.refs_1_, ...), custom_call_target="tpu_custom_call" | custom-call | flops 1811939328 | bytes 5603328 | tf_op jit(solution)/shard_map/pallas_call | solution.py:302
  69.0 3.3 %collective-permute-start.15 = (f32[16,128]{1,0:T(8,128)S(1)}, f32[16,128]{1,0:T(8,128)S(1)}, u32[]{:S(2)}, u32[]{:S(2)}) collective-permute-start(f32[16,128]{1,0:T(8,128)S(1)} %get-tuple-element.25), channel_id=1, source_target_pairs={{0,8},{1,9},{2,10},{3,11},{4,12},{5,13},{6,14},{7,15},{8,0},{9,1},... | collective-permute-start | bytes 24584 | tf_op jit(solution)/shard_map/ppermute | solution.py:32
  72.4 0.8 collective-permute-done.15.got_ref
  73.2 0.6 shard_map.81
  73.8 14.5 %all_to_all.10.mine_ref = f32[16,2,128]{2,1,0:T(2,128)S(1)} all-to-all(f32[16,2,128]{2,1,0:T(2,128)S(1)} %shard_map.81), channel_id=1, replica_groups={{0,1,2,3,4,5,6,7,128,129,130,131,132,133,134,135},{8,136,24,152,40,168,..., dimensions={0} | all-to-all | bytes 32768 | tf_op jit(solution)/shard_map/all_to_all | solution.py:68
  88.3 0.3 collective-permute-start.16
  88.7 0.8 collective-permute-done.16.got_ref
  89.5 1.2 %shard_map.82 = (f32[2,64]{1,0:T(2,128)}, f32[2,64]{1,0:T(2,128)}) custom-call(s32[4]{0:T(128)S(1)} %pad_add_fusion.place, f32[16,2,128]{2,1,0:T(2,128)S(1)} %all_to_all.10.mine_ref, f32[16,2,128]{2,1,0:T(2,128)S(1)} %collective-permute-done.16.got_ref), custom_call_target="tpu_custom_call" | custom-call | tf_op jit(solution)/shard_map/pallas_call | solution.py:362
  (9 shorter events, 0.1 us)
Async XLA Ops:
  0.6 6.2 %copy-start.3 = (bf16[144,512]{1,0:T(8,128)(2,1)S(1)}, bf16[144,512]{1,0:T(8,128)(2,1)}, u32[]{:S(2)}) copy-start(bf16[144,512]{1,0:T(8,128)(2,1)} %param.6) | copy-start | bytes 442372
  0.6 6.2 %copy-start.2 = (bf16[144,512]{1,0:T(8,128)(2,1)S(1)}, bf16[144,512]{1,0:T(8,128)(2,1)}, u32[]{:S(2)}) copy-start(bf16[144,512]{1,0:T(8,128)(2,1)} %param.8) | copy-start | bytes 442372
  1.7 5.2 %collective-permute-start = (bf16[144,512]{1,0:T(8,128)(2,1)S(1)}, bf16[144,512]{1,0:T(8,128)(2,1)S(1)}, u32[]{:S(2)}, u32[]{:S(2)}) collective-permute-start(bf16[144,512]{1,0:T(8,128)(2,1)S(1)} %broadcast_select_fusion), channel_id=1, source_target_pairs={{0,8},{1,9},{2,10},{3,11},{4,12},{5,13},{6,14},{7,15},{8,0},{9,1},... | collective-permute-start | bytes 442376 | tf_op jit(solution)/shard_map/ppermute | solution.py:32
  6.9 12.2 %all-to-all-start = ((bf16[16,80,128]{2,1,0:T(8,128)(2,1)}), bf16[16,80,128]{2,1,0:T(8,128)(2,1)S(1)}, u32[]{:S(2)}, u32[]{:S(2)}) async-start(bf16[16,80,128]{2,1,0:T(8,128)(2,1)} %shard_map.77), calls=%async_computation | async-start | bytes 655360 | tf_op jit(solution)/shard_map/all_to_all | solution.py:68
  10.6 9.3 %collective-permute-start.10 = (bf16[2,144,512]{2,1,0:T(8,128)(2,1)S(1)}, bf16[2,144,512]{2,1,0:T(8,128)(2,1)S(1)}, u32[]{:S(2)}, u32[]{:S(2)}) collective-permute-start(bf16[2,144,512]{2,1,0:T(8,128)(2,1)S(1)} %maximum_select_fusion), channel_id=1, source_target_pairs={{0,3},{1,2},{2,1},{3,0},{4,7},{5,6},{6,5},{7,4},{8,140},{9,141},{1... | collective-permute-start | bytes 884744 | tf_op jit(solution)/shard_map/ppermute | solution.py:32
  13.5 7.9 %collective-permute-start.8 = (bf16[2,144,512]{2,1,0:T(8,128)(2,1)S(1)}, bf16[2,144,512]{2,1,0:T(8,128)(2,1)S(1)}, u32[]{:S(2)}, u32[]{:S(2)}) collective-permute-start(bf16[2,144,512]{2,1,0:T(8,128)(2,1)S(1)} %maximum_select_fusion), channel_id=1, source_target_pairs={{0,1},{1,0},{2,3},{3,2},{4,5},{5,4},{6,7},{7,6},{8,12},{9,13},{10,... | collective-permute-start | bytes 884744 | tf_op jit(solution)/shard_map/ppermute | solution.py:32
  13.5 11.3 %collective-permute-start.9 = (bf16[2,144,512]{2,1,0:T(8,128)(2,1)S(1)}, bf16[2,144,512]{2,1,0:T(8,128)(2,1)S(1)}, u32[]{:S(2)}, u32[]{:S(2)}) collective-permute-start(bf16[2,144,512]{2,1,0:T(8,128)(2,1)S(1)} %maximum_select_fusion), channel_id=1, source_target_pairs={{0,2},{1,3},{2,0},{3,1},{4,6},{5,7},{6,4},{7,5},{8,136},{9,137},{1... | collective-permute-start | bytes 884744 | tf_op jit(solution)/shard_map/ppermute | solution.py:32
  24.9 32.5 %copy-start = (f32[2]{0:T(128)S(1)}, f32[2]{0:T(128)}, u32[]{:S(2)}) copy-start(f32[2]{0:T(128)} %sharpness.3) | copy-start | bytes 28
  25.0 32.4 %copy-start.1 = (f32[2]{0:T(128)S(1)}, f32[2]{0:T(128)}, u32[]{:S(2)}) copy-start(f32[2]{0:T(128)} %offsets.3) | copy-start | bytes 28
  25.0 16.6 %collective-permute-start.12 = (bf16[4,2,144,512]{3,2,1,0:T(8,128)(2,1)S(1)}, bf16[4,2,144,512]{3,2,1,0:T(8,128)(2,1)S(1)}, u32[]{:S(2)}, u32[]{:S(2)}) collective-permute-start(bf16[4,2,144,512]{3,2,1,0:T(8,128)(2,1)S(1)} %pad_maximum_fusion.refs_5_), channel_id=1, source_target_pairs={{0,132},{1,133},{2,134},{3,135},{4,128},{5,129},{6,130},{7,131},{8... | collective-permute-start | bytes 3538952 | tf_op jit(solution)/shard_map/ppermute | solution.py:32
  27.1 17.0 %collective-permute-start.11 = (bf16[4,2,144,512]{3,2,1,0:T(8,128)(2,1)S(1)}, bf16[4,2,144,512]{3,2,1,0:T(8,128)(2,1)S(1)}, u32[]{:S(2)}, u32[]{:S(2)}) collective-permute-start(bf16[4,2,144,512]{3,2,1,0:T(8,128)(2,1)S(1)} %pad_maximum_fusion.refs_5_), channel_id=1, source_target_pairs={{0,4},{1,5},{2,6},{3,7},{4,0},{5,1},{6,2},{7,3},{8,9},{9,8},{10,11... | collective-permute-start | bytes 3538952 | tf_op jit(solution)/shard_map/ppermute | solution.py:32
  27.1 10.6 %collective-permute-start.4 = (bf16[128,1152]{1,0:T(8,128)(2,1)S(1)}, bf16[128,1152]{1,0:T(8,128)(2,1)S(1)}, u32[]{:S(2)}, u32[]{:S(2)}) collective-permute-start(bf16[128,1152]{1,0:T(8,128)(2,1)S(1)} %shard_map.78.refs_0_), channel_id=1, source_target_pairs={{0,112},{1,113},{2,114},{3,115},{4,116},{5,117},{6,118},{7,119},{8... | collective-permute-start | bytes 884744 | tf_op jit(solution)/shard_map/ppermute | solution.py:32
  32.7 12.4 %collective-permute-start.1 = (bf16[128,1152]{1,0:T(8,128)(2,1)S(1)}, bf16[128,1152]{1,0:T(8,128)(2,1)S(1)}, u32[]{:S(2)}, u32[]{:S(2)}) collective-permute-start(bf16[128,1152]{1,0:T(8,128)(2,1)S(1)} %shard_map.78.refs_0_), channel_id=1, source_target_pairs={{0,16},{1,17},{2,18},{3,19},{4,20},{5,21},{6,22},{7,23},{8,24},{9,... | collective-permute-start | bytes 884744 | tf_op jit(solution)/shard_map/ppermute | solution.py:32
  37.7 7.7 %collective-permute-start.5 = (bf16[128,1152]{1,0:T(8,128)(2,1)S(1)}, bf16[128,1152]{1,0:T(8,128)(2,1)S(1)}, u32[]{:S(2)}, u32[]{:S(2)}) collective-permute-start(bf16[128,1152]{1,0:T(8,128)(2,1)S(1)} %collective-permute-done.4.refs_2_), channel_id=1, source_target_pairs={{0,112},{1,113},{2,114},{3,115},{4,116},{5,117},{6,118},{7,119},{8... | collective-permute-start | bytes 884744 | tf_op jit(solution)/shard_map/ppermute | solution.py:32
  41.7 15.7 %collective-permute-start.13 = (bf16[2,2,144,512]{3,2,1,0:T(8,128)(2,1)S(1)}, bf16[2,2,144,512]{3,2,1,0:T(8,128)(2,1)S(1)}, u32[]{:S(2)}, u32[]{:S(2)}) collective-permute-start(bf16[2,2,144,512]{3,2,1,0:T(8,128)(2,1)S(1)} %slice.8), channel_id=1, source_target_pairs={{0,4},{1,5},{2,6},{3,7},{4,0},{5,1},{6,2},{7,3},{8,9},{9,8},{10,11... | collective-permute-start | bytes 1769480 | tf_op jit(solution)/shard_map/ppermute | solution.py:32
  44.1 13.3 %collective-permute-start.14 = (bf16[2,2,144,512]{3,2,1,0:T(8,128)(2,1)S(1)}, bf16[2,2,144,512]{3,2,1,0:T(8,128)(2,1)S(1)}, u32[]{:S(2)}, u32[]{:S(2)}) collective-permute-start(bf16[2,2,144,512]{3,2,1,0:T(8,128)(2,1)S(1)} %slice.9), channel_id=1, source_target_pairs={{0,132},{1,133},{2,134},{3,135},{4,128},{5,129},{6,130},{7,131},{8... | collective-permute-start | bytes 1769480 | tf_op jit(solution)/shard_map/ppermute | solution.py:32
  45.1 9.6 %collective-permute-start.2 = (bf16[128,1152]{1,0:T(8,128)(2,1)S(1)}, bf16[128,1152]{1,0:T(8,128)(2,1)S(1)}, u32[]{:S(2)}, u32[]{:S(2)}) collective-permute-start(bf16[128,1152]{1,0:T(8,128)(2,1)S(1)} %collective-permute-done.1.refs_1_), channel_id=1, source_target_pairs={{0,16},{1,17},{2,18},{3,19},{4,20},{5,21},{6,22},{7,23},{8,24},{9,... | collective-permute-start | bytes 884744 | tf_op jit(solution)/shard_map/ppermute | solution.py:32
  45.4 9.4 %collective-permute-start.6 = (bf16[128,1152]{1,0:T(8,128)(2,1)S(1)}, bf16[128,1152]{1,0:T(8,128)(2,1)S(1)}, u32[]{:S(2)}, u32[]{:S(2)}) collective-permute-start(bf16[128,1152]{1,0:T(8,128)(2,1)S(1)} %collective-permute-done.5.refs_4_), channel_id=1, source_target_pairs={{0,112},{1,113},{2,114},{3,115},{4,116},{5,117},{6,118},{7,119},{8... | collective-permute-start | bytes 884744 | tf_op jit(solution)/shard_map/ppermute | solution.py:32
  54.7 10.1 %collective-permute-start.3 = (bf16[128,1152]{1,0:T(8,128)(2,1)S(1)}, bf16[128,1152]{1,0:T(8,128)(2,1)S(1)}, u32[]{:S(2)}, u32[]{:S(2)}) collective-permute-start(bf16[128,1152]{1,0:T(8,128)(2,1)S(1)} %collective-permute-done.2.refs_3_), channel_id=1, source_target_pairs={{0,16},{1,17},{2,18},{3,19},{4,20},{5,21},{6,22},{7,23},{8,24},{9,... | collective-permute-start | bytes 884744 | tf_op jit(solution)/shard_map/ppermute | solution.py:32
  54.7 10.1 %collective-permute-start.7 = (bf16[128,1152]{1,0:T(8,128)(2,1)S(1)}, bf16[128,1152]{1,0:T(8,128)(2,1)S(1)}, u32[]{:S(2)}, u32[]{:S(2)}) collective-permute-start(bf16[128,1152]{1,0:T(8,128)(2,1)S(1)} %collective-permute-done.6.refs_1_), channel_id=1, source_target_pairs={{0,112},{1,113},{2,114},{3,115},{4,116},{5,117},{6,118},{7,119},{8... | collective-permute-start | bytes 884744 | tf_op jit(solution)/shard_map/ppermute | solution.py:32
  69.0 4.2 %collective-permute-start.15 = (f32[16,128]{1,0:T(8,128)S(1)}, f32[16,128]{1,0:T(8,128)S(1)}, u32[]{:S(2)}, u32[]{:S(2)}) collective-permute-start(f32[16,128]{1,0:T(8,128)S(1)} %get-tuple-element.25), channel_id=1, source_target_pairs={{0,8},{1,9},{2,10},{3,11},{4,12},{5,13},{6,14},{7,15},{8,0},{9,1},... | collective-permute-start | bytes 24584 | tf_op jit(solution)/shard_map/ppermute | solution.py:32
  88.3 1.2 %collective-permute-start.16 = (f32[16,2,128]{2,1,0:T(2,128)S(1)}, f32[16,2,128]{2,1,0:T(2,128)S(1)}, u32[]{:S(2)}, u32[]{:S(2)}) collective-permute-start(f32[16,2,128]{2,1,0:T(2,128)S(1)} %all_to_all.10.mine_ref), channel_id=1, source_target_pairs={{0,8},{1,9},{2,10},{3,11},{4,12},{5,13},{6,14},{7,15},{8,0},{9,1},... | collective-permute-start | bytes 49160 | tf_op jit(solution)/shard_map/ppermute | solution.py:32

commit v5 on v4

--- a/solution.py
+++ b/solution.py
@@ -211,11 +211,11 @@
 
     def product(block, part, out):
         flat = image.at[block].reshape(depth, columns)
+        rows_at = slice(part * span, (part + 1) * span)
+        whole = depth // 256 * 256
         out[...] = jnp.dot(
-            text[part * span : (part + 1) * span, :],
-            flat[...],
-            preferred_element_type=jnp.float32,
-        )
+            text[rows_at, :whole], flat[:whole, :], preferred_element_type=jnp.float32
+        ) + jnp.dot(text[rows_at, whole:], flat[whole:, :], preferred_element_type=jnp.float32)
 
     def losses(block, part, products):
         owner, high = block // 2, block % 2

time: 90.9 us -> 90.9 us (level)
  no operation moved by 1% of the time
where the time goes in v5:
time: 90.9 us; the launch traced here: 90.6 us
  starting transfers between devices  36.5 us (40%)
  waiting for transfers between devices  21.5 us (24%)
  Pallas kernels  16 us (18%)
  blocking collectives  14.5 us (16%)
  other arithmetic  1.27 us (1%)
    ppermute x17, starting transfers between devices, send(): return lax.ppermute(value, AXES, pairs)  32.7 us
    ppermute x17, waiting for transfers between devices, send(): return lax.ppermute(value, AXES, pairs)  17.2 us
    all_to_all x1, blocking collectives, exchange(): lax.all_to_all(value, AXES, 0, 0, axis_index_groups=groups, tiled=True)  14.5 us
    pallas_call x2, Pallas kernels, pair_sums(): pl.pallas_call(functools.partial(pair_kernel, texts=len(texts), first=fir...  11.6 us
    all_to_all x1, waiting for transfers between devices, exchange(): lax.all_to_all(value, AXES, 0, 0, axis_index_groups=groups, tiled=True)  4.3 us
    all_to_all x1, starting transfers between devices, exchange(): lax.all_to_all(value, AXES, 0, 0, axis_index_groups=groups, tiled=True)  3.72 us
    pallas_call x1, Pallas kernels, text_shares(): pl.pallas_call(shares_kernel, in_specs=[VMEM, VMEM], out_specs=VMEM, out_...  1.86 us
  transfers between devices with their start and end apart: 18, of which 8 were waited for; matrix products, arithmetic and copies ran while one was open for 0% of the time, Pallas kernels for 11%

profile of v5, /device:TPU:1, one launch (start us, length us, event | category | flops | bytes accessed | tf_op | source)
XLA Modules:
  0.0 90.6 jit_solution(3139479930385985489)
XLA Ops:
  0.7 1.0 %broadcast_select_fusion = bf16[144,512]{1,0:T(8,128)(2,1)S(1)} fusion(bf16[144,512]{1,0:T(8,128)(2,1)} %param.8, bf16[144,512]{1,0:T(8,128)(2,1)} %param.6, pred[]{:T(512)S(6)} %eq.6), kind=kLoop, calls=%fused_computation.2 | loop fusion | flops 73728 | bytes 442369 | tf_op jit(solution)/shard_map/jit(_where)/select_n | solution.py:398
  1.7 3.3 %collective-permute-start = (bf16[144,512]{1,0:T(8,128)(2,1)S(1)}, bf16[144,512]{1,0:T(8,128)(2,1)S(1)}, u32[]{:S(2)}, u32[]{:S(2)}) collective-permute-start(bf16[144,512]{1,0:T(8,128)(2,1)S(1)} %broadcast_select_fusion), channel_id=1, source_target_pairs={{0,8},{1,9},{2,10},{3,11},{4,12},{5,13},{6,14},{7,15},{8,0},{9,1},... | collective-permute-start | bytes 442376 | tf_op jit(solution)/shard_map/ppermute | solution.py:32
  5.0 1.9 %shard_map.77 = bf16[16,80,128]{2,1,0:T(8,128)(2,1)} custom-call(bf16[144,512]{1,0:T(8,128)(2,1)} %learner_ref.1, bf16[144,512]{1,0:T(8,128)(2,1)} %refer_ref.1), custom_call_target="tpu_custom_call" | custom-call | tf_op jit(solution)/shard_map/pallas_call | solution.py:98
  6.9 0.0 collective-permute-done
  6.9 3.7 %all-to-all-start = ((bf16[16,80,128]{2,1,0:T(8,128)(2,1)}), bf16[16,80,128]{2,1,0:T(8,128)(2,1)S(1)}, u32[]{:S(2)}, u32[]{:S(2)}) async-start(bf16[16,80,128]{2,1,0:T(8,128)(2,1)} %shard_map.77), calls=%async_computation | async-start | bytes 655360 | tf_op jit(solution)/shard_map/all_to_all | solution.py:68
  10.6 2.8 %collective-permute-start.10 = (bf16[2,144,512]{2,1,0:T(8,128)(2,1)S(1)}, bf16[2,144,512]{2,1,0:T(8,128)(2,1)S(1)}, u32[]{:S(2)}, u32[]{:S(2)}) collective-permute-start(bf16[2,144,512]{2,1,0:T(8,128)(2,1)S(1)} %maximum_select_fusion), channel_id=1, source_target_pairs={{0,3},{1,2},{2,1},{3,0},{4,7},{5,6},{6,5},{7,4},{8,140},{9,141},{1... | collective-permute-start | bytes 884744 | tf_op jit(solution)/shard_map/ppermute | solution.py:32
  13.5 0.0 collective-permute-start.8
  13.5 1.3 %collective-permute-start.9 = (bf16[2,144,512]{2,1,0:T(8,128)(2,1)S(1)}, bf16[2,144,512]{2,1,0:T(8,128)(2,1)S(1)}, u32[]{:S(2)}, u32[]{:S(2)}) collective-permute-start(bf16[2,144,512]{2,1,0:T(8,128)(2,1)S(1)} %maximum_select_fusion), channel_id=1, source_target_pairs={{0,2},{1,3},{2,0},{3,1},{4,6},{5,7},{6,4},{7,5},{8,136},{9,137},{1... | collective-permute-start | bytes 884744 | tf_op jit(solution)/shard_map/ppermute | solution.py:32
  14.7 0.1 pad_add_fusion.place
  14.8 4.3 %all-to-all-done.in_ref = bf16[16,80,128]{2,1,0:T(8,128)(2,1)S(1)} async-done(((bf16[16,80,128]{2,1,0:T(8,128)(2,1)}), bf16[16,80,128]{2,1,0:T(8,128)(2,1)S(1)}, u32[]{:S(2)}, u32[]{:S(2)}) %all-to-all-start) | async-done | bytes 327712 | tf_op jit(solution)/shard_map/all_to_all | solution.py:68
  19.1 0.8 shard_map.78.refs_0_
  20.0 0.0 collective-permute-done.10
  20.0 1.4 %collective-permute-done.8 = bf16[2,144,512]{2,1,0:T(8,128)(2,1)S(1)} collective-permute-done((bf16[2,144,512]{2,1,0:T(8,128)(2,1)S(1)}, bf16[2,144,512]{2,1,0:T(8,128)(2,1)S(1)}, u32[]{:S(2)}, u32[]{:S(2)}) %collective-permute-start.8) | collective-permute-done | bytes 294944 | tf_op jit(solution)/shard_map/ppermute | solution.py:32
  21.3 3.5 %collective-permute-done.9 = bf16[2,144,512]{2,1,0:T(8,128)(2,1)S(1)} collective-permute-done((bf16[2,144,512]{2,1,0:T(8,128)(2,1)S(1)}, bf16[2,144,512]{2,1,0:T(8,128)(2,1)S(1)}, u32[]{:S(2)}, u32[]{:S(2)}) %collective-permute-start.9) | collective-permute-done | bytes 294944 | tf_op jit(solution)/shard_map/ppermute | solution.py:32
  24.8 0.1 pad_maximum_fusion.refs_5_
  24.9 0.0 copy-start
  25.0 0.0 copy-start.1
  25.0 2.1 %collective-permute-start.12 = (bf16[4,2,144,512]{3,2,1,0:T(8,128)(2,1)S(1)}, bf16[4,2,144,512]{3,2,1,0:T(8,128)(2,1)S(1)}, u32[]{:S(2)}, u32[]{:S(2)}) collective-permute-start(bf16[4,2,144,512]{3,2,1,0:T(8,128)(2,1)S(1)} %pad_maximum_fusion.refs_5_), channel_id=1, source_target_pairs={{0,132},{1,133},{2,134},{3,135},{4,128},{5,129},{6,130},{7,131},{8... | collective-permute-start | bytes 3538952 | tf_op jit(solution)/shard_map/ppermute | solution.py:32
  27.1 0.0 collective-permute-start.11
  27.1 5.6 %collective-permute-start.4 = (bf16[128,1152]{1,0:T(8,128)(2,1)S(1)}, bf16[128,1152]{1,0:T(8,128)(2,1)S(1)}, u32[]{:S(2)}, u32[]{:S(2)}) collective-permute-start(bf16[128,1152]{1,0:T(8,128)(2,1)S(1)} %shard_map.78.refs_0_), channel_id=1, source_target_pairs={{0,112},{1,113},{2,114},{3,115},{4,116},{5,117},{6,118},{7,119},{8... | collective-permute-start | bytes 884744 | tf_op jit(solution)/shard_map/ppermute | solution.py:32
  32.7 0.0 collective-permute-start.1
  32.7 5.0 %collective-permute-done.4.refs_2_ = bf16[128,1152]{1,0:T(8,128)(2,1)S(1)} collective-permute-done((bf16[128,1152]{1,0:T(8,128)(2,1)S(1)}, bf16[128,1152]{1,0:T(8,128)(2,1)S(1)}, u32[]{:S(2)}, u32[]{:S(2)}) %collective-permute-start.4) | collective-permute-done | bytes 294944 | tf_op jit(solution)/shard_map/ppermute | solution.py:32
  37.7 3.4 %collective-permute-start.5 = (bf16[128,1152]{1,0:T(8,128)(2,1)S(1)}, bf16[128,1152]{1,0:T(8,128)(2,1)S(1)}, u32[]{:S(2)}, u32[]{:S(2)}) collective-permute-start(bf16[128,1152]{1,0:T(8,128)(2,1)S(1)} %collective-permute-done.4.refs_2_), channel_id=1, source_target_pairs={{0,112},{1,113},{2,114},{3,115},{4,116},{5,117},{6,118},{7,119},{8... | collective-permute-start | bytes 884744 | tf_op jit(solution)/shard_map/ppermute | solution.py:32
  41.1 0.5 collective-permute-done.12.refs_9_
  41.7 2.4 %collective-permute-start.13 = (bf16[2,2,144,512]{3,2,1,0:T(8,128)(2,1)S(1)}, bf16[2,2,144,512]{3,2,1,0:T(8,128)(2,1)S(1)}, u32[]{:S(2)}, u32[]{:S(2)}) collective-permute-start(bf16[2,2,144,512]{3,2,1,0:T(8,128)(2,1)S(1)} %slice.8), channel_id=1, source_target_pairs={{0,4},{1,5},{2,6},{3,7},{4,0},{5,1},{6,2},{7,3},{8,9},{9,8},{10,11... | collective-permute-start | bytes 1769480 | tf_op jit(solution)/shard_map/ppermute | solution.py:32
  44.1 0.0 collective-permute-done.11.refs_6_
  44.1 1.0 %collective-permute-start.14 = (bf16[2,2,144,512]{3,2,1,0:T(8,128)(2,1)S(1)}, bf16[2,2,144,512]{3,2,1,0:T(8,128)(2,1)S(1)}, u32[]{:S(2)}, u32[]{:S(2)}) collective-permute-start(bf16[2,2,144,512]{3,2,1,0:T(8,128)(2,1)S(1)} %slice.9), channel_id=1, source_target_pairs={{0,132},{1,133},{2,134},{3,135},{4,128},{5,129},{6,130},{7,131},{8... | collective-permute-start | bytes 1769480 | tf_op jit(solution)/shard_map/ppermute | solution.py:32
  45.1 0.0 collective-permute-done.1.refs_1_
  45.1 0.3 collective-permute-start.2
  45.4 0.0 collective-permute-done.5.refs_4_
  45.4 4.2 %collective-permute-start.6 = (bf16[128,1152]{1,0:T(8,128)(2,1)S(1)}, bf16[128,1152]{1,0:T(8,128)(2,1)S(1)}, u32[]{:S(2)}, u32[]{:S(2)}) collective-permute-start(bf16[128,1152]{1,0:T(8,128)(2,1)S(1)} %collective-permute-done.5.refs_4_), channel_id=1, source_target_pairs={{0,112},{1,113},{2,114},{3,115},{4,116},{5,117},{6,118},{7,119},{8... | collective-permute-start | bytes 884744 | tf_op jit(solution)/shard_map/ppermute | solution.py:32
  49.6 5.1 %collective-permute-done.2.refs_3_ = bf16[128,1152]{1,0:T(8,128)(2,1)S(1)} collective-permute-done((bf16[128,1152]{1,0:T(8,128)(2,1)S(1)}, bf16[128,1152]{1,0:T(8,128)(2,1)S(1)}, u32[]{:S(2)}, u32[]{:S(2)}) %collective-permute-start.2) | collective-permute-done | bytes 294944 | tf_op jit(solution)/shard_map/ppermute | solution.py:32
  54.7 0.0 collective-permute-start.3
  54.7 0.0 collective-permute-done.6.refs_1_
  54.7 2.7 %collective-permute-start.7 = (bf16[128,1152]{1,0:T(8,128)(2,1)S(1)}, bf16[128,1152]{1,0:T(8,128)(2,1)S(1)}, u32[]{:S(2)}, u32[]{:S(2)}) collective-permute-start(bf16[128,1152]{1,0:T(8,128)(2,1)S(1)} %collective-permute-done.6.refs_1_), channel_id=1, source_target_pairs={{0,112},{1,113},{2,114},{3,115},{4,116},{5,117},{6,118},{7,119},{8... | collective-permute-start | bytes 884744 | tf_op jit(solution)/shard_map/ppermute | solution.py:32
  57.4 0.0 collective-permute-done.13.refs_7_
  57.4 0.0 collective-permute-done.14.refs_8_
  57.4 7.4 %shard_map.79 = (f32[16,128]{1,0:T(8,128)S(1)}, f32[16,128]{1,0:T(8,128)S(1)}, bf16[4,2,4,144,512]{4,3,2,1,0:T(8,128)(2,1)S(1)}, f32[4,1,512]{2,1,0:T(1,128)S(1)}) custom-call(f32[2]{0:T(128)S(1)} %copy-done, f32[2]{0:T(128)S(1)} %copy-done.1, s32[4]{0:T(128)S(1)} %pad_add_fusion.place, bf16[128,1152]{1,0:T(8,128)(2,1)S(1)} %shard_map.78.refs_0_, ...), custom_call_target="tpu_custom_call" | custom-call | flops 3019898880 | bytes 6193152 | tf_op jit(solution)/shard_map/pallas_call | solution.py:302
  64.8 0.0 collective-permute-done.3.refs_0_
  64.8 0.0 collective-permute-done.7.refs_2_
  64.8 4.2 %shard_map.80 = (f32[16,128]{1,0:T(8,128)S(1)}, f32[16,128]{1,0:T(8,128)S(1)}) custom-call(f32[2]{0:T(128)S(1)} %copy-done, f32[2]{0:T(128)S(1)} %copy-done.1, s32[4]{0:T(128)S(1)} %pad_add_fusion.place, bf16[128,1152]{1,0:T(8,128)(2,1)S(1)} %collective-permute-done.3.refs_0_, bf16[128,1152]{1,0:T(8,128)(2,1)S(1)} %collective-permute-done.6.refs_1_, ...), custom_call_target="tpu_custom_call" | custom-call | flops 1811939328 | bytes 5603328 | tf_op jit(solution)/shard_map/pallas_call | solution.py:302
  69.0 3.3 %collective-permute-start.15 = (f32[16,128]{1,0:T(8,128)S(1)}, f32[16,128]{1,0:T(8,128)S(1)}, u32[]{:S(2)}, u32[]{:S(2)}) collective-permute-start(f32[16,128]{1,0:T(8,128)S(1)} %get-tuple-element.25), channel_id=1, source_target_pairs={{0,8},{1,9},{2,10},{3,11},{4,12},{5,13},{6,14},{7,15},{8,0},{9,1},... | collective-permute-start | bytes 24584 | tf_op jit(solution)/shard_map/ppermute | solution.py:32
  72.3 0.8 collective-permute-done.15.got_ref
  73.1 0.6 shard_map.81
  73.7 14.5 %all_to_all.10.mine_ref = f32[16,2,128]{2,1,0:T(2,128)S(1)} all-to-all(f32[16,2,128]{2,1,0:T(2,128)S(1)} %shard_map.81), channel_id=1, replica_groups={{0,1,2,3,4,5,6,7,128,129,130,131,132,133,134,135},{8,136,24,152,40,168,..., dimensions={0} | all-to-all | bytes 32768 | tf_op jit(solution)/shard_map/all_to_all | solution.py:68
  88.2 0.3 collective-permute-start.16
  88.6 0.9 collective-permute-done.16.got_ref
  89.4 1.2 %shard_map.82 = (f32[2,64]{1,0:T(2,128)}, f32[2,64]{1,0:T(2,128)}) custom-call(s32[4]{0:T(128)S(1)} %pad_add_fusion.place, f32[16,2,128]{2,1,0:T(2,128)S(1)} %all_to_all.10.mine_ref, f32[16,2,128]{2,1,0:T(2,128)S(1)} %collective-permute-done.16.got_ref), custom_call_target="tpu_custom_call" | custom-call | tf_op jit(solution)/shard_map/pallas_call | solution.py:362
  (9 shorter events, 0.1 us)
Async XLA Ops:
  0.6 6.2 %copy-start.3 = (bf16[144,512]{1,0:T(8,128)(2,1)S(1)}, bf16[144,512]{1,0:T(8,128)(2,1)}, u32[]{:S(2)}) copy-start(bf16[144,512]{1,0:T(8,128)(2,1)} %param.6) | copy-start | bytes 442372
  0.6 6.2 %copy-start.2 = (bf16[144,512]{1,0:T(8,128)(2,1)S(1)}, bf16[144,512]{1,0:T(8,128)(2,1)}, u32[]{:S(2)}) copy-start(bf16[144,512]{1,0:T(8,128)(2,1)} %param.8) | copy-start | bytes 442372
  1.7 5.2 %collective-permute-start = (bf16[144,512]{1,0:T(8,128)(2,1)S(1)}, bf16[144,512]{1,0:T(8,128)(2,1)S(1)}, u32[]{:S(2)}, u32[]{:S(2)}) collective-permute-start(bf16[144,512]{1,0:T(8,128)(2,1)S(1)} %broadcast_select_fusion), channel_id=1, source_target_pairs={{0,8},{1,9},{2,10},{3,11},{4,12},{5,13},{6,14},{7,15},{8,0},{9,1},... | collective-permute-start | bytes 442376 | tf_op jit(solution)/shard_map/ppermute | solution.py:32
  6.9 12.2 %all-to-all-start = ((bf16[16,80,128]{2,1,0:T(8,128)(2,1)}), bf16[16,80,128]{2,1,0:T(8,128)(2,1)S(1)}, u32[]{:S(2)}, u32[]{:S(2)}) async-start(bf16[16,80,128]{2,1,0:T(8,128)(2,1)} %shard_map.77), calls=%async_computation | async-start | bytes 655360 | tf_op jit(solution)/shard_map/all_to_all | solution.py:68
  10.6 9.3 %collective-permute-start.10 = (bf16[2,144,512]{2,1,0:T(8,128)(2,1)S(1)}, bf16[2,144,512]{2,1,0:T(8,128)(2,1)S(1)}, u32[]{:S(2)}, u32[]{:S(2)}) collective-permute-start(bf16[2,144,512]{2,1,0:T(8,128)(2,1)S(1)} %maximum_select_fusion), channel_id=1, source_target_pairs={{0,3},{1,2},{2,1},{3,0},{4,7},{5,6},{6,5},{7,4},{8,140},{9,141},{1... | collective-permute-start | bytes 884744 | tf_op jit(solution)/shard_map/ppermute | solution.py:32
  13.5 7.9 %collective-permute-start.8 = (bf16[2,144,512]{2,1,0:T(8,128)(2,1)S(1)}, bf16[2,144,512]{2,1,0:T(8,128)(2,1)S(1)}, u32[]{:S(2)}, u32[]{:S(2)}) collective-permute-start(bf16[2,144,512]{2,1,0:T(8,128)(2,1)S(1)} %maximum_select_fusion), channel_id=1, source_target_pairs={{0,1},{1,0},{2,3},{3,2},{4,5},{5,4},{6,7},{7,6},{8,12},{9,13},{10,... | collective-permute-start | bytes 884744 | tf_op jit(solution)/shard_map/ppermute | solution.py:32
  13.5 11.3 %collective-permute-start.9 = (bf16[2,144,512]{2,1,0:T(8,128)(2,1)S(1)}, bf16[2,144,512]{2,1,0:T(8,128)(2,1)S(1)}, u32[]{:S(2)}, u32[]{:S(2)}) collective-permute-start(bf16[2,144,512]{2,1,0:T(8,128)(2,1)S(1)} %maximum_select_fusion), channel_id=1, source_target_pairs={{0,2},{1,3},{2,0},{3,1},{4,6},{5,7},{6,4},{7,5},{8,136},{9,137},{1... | collective-permute-start | bytes 884744 | tf_op jit(solution)/shard_map/ppermute | solution.py:32
  24.9 32.5 %copy-start = (f32[2]{0:T(128)S(1)}, f32[2]{0:T(128)}, u32[]{:S(2)}) copy-start(f32[2]{0:T(128)} %sharpness.3) | copy-start | bytes 28
  25.0 32.4 %copy-start.1 = (f32[2]{0:T(128)S(1)}, f32[2]{0:T(128)}, u32[]{:S(2)}) copy-start(f32[2]{0:T(128)} %offsets.3) | copy-start | bytes 28
  25.0 16.6 %collective-permute-start.12 = (bf16[4,2,144,512]{3,2,1,0:T(8,128)(2,1)S(1)}, bf16[4,2,144,512]{3,2,1,0:T(8,128)(2,1)S(1)}, u32[]{:S(2)}, u32[]{:S(2)}) collective-permute-start(bf16[4,2,144,512]{3,2,1,0:T(8,128)(2,1)S(1)} %pad_maximum_fusion.refs_5_), channel_id=1, source_target_pairs={{0,132},{1,133},{2,134},{3,135},{4,128},{5,129},{6,130},{7,131},{8... | collective-permute-start | bytes 3538952 | tf_op jit(solution)/shard_map/ppermute | solution.py:32
  27.1 17.0 %collective-permute-start.11 = (bf16[4,2,144,512]{3,2,1,0:T(8,128)(2,1)S(1)}, bf16[4,2,144,512]{3,2,1,0:T(8,128)(2,1)S(1)}, u32[]{:S(2)}, u32[]{:S(2)}) collective-permute-start(bf16[4,2,144,512]{3,2,1,0:T(8,128)(2,1)S(1)} %pad_maximum_fusion.refs_5_), channel_id=1, source_target_pairs={{0,4},{1,5},{2,6},{3,7},{4,0},{5,1},{6,2},{7,3},{8,9},{9,8},{10,11... | collective-permute-start | bytes 3538952 | tf_op jit(solution)/shard_map/ppermute | solution.py:32
  27.1 10.6 %collective-permute-start.4 = (bf16[128,1152]{1,0:T(8,128)(2,1)S(1)}, bf16[128,1152]{1,0:T(8,128)(2,1)S(1)}, u32[]{:S(2)}, u32[]{:S(2)}) collective-permute-start(bf16[128,1152]{1,0:T(8,128)(2,1)S(1)} %shard_map.78.refs_0_), channel_id=1, source_target_pairs={{0,112},{1,113},{2,114},{3,115},{4,116},{5,117},{6,118},{7,119},{8... | collective-permute-start | bytes 884744 | tf_op jit(solution)/shard_map/ppermute | solution.py:32
  32.7 12.4 %collective-permute-start.1 = (bf16[128,1152]{1,0:T(8,128)(2,1)S(1)}, bf16[128,1152]{1,0:T(8,128)(2,1)S(1)}, u32[]{:S(2)}, u32[]{:S(2)}) collective-permute-start(bf16[128,1152]{1,0:T(8,128)(2,1)S(1)} %shard_map.78.refs_0_), channel_id=1, source_target_pairs={{0,16},{1,17},{2,18},{3,19},{4,20},{5,21},{6,22},{7,23},{8,24},{9,... | collective-permute-start | bytes 884744 | tf_op jit(solution)/shard_map/ppermute | solution.py:32
  37.7 7.7 %collective-permute-start.5 = (bf16[128,1152]{1,0:T(8,128)(2,1)S(1)}, bf16[128,1152]{1,0:T(8,128)(2,1)S(1)}, u32[]{:S(2)}, u32[]{:S(2)}) collective-permute-start(bf16[128,1152]{1,0:T(8,128)(2,1)S(1)} %collective-permute-done.4.refs_2_), channel_id=1, source_target_pairs={{0,112},{1,113},{2,114},{3,115},{4,116},{5,117},{6,118},{7,119},{8... | collective-permute-start | bytes 884744 | tf_op jit(solution)/shard_map/ppermute | solution.py:32
  41.7 15.7 %collective-permute-start.13 = (bf16[2,2,144,512]{3,2,1,0:T(8,128)(2,1)S(1)}, bf16[2,2,144,512]{3,2,1,0:T(8,128)(2,1)S(1)}, u32[]{:S(2)}, u32[]{:S(2)}) collective-permute-start(bf16[2,2,144,512]{3,2,1,0:T(8,128)(2,1)S(1)} %slice.8), channel_id=1, source_target_pairs={{0,4},{1,5},{2,6},{3,7},{4,0},{5,1},{6,2},{7,3},{8,9},{9,8},{10,11... | collective-permute-start | bytes 1769480 | tf_op jit(solution)/shard_map/ppermute | solution.py:32
  44.1 13.3 %collective-permute-start.14 = (bf16[2,2,144,512]{3,2,1,0:T(8,128)(2,1)S(1)}, bf16[2,2,144,512]{3,2,1,0:T(8,128)(2,1)S(1)}, u32[]{:S(2)}, u32[]{:S(2)}) collective-permute-start(bf16[2,2,144,512]{3,2,1,0:T(8,128)(2,1)S(1)} %slice.9), channel_id=1, source_target_pairs={{0,132},{1,133},{2,134},{3,135},{4,128},{5,129},{6,130},{7,131},{8... | collective-permute-start | bytes 1769480 | tf_op jit(solution)/shard_map/ppermute | solution.py:32
  45.1 9.6 %collective-permute-start.2 = (bf16[128,1152]{1,0:T(8,128)(2,1)S(1)}, bf16[128,1152]{1,0:T(8,128)(2,1)S(1)}, u32[]{:S(2)}, u32[]{:S(2)}) collective-permute-start(bf16[128,1152]{1,0:T(8,128)(2,1)S(1)} %collective-permute-done.1.refs_1_), channel_id=1, source_target_pairs={{0,16},{1,17},{2,18},{3,19},{4,20},{5,21},{6,22},{7,23},{8,24},{9,... | collective-permute-start | bytes 884744 | tf_op jit(solution)/shard_map/ppermute | solution.py:32
  45.4 9.4 %collective-permute-start.6 = (bf16[128,1152]{1,0:T(8,128)(2,1)S(1)}, bf16[128,1152]{1,0:T(8,128)(2,1)S(1)}, u32[]{:S(2)}, u32[]{:S(2)}) collective-permute-start(bf16[128,1152]{1,0:T(8,128)(2,1)S(1)} %collective-permute-done.5.refs_4_), channel_id=1, source_target_pairs={{0,112},{1,113},{2,114},{3,115},{4,116},{5,117},{6,118},{7,119},{8... | collective-permute-start | bytes 884744 | tf_op jit(solution)/shard_map/ppermute | solution.py:32
  54.7 10.1 %collective-permute-start.3 = (bf16[128,1152]{1,0:T(8,128)(2,1)S(1)}, bf16[128,1152]{1,0:T(8,128)(2,1)S(1)}, u32[]{:S(2)}, u32[]{:S(2)}) collective-permute-start(bf16[128,1152]{1,0:T(8,128)(2,1)S(1)} %collective-permute-done.2.refs_3_), channel_id=1, source_target_pairs={{0,16},{1,17},{2,18},{3,19},{4,20},{5,21},{6,22},{7,23},{8,24},{9,... | collective-permute-start | bytes 884744 | tf_op jit(solution)/shard_map/ppermute | solution.py:32
  54.7 10.1 %collective-permute-start.7 = (bf16[128,1152]{1,0:T(8,128)(2,1)S(1)}, bf16[128,1152]{1,0:T(8,128)(2,1)S(1)}, u32[]{:S(2)}, u32[]{:S(2)}) collective-permute-start(bf16[128,1152]{1,0:T(8,128)(2,1)S(1)} %collective-permute-done.6.refs_1_), channel_id=1, source_target_pairs={{0,112},{1,113},{2,114},{3,115},{4,116},{5,117},{6,118},{7,119},{8... | collective-permute-start | bytes 884744 | tf_op jit(solution)/shard_map/ppermute | solution.py:32
  69.0 4.2 %collective-permute-start.15 = (f32[16,128]{1,0:T(8,128)S(1)}, f32[16,128]{1,0:T(8,128)S(1)}, u32[]{:S(2)}, u32[]{:S(2)}) collective-permute-start(f32[16,128]{1,0:T(8,128)S(1)} %get-tuple-element.25), channel_id=1, source_target_pairs={{0,8},{1,9},{2,10},{3,11},{4,12},{5,13},{6,14},{7,15},{8,0},{9,1},... | collective-permute-start | bytes 24584 | tf_op jit(solution)/shard_map/ppermute | solution.py:32
  88.2 1.2 %collective-permute-start.16 = (f32[16,2,128]{2,1,0:T(2,128)S(1)}, f32[16,2,128]{2,1,0:T(2,128)S(1)}, u32[]{:S(2)}, u32[]{:S(2)}) collective-permute-start(f32[16,2,128]{2,1,0:T(2,128)S(1)} %all_to_all.10.mine_ref), channel_id=1, source_target_pairs={{0,8},{1,9},{2,10},{3,11},{4,12},{5,13},{6,14},{7,15},{8,0},{9,1},... | collective-permute-start | bytes 49160 | tf_op jit(solution)/shard_map/ppermute | solution.py:32

commit v6 on v5

--- a/solution.py
+++ b/solution.py
@@ -258,12 +258,12 @@
     steps = [(block, part) for block in range(4) for part in range(parts)]
     buffers = (even, odd)
     for n, step in enumerate(steps + [None]):
+        if n > 0:
+            losses(*steps[n - 1], buffers[(n - 1) % 2])
         if step is not None:
             if first and step[1] == 0:
                 scale_block(step[0])
             product(*step, buffers[n % 2])
-        if n > 0:
-            losses(*steps[n - 1], buffers[(n - 1) % 2])
 
     text_sums[...] = jnp.zeros_like(text_sums) if first else before_text[...]
     for i, planes in enumerate((0, 1, 7, 2, 6) if first else (3, 5, 4)):

time: 90.9 us -> 90.9 us (level)
  no operation moved by 1% of the time
where the time goes in v6:
time: 90.9 us; the launch traced here: 90.6 us
  starting transfers between devices  36.5 us (40%)
  waiting for transfers between devices  21.5 us (24%)
  Pallas kernels  16 us (18%)
  blocking collectives  14.5 us (16%)
  other arithmetic  1.27 us (1%)
    ppermute x17, starting transfers between devices, send(): return lax.ppermute(value, AXES, pairs)  32.8 us
    ppermute x17, waiting for transfers between devices, send(): return lax.ppermute(value, AXES, pairs)  17.2 us
    all_to_all x1, blocking collectives, exchange(): lax.all_to_all(value, AXES, 0, 0, axis_index_groups=groups, tiled=True)  14.5 us
    pallas_call x2, Pallas kernels, pair_sums(): pl.pallas_call(functools.partial(pair_kernel, texts=len(texts), first=fir...  11.5 us
    all_to_all x1, waiting for transfers between devices, exchange(): lax.all_to_all(value, AXES, 0, 0, axis_index_groups=groups, tiled=True)  4.3 us
    all_to_all x1, starting transfers between devices, exchange(): lax.all_to_all(value, AXES, 0, 0, axis_index_groups=groups, tiled=True)  3.72 us
    pallas_call x1, Pallas kernels, text_shares(): pl.pallas_call(shares_kernel, in_specs=[VMEM, VMEM], out_specs=VMEM, out_...  1.86 us
  transfers between devices with their start and end apart: 18, of which 8 were waited for; matrix products, arithmetic and copies ran while one was open for 0% of the time, Pallas kernels for 11%

profile of v6, /device:TPU:1, one launch (start us, length us, event | category | flops | bytes accessed | tf_op | source)
XLA Modules:
  0.0 90.6 jit_solution(15806118247009719481)
XLA Ops:
  0.7 1.0 %broadcast_select_fusion = bf16[144,512]{1,0:T(8,128)(2,1)S(1)} fusion(bf16[144,512]{1,0:T(8,128)(2,1)} %param.8, bf16[144,512]{1,0:T(8,128)(2,1)} %param.6, pred[]{:T(512)S(6)} %eq.6), kind=kLoop, calls=%fused_computation.2 | loop fusion | flops 73728 | bytes 442369 | tf_op jit(solution)/shard_map/jit(_where)/select_n | solution.py:398
  1.7 3.3 %collective-permute-start = (bf16[144,512]{1,0:T(8,128)(2,1)S(1)}, bf16[144,512]{1,0:T(8,128)(2,1)S(1)}, u32[]{:S(2)}, u32[]{:S(2)}) collective-permute-start(bf16[144,512]{1,0:T(8,128)(2,1)S(1)} %broadcast_select_fusion), channel_id=1, source_target_pairs={{0,8},{1,9},{2,10},{3,11},{4,12},{5,13},{6,14},{7,15},{8,0},{9,1},... | collective-permute-start | bytes 442376 | tf_op jit(solution)/shard_map/ppermute | solution.py:32
  5.0 1.9 %shard_map.77 = bf16[16,80,128]{2,1,0:T(8,128)(2,1)} custom-call(bf16[144,512]{1,0:T(8,128)(2,1)} %learner_ref.1, bf16[144,512]{1,0:T(8,128)(2,1)} %refer_ref.1), custom_call_target="tpu_custom_call" | custom-call | tf_op jit(solution)/shard_map/pallas_call | solution.py:98
  6.9 0.0 collective-permute-done
  6.9 3.7 %all-to-all-start = ((bf16[16,80,128]{2,1,0:T(8,128)(2,1)}), bf16[16,80,128]{2,1,0:T(8,128)(2,1)S(1)}, u32[]{:S(2)}, u32[]{:S(2)}) async-start(bf16[16,80,128]{2,1,0:T(8,128)(2,1)} %shard_map.77), calls=%async_computation | async-start | bytes 655360 | tf_op jit(solution)/shard_map/all_to_all | solution.py:68
  10.6 2.8 %collective-permute-start.10 = (bf16[2,144,512]{2,1,0:T(8,128)(2,1)S(1)}, bf16[2,144,512]{2,1,0:T(8,128)(2,1)S(1)}, u32[]{:S(2)}, u32[]{:S(2)}) collective-permute-start(bf16[2,144,512]{2,1,0:T(8,128)(2,1)S(1)} %maximum_select_fusion), channel_id=1, source_target_pairs={{0,3},{1,2},{2,1},{3,0},{4,7},{5,6},{6,5},{7,4},{8,140},{9,141},{1... | collective-permute-start | bytes 884744 | tf_op jit(solution)/shard_map/ppermute | solution.py:32
  13.5 0.0 collective-permute-start.8
  13.5 1.3 %collective-permute-start.9 = (bf16[2,144,512]{2,1,0:T(8,128)(2,1)S(1)}, bf16[2,144,512]{2,1,0:T(8,128)(2,1)S(1)}, u32[]{:S(2)}, u32[]{:S(2)}) collective-permute-start(bf16[2,144,512]{2,1,0:T(8,128)(2,1)S(1)} %maximum_select_fusion), channel_id=1, source_target_pairs={{0,2},{1,3},{2,0},{3,1},{4,6},{5,7},{6,4},{7,5},{8,136},{9,137},{1... | collective-permute-start | bytes 884744 | tf_op jit(solution)/shard_map/ppermute | solution.py:32
  14.7 0.1 pad_add_fusion.place
  14.8 4.3 %all-to-all-done.in_ref = bf16[16,80,128]{2,1,0:T(8,128)(2,1)S(1)} async-done(((bf16[16,80,128]{2,1,0:T(8,128)(2,1)}), bf16[16,80,128]{2,1,0:T(8,128)(2,1)S(1)}, u32[]{:S(2)}, u32[]{:S(2)}) %all-to-all-start) | async-done | bytes 327712 | tf_op jit(solution)/shard_map/all_to_all | solution.py:68
  19.1 0.8 shard_map.78.refs_0_
  20.0 0.0 collective-permute-done.10
  20.0 1.4 %collective-permute-done.8 = bf16[2,144,512]{2,1,0:T(8,128)(2,1)S(1)} collective-permute-done((bf16[2,144,512]{2,1,0:T(8,128)(2,1)S(1)}, bf16[2,144,512]{2,1,0:T(8,128)(2,1)S(1)}, u32[]{:S(2)}, u32[]{:S(2)}) %collective-permute-start.8) | collective-permute-done | bytes 294944 | tf_op jit(solution)/shard_map/ppermute | solution.py:32
  21.3 3.5 %collective-permute-done.9 = bf16[2,144,512]{2,1,0:T(8,128)(2,1)S(1)} collective-permute-done((bf16[2,144,512]{2,1,0:T(8,128)(2,1)S(1)}, bf16[2,144,512]{2,1,0:T(8,128)(2,1)S(1)}, u32[]{:S(2)}, u32[]{:S(2)}) %collective-permute-start.9) | collective-permute-done | bytes 294944 | tf_op jit(solution)/shard_map/ppermute | solution.py:32
  24.8 0.1 pad_maximum_fusion.refs_5_
  24.9 0.0 copy-start
  25.0 0.0 copy-start.1
  25.0 2.1 %collective-permute-start.12 = (bf16[4,2,144,512]{3,2,1,0:T(8,128)(2,1)S(1)}, bf16[4,2,144,512]{3,2,1,0:T(8,128)(2,1)S(1)}, u32[]{:S(2)}, u32[]{:S(2)}) collective-permute-start(bf16[4,2,144,512]{3,2,1,0:T(8,128)(2,1)S(1)} %pad_maximum_fusion.refs_5_), channel_id=1, source_target_pairs={{0,132},{1,133},{2,134},{3,135},{4,128},{5,129},{6,130},{7,131},{8... | collective-permute-start | bytes 3538952 | tf_op jit(solution)/shard_map/ppermute | solution.py:32
  27.1 0.0 collective-permute-start.11
  27.1 5.6 %collective-permute-start.4 = (bf16[128,1152]{1,0:T(8,128)(2,1)S(1)}, bf16[128,1152]{1,0:T(8,128)(2,1)S(1)}, u32[]{:S(2)}, u32[]{:S(2)}) collective-permute-start(bf16[128,1152]{1,0:T(8,128)(2,1)S(1)} %shard_map.78.refs_0_), channel_id=1, source_target_pairs={{0,112},{1,113},{2,114},{3,115},{4,116},{5,117},{6,118},{7,119},{8... | collective-permute-start | bytes 884744 | tf_op jit(solution)/shard_map/ppermute | solution.py:32
  32.7 0.0 collective-permute-start.1
  32.7 5.0 %collective-permute-done.4.refs_2_ = bf16[128,1152]{1,0:T(8,128)(2,1)S(1)} collective-permute-done((bf16[128,1152]{1,0:T(8,128)(2,1)S(1)}, bf16[128,1152]{1,0:T(8,128)(2,1)S(1)}, u32[]{:S(2)}, u32[]{:S(2)}) %collective-permute-start.4) | collective-permute-done | bytes 294944 | tf_op jit(solution)/shard_map/ppermute | solution.py:32
  37.7 3.4 %collective-permute-start.5 = (bf16[128,1152]{1,0:T(8,128)(2,1)S(1)}, bf16[128,1152]{1,0:T(8,128)(2,1)S(1)}, u32[]{:S(2)}, u32[]{:S(2)}) collective-permute-start(bf16[128,1152]{1,0:T(8,128)(2,1)S(1)} %collective-permute-done.4.refs_2_), channel_id=1, source_target_pairs={{0,112},{1,113},{2,114},{3,115},{4,116},{5,117},{6,118},{7,119},{8... | collective-permute-start | bytes 884744 | tf_op jit(solution)/shard_map/ppermute | solution.py:32
  41.1 0.5 collective-permute-done.12.refs_9_
  41.7 2.4 %collective-permute-start.13 = (bf16[2,2,144,512]{3,2,1,0:T(8,128)(2,1)S(1)}, bf16[2,2,144,512]{3,2,1,0:T(8,128)(2,1)S(1)}, u32[]{:S(2)}, u32[]{:S(2)}) collective-permute-start(bf16[2,2,144,512]{3,2,1,0:T(8,128)(2,1)S(1)} %slice.8), channel_id=1, source_target_pairs={{0,4},{1,5},{2,6},{3,7},{4,0},{5,1},{6,2},{7,3},{8,9},{9,8},{10,11... | collective-permute-start | bytes 1769480 | tf_op jit(solution)/shard_map/ppermute | solution.py:32
  44.1 0.0 collective-permute-done.11.refs_6_
  44.1 1.0 %collective-permute-start.14 = (bf16[2,2,144,512]{3,2,1,0:T(8,128)(2,1)S(1)}, bf16[2,2,144,512]{3,2,1,0:T(8,128)(2,1)S(1)}, u32[]{:S(2)}, u32[]{:S(2)}) collective-permute-start(bf16[2,2,144,512]{3,2,1,0:T(8,128)(2,1)S(1)} %slice.9), channel_id=1, source_target_pairs={{0,132},{1,133},{2,134},{3,135},{4,128},{5,129},{6,130},{7,131},{8... | collective-permute-start | bytes 1769480 | tf_op jit(solution)/shard_map/ppermute | solution.py:32
  45.1 0.0 collective-permute-done.1.refs_1_
  45.1 0.3 collective-permute-start.2
  45.4 0.0 collective-permute-done.5.refs_4_
  45.4 4.2 %collective-permute-start.6 = (bf16[128,1152]{1,0:T(8,128)(2,1)S(1)}, bf16[128,1152]{1,0:T(8,128)(2,1)S(1)}, u32[]{:S(2)}, u32[]{:S(2)}) collective-permute-start(bf16[128,1152]{1,0:T(8,128)(2,1)S(1)} %collective-permute-done.5.refs_4_), channel_id=1, source_target_pairs={{0,112},{1,113},{2,114},{3,115},{4,116},{5,117},{6,118},{7,119},{8... | collective-permute-start | bytes 884744 | tf_op jit(solution)/shard_map/ppermute | solution.py:32
  49.6 5.1 %collective-permute-done.2.refs_3_ = bf16[128,1152]{1,0:T(8,128)(2,1)S(1)} collective-permute-done((bf16[128,1152]{1,0:T(8,128)(2,1)S(1)}, bf16[128,1152]{1,0:T(8,128)(2,1)S(1)}, u32[]{:S(2)}, u32[]{:S(2)}) %collective-permute-start.2) | collective-permute-done | bytes 294944 | tf_op jit(solution)/shard_map/ppermute | solution.py:32
  54.7 0.0 collective-permute-start.3
  54.7 0.0 collective-permute-done.6.refs_1_
  54.7 2.7 %collective-permute-start.7 = (bf16[128,1152]{1,0:T(8,128)(2,1)S(1)}, bf16[128,1152]{1,0:T(8,128)(2,1)S(1)}, u32[]{:S(2)}, u32[]{:S(2)}) collective-permute-start(bf16[128,1152]{1,0:T(8,128)(2,1)S(1)} %collective-permute-done.6.refs_1_), channel_id=1, source_target_pairs={{0,112},{1,113},{2,114},{3,115},{4,116},{5,117},{6,118},{7,119},{8... | collective-permute-start | bytes 884744 | tf_op jit(solution)/shard_map/ppermute | solution.py:32
  57.4 0.0 collective-permute-done.13.refs_7_
  57.4 0.0 collective-permute-done.14.refs_8_
  57.4 7.4 %shard_map.79 = (f32[16,128]{1,0:T(8,128)S(1)}, f32[16,128]{1,0:T(8,128)S(1)}, bf16[4,2,4,144,512]{4,3,2,1,0:T(8,128)(2,1)S(1)}, f32[4,1,512]{2,1,0:T(1,128)S(1)}) custom-call(f32[2]{0:T(128)S(1)} %copy-done, f32[2]{0:T(128)S(1)} %copy-done.1, s32[4]{0:T(128)S(1)} %pad_add_fusion.place, bf16[128,1152]{1,0:T(8,128)(2,1)S(1)} %shard_map.78.refs_0_, ...), custom_call_target="tpu_custom_call" | custom-call | flops 3019898880 | bytes 6193152 | tf_op jit(solution)/shard_map/pallas_call | solution.py:302
  64.8 0.0 collective-permute-done.3.refs_0_
  64.8 0.0 collective-permute-done.7.refs_2_
  64.8 4.2 %shard_map.80 = (f32[16,128]{1,0:T(8,128)S(1)}, f32[16,128]{1,0:T(8,128)S(1)}) custom-call(f32[2]{0:T(128)S(1)} %copy-done, f32[2]{0:T(128)S(1)} %copy-done.1, s32[4]{0:T(128)S(1)} %pad_add_fusion.place, bf16[128,1152]{1,0:T(8,128)(2,1)S(1)} %collective-permute-done.3.refs_0_, bf16[128,1152]{1,0:T(8,128)(2,1)S(1)} %collective-permute-done.6.refs_1_, ...), custom_call_target="tpu_custom_call" | custom-call | flops 1811939328 | bytes 5603328 | tf_op jit(solution)/shard_map/pallas_call | solution.py:302
  69.0 3.3 %collective-permute-start.15 = (f32[16,128]{1,0:T(8,128)S(1)}, f32[16,128]{1,0:T(8,128)S(1)}, u32[]{:S(2)}, u32[]{:S(2)}) collective-permute-start(f32[16,128]{1,0:T(8,128)S(1)} %get-tuple-element.25), channel_id=1, source_target_pairs={{0,8},{1,9},{2,10},{3,11},{4,12},{5,13},{6,14},{7,15},{8,0},{9,1},... | collective-permute-start | bytes 24584 | tf_op jit(solution)/shard_map/ppermute | solution.py:32
  72.3 0.8 collective-permute-done.15.got_ref
  73.1 0.6 shard_map.81
  73.7 14.5 %all_to_all.10.mine_ref = f32[16,2,128]{2,1,0:T(2,128)S(1)} all-to-all(f32[16,2,128]{2,1,0:T(2,128)S(1)} %shard_map.81), channel_id=1, replica_groups={{0,1,2,3,4,5,6,7,128,129,130,131,132,133,134,135},{8,136,24,152,40,168,..., dimensions={0} | all-to-all | bytes 32768 | tf_op jit(solution)/shard_map/all_to_all | solution.py:68
  88.2 0.3 collective-permute-start.16
  88.6 0.8 collective-permute-done.16.got_ref
  89.4 1.2 %shard_map.82 = (f32[2,64]{1,0:T(2,128)}, f32[2,64]{1,0:T(2,128)}) custom-call(s32[4]{0:T(128)S(1)} %pad_add_fusion.place, f32[16,2,128]{2,1,0:T(2,128)S(1)} %all_to_all.10.mine_ref, f32[16,2,128]{2,1,0:T(2,128)S(1)} %collective-permute-done.16.got_ref), custom_call_target="tpu_custom_call" | custom-call | tf_op jit(solution)/shard_map/pallas_call | solution.py:362
  (9 shorter events, 0.1 us)
Async XLA Ops:
  0.6 6.2 %copy-start.3 = (bf16[144,512]{1,0:T(8,128)(2,1)S(1)}, bf16[144,512]{1,0:T(8,128)(2,1)}, u32[]{:S(2)}) copy-start(bf16[144,512]{1,0:T(8,128)(2,1)} %param.6) | copy-start | bytes 442372
  0.6 6.2 %copy-start.2 = (bf16[144,512]{1,0:T(8,128)(2,1)S(1)}, bf16[144,512]{1,0:T(8,128)(2,1)}, u32[]{:S(2)}) copy-start(bf16[144,512]{1,0:T(8,128)(2,1)} %param.8) | copy-start | bytes 442372
  1.7 5.2 %collective-permute-start = (bf16[144,512]{1,0:T(8,128)(2,1)S(1)}, bf16[144,512]{1,0:T(8,128)(2,1)S(1)}, u32[]{:S(2)}, u32[]{:S(2)}) collective-permute-start(bf16[144,512]{1,0:T(8,128)(2,1)S(1)} %broadcast_select_fusion), channel_id=1, source_target_pairs={{0,8},{1,9},{2,10},{3,11},{4,12},{5,13},{6,14},{7,15},{8,0},{9,1},... | collective-permute-start | bytes 442376 | tf_op jit(solution)/shard_map/ppermute | solution.py:32
  6.9 12.2 %all-to-all-start = ((bf16[16,80,128]{2,1,0:T(8,128)(2,1)}), bf16[16,80,128]{2,1,0:T(8,128)(2,1)S(1)}, u32[]{:S(2)}, u32[]{:S(2)}) async-start(bf16[16,80,128]{2,1,0:T(8,128)(2,1)} %shard_map.77), calls=%async_computation | async-start | bytes 655360 | tf_op jit(solution)/shard_map/all_to_all | solution.py:68
  10.6 9.3 %collective-permute-start.10 = (bf16[2,144,512]{2,1,0:T(8,128)(2,1)S(1)}, bf16[2,144,512]{2,1,0:T(8,128)(2,1)S(1)}, u32[]{:S(2)}, u32[]{:S(2)}) collective-permute-start(bf16[2,144,512]{2,1,0:T(8,128)(2,1)S(1)} %maximum_select_fusion), channel_id=1, source_target_pairs={{0,3},{1,2},{2,1},{3,0},{4,7},{5,6},{6,5},{7,4},{8,140},{9,141},{1... | collective-permute-start | bytes 884744 | tf_op jit(solution)/shard_map/ppermute | solution.py:32
  13.5 7.9 %collective-permute-start.8 = (bf16[2,144,512]{2,1,0:T(8,128)(2,1)S(1)}, bf16[2,144,512]{2,1,0:T(8,128)(2,1)S(1)}, u32[]{:S(2)}, u32[]{:S(2)}) collective-permute-start(bf16[2,144,512]{2,1,0:T(8,128)(2,1)S(1)} %maximum_select_fusion), channel_id=1, source_target_pairs={{0,1},{1,0},{2,3},{3,2},{4,5},{5,4},{6,7},{7,6},{8,12},{9,13},{10,... | collective-permute-start | bytes 884744 | tf_op jit(solution)/shard_map/ppermute | solution.py:32
  13.5 11.3 %collective-permute-start.9 = (bf16[2,144,512]{2,1,0:T(8,128)(2,1)S(1)}, bf16[2,144,512]{2,1,0:T(8,128)(2,1)S(1)}, u32[]{:S(2)}, u32[]{:S(2)}) collective-permute-start(bf16[2,144,512]{2,1,0:T(8,128)(2,1)S(1)} %maximum_select_fusion), channel_id=1, source_target_pairs={{0,2},{1,3},{2,0},{3,1},{4,6},{5,7},{6,4},{7,5},{8,136},{9,137},{1... | collective-permute-start | bytes 884744 | tf_op jit(solution)/shard_map/ppermute | solution.py:32
  24.9 32.5 %copy-start = (f32[2]{0:T(128)S(1)}, f32[2]{0:T(128)}, u32[]{:S(2)}) copy-start(f32[2]{0:T(128)} %sharpness.3) | copy-start | bytes 28
  25.0 32.4 %copy-start.1 = (f32[2]{0:T(128)S(1)}, f32[2]{0:T(128)}, u32[]{:S(2)}) copy-start(f32[2]{0:T(128)} %offsets.3) | copy-start | bytes 28
  25.0 16.6 %collective-permute-start.12 = (bf16[4,2,144,512]{3,2,1,0:T(8,128)(2,1)S(1)}, bf16[4,2,144,512]{3,2,1,0:T(8,128)(2,1)S(1)}, u32[]{:S(2)}, u32[]{:S(2)}) collective-permute-start(bf16[4,2,144,512]{3,2,1,0:T(8,128)(2,1)S(1)} %pad_maximum_fusion.refs_5_), channel_id=1, source_target_pairs={{0,132},{1,133},{2,134},{3,135},{4,128},{5,129},{6,130},{7,131},{8... | collective-permute-start | bytes 3538952 | tf_op jit(solution)/shard_map/ppermute | solution.py:32
  27.1 17.0 %collective-permute-start.11 = (bf16[4,2,144,512]{3,2,1,0:T(8,128)(2,1)S(1)}, bf16[4,2,144,512]{3,2,1,0:T(8,128)(2,1)S(1)}, u32[]{:S(2)}, u32[]{:S(2)}) collective-permute-start(bf16[4,2,144,512]{3,2,1,0:T(8,128)(2,1)S(1)} %pad_maximum_fusion.refs_5_), channel_id=1, source_target_pairs={{0,4},{1,5},{2,6},{3,7},{4,0},{5,1},{6,2},{7,3},{8,9},{9,8},{10,11... | collective-permute-start | bytes 3538952 | tf_op jit(solution)/shard_map/ppermute | solution.py:32
  27.1 10.6 %collective-permute-start.4 = (bf16[128,1152]{1,0:T(8,128)(2,1)S(1)}, bf16[128,1152]{1,0:T(8,128)(2,1)S(1)}, u32[]{:S(2)}, u32[]{:S(2)}) collective-permute-start(bf16[128,1152]{1,0:T(8,128)(2,1)S(1)} %shard_map.78.refs_0_), channel_id=1, source_target_pairs={{0,112},{1,113},{2,114},{3,115},{4,116},{5,117},{6,118},{7,119},{8... | collective-permute-start | bytes 884744 | tf_op jit(solution)/shard_map/ppermute | solution.py:32
  32.7 12.4 %collective-permute-start.1 = (bf16[128,1152]{1,0:T(8,128)(2,1)S(1)}, bf16[128,1152]{1,0:T(8,128)(2,1)S(1)}, u32[]{:S(2)}, u32[]{:S(2)}) collective-permute-start(bf16[128,1152]{1,0:T(8,128)(2,1)S(1)} %shard_map.78.refs_0_), channel_id=1, source_target_pairs={{0,16},{1,17},{2,18},{3,19},{4,20},{5,21},{6,22},{7,23},{8,24},{9,... | collective-permute-start | bytes 884744 | tf_op jit(solution)/shard_map/ppermute | solution.py:32
  37.7 7.7 %collective-permute-start.5 = (bf16[128,1152]{1,0:T(8,128)(2,1)S(1)}, bf16[128,1152]{1,0:T(8,128)(2,1)S(1)}, u32[]{:S(2)}, u32[]{:S(2)}) collective-permute-start(bf16[128,1152]{1,0:T(8,128)(2,1)S(1)} %collective-permute-done.4.refs_2_), channel_id=1, source_target_pairs={{0,112},{1,113},{2,114},{3,115},{4,116},{5,117},{6,118},{7,119},{8... | collective-permute-start | bytes 884744 | tf_op jit(solution)/shard_map/ppermute | solution.py:32
  41.7 15.7 %collective-permute-start.13 = (bf16[2,2,144,512]{3,2,1,0:T(8,128)(2,1)S(1)}, bf16[2,2,144,512]{3,2,1,0:T(8,128)(2,1)S(1)}, u32[]{:S(2)}, u32[]{:S(2)}) collective-permute-start(bf16[2,2,144,512]{3,2,1,0:T(8,128)(2,1)S(1)} %slice.8), channel_id=1, source_target_pairs={{0,4},{1,5},{2,6},{3,7},{4,0},{5,1},{6,2},{7,3},{8,9},{9,8},{10,11... | collective-permute-start | bytes 1769480 | tf_op jit(solution)/shard_map/ppermute | solution.py:32
  44.1 13.3 %collective-permute-start.14 = (bf16[2,2,144,512]{3,2,1,0:T(8,128)(2,1)S(1)}, bf16[2,2,144,512]{3,2,1,0:T(8,128)(2,1)S(1)}, u32[]{:S(2)}, u32[]{:S(2)}) collective-permute-start(bf16[2,2,144,512]{3,2,1,0:T(8,128)(2,1)S(1)} %slice.9), channel_id=1, source_target_pairs={{0,132},{1,133},{2,134},{3,135},{4,128},{5,129},{6,130},{7,131},{8... | collective-permute-start | bytes 1769480 | tf_op jit(solution)/shard_map/ppermute | solution.py:32
  45.1 9.6 %collective-permute-start.2 = (bf16[128,1152]{1,0:T(8,128)(2,1)S(1)}, bf16[128,1152]{1,0:T(8,128)(2,1)S(1)}, u32[]{:S(2)}, u32[]{:S(2)}) collective-permute-start(bf16[128,1152]{1,0:T(8,128)(2,1)S(1)} %collective-permute-done.1.refs_1_), channel_id=1, source_target_pairs={{0,16},{1,17},{2,18},{3,19},{4,20},{5,21},{6,22},{7,23},{8,24},{9,... | collective-permute-start | bytes 884744 | tf_op jit(solution)/shard_map/ppermute | solution.py:32
  45.4 9.4 %collective-permute-start.6 = (bf16[128,1152]{1,0:T(8,128)(2,1)S(1)}, bf16[128,1152]{1,0:T(8,128)(2,1)S(1)}, u32[]{:S(2)}, u32[]{:S(2)}) collective-permute-start(bf16[128,1152]{1,0:T(8,128)(2,1)S(1)} %collective-permute-done.5.refs_4_), channel_id=1, source_target_pairs={{0,112},{1,113},{2,114},{3,115},{4,116},{5,117},{6,118},{7,119},{8... | collective-permute-start | bytes 884744 | tf_op jit(solution)/shard_map/ppermute | solution.py:32
  54.7 10.1 %collective-permute-start.3 = (bf16[128,1152]{1,0:T(8,128)(2,1)S(1)}, bf16[128,1152]{1,0:T(8,128)(2,1)S(1)}, u32[]{:S(2)}, u32[]{:S(2)}) collective-permute-start(bf16[128,1152]{1,0:T(8,128)(2,1)S(1)} %collective-permute-done.2.refs_3_), channel_id=1, source_target_pairs={{0,16},{1,17},{2,18},{3,19},{4,20},{5,21},{6,22},{7,23},{8,24},{9,... | collective-permute-start | bytes 884744 | tf_op jit(solution)/shard_map/ppermute | solution.py:32
  54.7 10.1 %collective-permute-start.7 = (bf16[128,1152]{1,0:T(8,128)(2,1)S(1)}, bf16[128,1152]{1,0:T(8,128)(2,1)S(1)}, u32[]{:S(2)}, u32[]{:S(2)}) collective-permute-start(bf16[128,1152]{1,0:T(8,128)(2,1)S(1)} %collective-permute-done.6.refs_1_), channel_id=1, source_target_pairs={{0,112},{1,113},{2,114},{3,115},{4,116},{5,117},{6,118},{7,119},{8... | collective-permute-start | bytes 884744 | tf_op jit(solution)/shard_map/ppermute | solution.py:32
  69.0 4.2 %collective-permute-start.15 = (f32[16,128]{1,0:T(8,128)S(1)}, f32[16,128]{1,0:T(8,128)S(1)}, u32[]{:S(2)}, u32[]{:S(2)}) collective-permute-start(f32[16,128]{1,0:T(8,128)S(1)} %get-tuple-element.25), channel_id=1, source_target_pairs={{0,8},{1,9},{2,10},{3,11},{4,12},{5,13},{6,14},{7,15},{8,0},{9,1},... | collective-permute-start | bytes 24584 | tf_op jit(solution)/shard_map/ppermute | solution.py:32
  88.2 1.2 %collective-permute-start.16 = (f32[16,2,128]{2,1,0:T(2,128)S(1)}, f32[16,2,128]{2,1,0:T(2,128)S(1)}, u32[]{:S(2)}, u32[]{:S(2)}) collective-permute-start(f32[16,2,128]{2,1,0:T(2,128)S(1)} %all_to_all.10.mine_ref), channel_id=1, source_target_pairs={{0,8},{1,9},{2,10},{3,11},{4,12},{5,13},{6,14},{7,15},{8,0},{9,1},... | collective-permute-start | bytes 49160 | tf_op jit(solution)/shard_map/ppermute | solution.py:32
